TPU v7x, 32 devices: a whole 2x2x4 slice. The times are simulated.
32 devices in a mesh: dp: 8 (over y, x, core), bag: 4 (over z).
Axes of the slice: x: 2, y: 2, z: 4, core: 2. Of those that a mesh axis runs over, the one named last changes fastest.
Arguments:
- home_tokens: bfloat16 [4096, 3072], P('dp', 'bag'), may hold values from -6 to 6
- mod_weight: bfloat16 [2, 3072, 3072], P(None, None, 'bag'), may hold values from -0.109375 to 0.109375
- qkv_weight: bfloat16 [3, 3072, 3072], P(None, None, 'bag')
- norm_gain: float32 [2, 3072], P(None, 'bag'), may hold values from 0.5 to 8
- output_weight: bfloat16 [3072, 3072], P('bag'), may hold values from -0.109375 to 0.109375
- row_plan: int32 [4096], replicated, may hold values from 0 to 5119, as said below
- sample_lengths: int32 [8, 4], replicated, may hold values from 0 to 640, as said below
- modality: int32 [8, 4], replicated, may hold values from 0 to 1
Outputs:
- block_output: bfloat16 [4096, 3072], P('dp', 'bag')
Inputs may be any that keep to these rules, and one draw needn't show every extreme that they name: `row_plan`: row r sits on home r // 512; no two rows share a value; the rows of bag j fill exactly its slots 0 to sample_ends[j, 3] - 1; no home sends more than 128 rows to one bag, and some home sends exactly 128 rows to some bag. `sample_lengths`: row j lists the lengths of the samples of bag j in slot order, zeros allowed; each row sums to at most 640, and some bag holds one sample of 640 tokens.
All inputs are finite; a program needn't handle non-finite values.
Results may differ from a plain program's by a relative error of at most 0.013.
The roundings to bfloat16 on the way count: a program that leaves them out, or rounds other values in their place, can miss the bound.
Values may be sent and summed in bfloat16 or wider, within the bound.
No kernel may reach another device: no remote copies, remote signals or barrier semaphores. Data moves between devices by JAX's collectives and lax.ppermute only.
A program may use at most 192 MiB of HBM per device.

v0:
```python
import jax
import jax.numpy as jnp
from jax import lax
from jax.sharding import PartitionSpec as P

HD = 64


epsilon = 1e-06


def head_norm(heads_in, gains):
    centre = jnp.mean(heads_in, axis=-1, keepdims=True)
    shifted = heads_in - centre
    spread = jnp.mean(shifted * shifted, axis=-1, keepdims=True)
    return shifted * lax.rsqrt(spread + epsilon) * gains


def body(
    home_tokens,
    mod_weight,
    qkv_weight,
    norm_gain,
    output_weight,
    row_plan,
    sample_lengths,
    modality,
):
    dev_count = lax.axis_size("dp")
    members = lax.axis_size("bag")
    my_home = lax.axis_index("dp")
    resident_rows, width_part = home_tokens.shape
    pack_size = resident_rows + resident_rows // 4
    total_rows = row_plan.shape[0]
    capacity = 2 * resident_rows // dev_count
    send_slots = capacity * dev_count
    head_width = output_weight.shape[0]
    head_count = head_width // HD
    bag_ids = jnp.arange(dev_count, dtype=jnp.int32)
    sample_ends = jnp.cumsum(sample_lengths, axis=1)
    dest_bag = row_plan // pack_size
    dest_slot = row_plan % pack_size
    bag_match = dest_bag[:, None] == bag_ids[None, :]
    rows_per_resident = bag_match.astype(jnp.bfloat16).reshape(dev_count, resident_rows, dev_count)
    row_ids = jnp.arange(resident_rows, dtype=jnp.int32)
    lower_bound = (row_ids[:, None] > row_ids[None, :]).astype(jnp.bfloat16)
    preceding_rows = jnp.einsum(
        "mt,pta->pma", lower_bound, rows_per_resident, preferred_element_type=jnp.float32
    )
    position = (
        jnp.sum(preceding_rows * rows_per_resident.astype(jnp.float32), axis=2)
        .astype(jnp.int32)
        .reshape(total_rows)
    )
    home_of = jnp.arange(total_rows, dtype=jnp.int32) // resident_rows
    send_index = position * dev_count + dest_bag
    recv_index = jnp.where(dest_bag == my_home, position * dev_count + home_of, send_slots)
    slot_table = (
        jnp.full((send_slots,), pack_size, jnp.int32).at[recv_index].set(dest_slot, mode="drop")
    )
    slot_source = (
        jnp.full((pack_size,), send_slots, jnp.int32)
        .at[slot_table]
        .set(jnp.arange(send_slots, dtype=jnp.int32), mode="drop")
    )
    own_start = my_home * resident_rows
    own_hits = lax.dynamic_slice_in_dim(bag_match.astype(jnp.int32), own_start, resident_rows, 0)
    own_slot = lax.dynamic_slice_in_dim(dest_slot, own_start, resident_rows, 0)
    own_index = lax.dynamic_slice_in_dim(send_index, own_start, resident_rows, 0)
    row_ends = jnp.dot(own_hits, sample_ends)
    row_sample = jnp.sum((own_slot[:, None] >= row_ends).astype(jnp.int32), axis=1)
    sample_hits = (
        row_sample[:, None] == jnp.arange(sample_ends.shape[1], dtype=jnp.int32)[None, :]
    ).astype(jnp.int32)
    row_modality = jnp.sum(jnp.dot(own_hits, modality) * sample_hits, axis=1)
    is_first = (row_modality == 0)[:, None]
    pieces = lax.all_gather(home_tokens, "bag", axis=1, tiled=True)
    weight_rows = mod_weight
    blank = jnp.zeros_like(pieces)
    first_part = jnp.where(is_first, pieces, blank)
    second_part = jnp.where(is_first, blank, pieces)
    running = jnp.dot(first_part, weight_rows[0], preferred_element_type=jnp.float32)
    projected = (
        running + jnp.dot(second_part, weight_rows[1], preferred_element_type=jnp.float32)
    ).astype(jnp.bfloat16)
    send_onehot = (jnp.arange(send_slots, dtype=jnp.int32)[:, None] == own_index[None, :]).astype(
        jnp.bfloat16
    )
    send_flat = jnp.dot(send_onehot, projected, preferred_element_type=jnp.float32).astype(
        jnp.bfloat16
    )
    outgoing_rows = send_flat.reshape(capacity, dev_count, width_part)
    arrived = lax.all_to_all(outgoing_rows, "dp", split_axis=1, concat_axis=1, tiled=True)
    slot_onehot = (slot_source[:, None] == jnp.arange(send_slots, dtype=jnp.int32)[None, :]).astype(
        jnp.bfloat16
    )
    packed_part = jnp.dot(
        slot_onehot, arrived.reshape(send_slots, width_part), preferred_element_type=jnp.float32
    ).astype(jnp.bfloat16)
    weight_rows = qkv_weight
    stacked = jnp.einsum(
        "pn,knh->kph",
        lax.all_gather(packed_part, "bag", axis=1, tiled=True),
        weight_rows,
        preferred_element_type=jnp.float32,
    )
    my_ends = jnp.sum(jnp.where((bag_ids == my_home)[:, None], sample_ends, 0), axis=0)
    slot_ids = jnp.arange(pack_size, dtype=jnp.int32)
    sample_ids = jnp.sum((slot_ids[:, None] >= my_ends[None, :]).astype(jnp.int32), axis=1)
    queries = head_norm(
        stacked[0].reshape(pack_size, head_count, HD), norm_gain[0].reshape(head_count, HD)
    ).astype(jnp.bfloat16)
    keys_normed = head_norm(
        stacked[1].reshape(pack_size, head_count, HD), norm_gain[1].reshape(head_count, HD)
    ).astype(jnp.bfloat16)
    values = stacked[2].astype(jnp.bfloat16).reshape(pack_size, head_count, HD)
    blocks = max(1, pack_size // 512)
    block_rows = pack_size // blocks

    def attend(block_index):
        offset = block_index * block_rows
        query_block = lax.dynamic_slice_in_dim(queries, offset, block_rows, 0)
        sample_block = lax.dynamic_slice_in_dim(sample_ids, offset, block_rows, 0)
        scores = jnp.einsum(
            "qhd,khd->hqk", query_block, keys_normed, preferred_element_type=jnp.float32
        ) * HD ** (-0.5)
        scores = jnp.where((sample_block[:, None] == sample_ids[None, :])[None], scores, -jnp.inf)
        row_max = jnp.max(scores, axis=2, keepdims=True)
        raised = jnp.exp(scores - row_max)
        weights_soft = (raised / jnp.sum(raised, axis=2, keepdims=True)).astype(jnp.bfloat16)
        return jnp.einsum(
            "hqk,khd->qhd", weights_soft, values, preferred_element_type=jnp.float32
        ).astype(jnp.bfloat16)

    attended = lax.map(attend, jnp.arange(blocks, dtype=jnp.int32)).reshape(pack_size, head_width)
    partial_value = jnp.dot(attended, output_weight, preferred_element_type=jnp.float32)
    partial_low = partial_value.astype(jnp.bfloat16)
    back_rows = jnp.take(partial_low, slot_table, axis=0, mode="fill", fill_value=0)
    back_rows = back_rows.reshape(capacity, dev_count * members, width_part)
    returned = lax.all_to_all(back_rows, ("dp", "bag"), split_axis=1, concat_axis=1, tiled=True)
    combined = jnp.sum(
        returned.reshape(capacity, dev_count, members, width_part).astype(jnp.float32), axis=2
    )
    combined = combined.reshape(send_slots, width_part)
    result = jnp.take(combined, own_index, axis=0)
    return result.astype(jnp.bfloat16)


def solution(mesh):
    in_specs = (
        P("dp", "bag"),
        P(None, None, "bag"),
        P(None, None, "bag"),
        P(None, "bag"),
        P("bag", None),
        P(),
        P(),
        P(),
    )
    out_specs = P("dp", "bag")
    return jax.shard_map(body, mesh=mesh, in_specs=in_specs, out_specs=out_specs, check_vma=False)
```

profile of v0, /device:TPU:0, one launch (start us, length us, event | category | flops | bytes accessed | tf_op | source)
XLA Modules:
  0.0 454.2 jit_solution(9582067303599934686)
XLA Ops:
  6.5 0.0 copy-start
  6.5 0.0 all-gather.3.cloned.1.call-start
  6.5 0.7 all-gather.3.cloned.1.call-update
  7.3 0.7 add_select_fusion.2
  8.0 0.3 fusion.39
  8.3 0.7 reduce_window_sum.11
  9.0 0.7 compare_select_fusion
  9.8 0.1 dynamic_slice.17
  9.9 0.1 compare_and_fusion.1
  9.9 0.1 fusion.42
  10.1 0.0 copy-done
  10.1 0.1 fusion.40
  10.3 64.9 %all-gather.3.cloned.1.call-done = bf16[512,3072]{1,0:T(8,128)(2,1)} async-done(((bf16[512,768]{1,0:T(8,128)(2,1)}), bf16[512,3072]{1,0:T(8,128)(2,1)}) %all-gather.3.cloned.1.call-update) | async-done | bytes 3145744 | tf_op jit(solution)/shard_map/all_gather | solution.py:77
  75.1 5.9 %fusion.6 = f32[512,768]{1,0:T(8,128)S(1)} fusion(bf16[2,3072,768]{2,1,0:T(8,128)(2,1)} %param.9, bf16[512,3072]{1,0:T(8,128)(2,1)} %all-gather.3.cloned.1.call-done, pred[512]{0:T(512)(128)(4,1)S(1)} %broadcast_compare_fusion.1), kind=kOutput, calls=%fused_computation.16 | convolution fusion | flops 2417491968 | bytes 9437696 | tf_op jit(solution)/shard_map/dot_general | solution.py:84
  81.1 7.3 %fusion.28 = bf16[128,8,768]{2,1,0:T(8,128)(2,1)S(1)} fusion(s32[512]{0:T(512)S(1)} %get-tuple-element.24, f32[512,768]{1,0:T(8,128)S(1)} %fusion.6, bf16[2,3072,768]{2,1,0:T(8,128)(2,1)} %param.9, bf16[512,3072]{1,0:T(8,128)(2,1)} %all-gather.3.cloned.1.call-done, pred[512]{0:T(512)(128)(4,1)S(1)} %broadcast_compare_fusion.1), kind=kOutput, calls=%fused_computation.46 | convolution fusion | flops 3224895488 | bytes 11012608 | tf_op jit(solution)/shard_map/dot_general | solution.py:89
  88.4 1.4 copy.44
  89.9 3.7 all-to-all-start
  93.5 0.0 all-gather.5.cloned.1.call-start
  93.6 15.5 %scatter_custom_fusion = s32[1024]{0:T(1024)S(1)} fusion(s32[4096]{0:T(1024)S(1)} %get-tuple-element.30, s32[4096]{0:T(1024)S(1)} %get-tuple-element.31, s32[]{:T(128)} %constant.96.clone.1), kind=kCustom, calls=%fused_computation.109 | custom fusion | bytes 4100 | tf_op jit(solution)/shard_map/scatter | solution.py:59
  109.1 4.3 scatter_custom_fusion.1
  113.5 0.0 copy-start.3
  113.5 1.1 all-to-all-done
  114.6 2.7 fusion.30
  117.3 0.0 all-gather.5.cloned.1.call-update
  117.3 0.0 copy-done.3
  117.3 0.1 mul.86
  117.4 0.1 mul.80
  117.5 0.1 broadcast_in_dim.119
  117.6 0.1 copy.43
  117.6 0.1 select_reduce_fusion
  117.8 0.1 convert_reduce_fusion.1
  117.9 0.3 broadcast_compare_fusion
  118.2 73.8 %all-gather.5.cloned.1.call-done = bf16[640,3072]{1,0:T(8,128)(2,1)} async-done(((bf16[640,768]{1,0:T(8,128)(2,1)}), bf16[640,3072]{1,0:T(8,128)(2,1)}) %all-gather.5.cloned.1.call-update) | async-done | bytes 3932176 | tf_op jit(solution)/shard_map/all_gather | solution.py:103
  192.0 13.4 %fusion.19 = f32[3,640,768]{2,1,0:T(8,128)S(1)} fusion(bf16[3,3072,768]{2,1,0:T(8,128)(2,1)} %param.10, bf16[640,3072]{1,0:T(8,128)(2,1)} %all-gather.5.cloned.1.call-done), kind=kOutput, calls=%fused_computation.31 | convolution fusion | flops 9059696640 | bytes 23986176 | tf_op jit(solution)/shard_map/pn,knh->kph/dot_general | solution.py:101
  205.3 0.1 slice.51
  205.4 2.1 fusion.76
  207.6 0.6 copy.46
  208.2 1.9 copy.47
  210.1 2.8 copy.48
  212.9 1.7 reduce_sum.107
  214.6 1.8 multiply_reduce_fusion
  216.5 0.1 reduce_sum.105
  216.6 0.0 copy-start.2
  216.6 0.3 multiply_reduce_fusion.1
  216.9 1.2 copy-done.2
  218.2 0.0 slice-start
  218.2 8.3 %fusion.46 = f32[12,640,640]{1,2,0:T(8,128)} fusion(f32[640,12,64]{0,2,1:T(8,128)S(1)} %bitcast.58, f32[640,12,64]{0,2,1:T(8,128)S(1)} %bitcast.61, f32[12,64]{1,0:T(8,128)S(1)} %mul.86, f32[640,12]{0,1:T(8,128)S(1)} %get-tuple-element.36, f32[640,12]{0,1:T(8,128)S(1)} %broadcast_multiply_fusion, f32[12,64]{1,0:T(8,128)S(1)} %mul.80, ...), kind=kOutput, calls=%fused_computation.61 | convolution fusion | flops 633077760 | bytes 23721984 | tf_op jit(solution)/shard_map/while/body/eval_jaxpr/qhd,khd->hqk/dot_general | solution.py:124
  226.4 0.0 slice-start.1
  226.4 26.0 %fusion.77 = (f32[12,640]{1,0:T(8,128)S(1)}, f32[12,640,640]{1,2,0:T(8,128)}) fusion(f32[12,640,640]{1,2,0:T(8,128)} %fusion.46, pred[640,640]{0,1:T(8,128)(4,1)S(1)} %broadcast_compare_fusion), kind=kOutput, calls=%fused_computation.119 | output fusion | flops 29491840 | bytes 39761920 | tf_op jit(solution)/shard_map/while/body/eval_jaxpr/sub | solution.py:129
  252.4 8.4 %fusion.29 = bf16[12,64,640]{2,1,0:T(8,128)(2,1)S(1)} fusion(bf16[640,12,64]{0,2,1:T(8,128)(2,1)S(1)} %bitcast.62, f32[12,640,640]{1,2,0:T(8,128)} %get-tuple-element.35, f32[12,640]{1,0:T(8,128)S(1)} %get-tuple-element.34), kind=kOutput, calls=%fused_computation.47 | convolution fusion | flops 639467520 | bytes 21657600 | tf_op jit(solution)/shard_map/while/body/eval_jaxpr/hqk,khd->qhd/dot_general | solution.py:131
  260.8 0.0 slice-done
  260.8 0.0 slice-done.1
  260.9 5.1 %convolution_convert_fusion = bf16[640,3072]{1,0:T(8,128)(2,1)} fusion(bf16[640,768]{0,1:T(8,128)(2,1)S(1)} %bitcast.68, bf16[768,3072]{1,0:T(8,128)(2,1)S(1)} %bitcast.67), kind=kOutput, calls=%fused_computation.15 | convolution fusion | flops 3021864960 | bytes 9633792 | tf_op jit(solution)/shard_map/dot_general | solution.py:136
  266.0 14.8 %gather_fusion = bf16[1024,3072]{1,0:T(8,128)(2,1)} fusion(bf16[640,3072]{1,0:T(8,128)(2,1)} %convolution_convert_fusion, s32[1024]{0:T(1024)S(1)} %get-tuple-element.32), kind=kCustom, calls=%fused_computation | custom fusion | bytes 12587008 | tf_op jit(solution)/shard_map/jit(_take)/gather | solution.py:138
  280.8 10.7 %gather.11 = bf16[128,32,768]{2,1,0:T(8,128)(2,1)} reshape(bf16[1024,3072]{1,0:T(8,128)(2,1)} %gather_fusion) | data formatting | bytes 12582912 | tf_op jit(solution)/shard_map/jit(_take)/gather | solution.py:138
  291.5 7.6 %copy_select_fusion = bf16[128,32,768]{2,0,1:T(8,128)(2,1)} fusion(bf16[128,32,768]{2,1,0:T(8,128)(2,1)} %gather.11, pred[128,32]{0,1:T(8,128)(4,1)S(1)} %bitcast.65), kind=kLoop, calls=%fused_computation.14 | loop fusion | flops 3145728 | bytes 12587008 | tf_op jit(solution)/shard_map/jit(_take)/select_n | solution.py:138
  299.2 3.6 all-to-all-start.1
  302.8 136.9 %all-to-all-done.1 = bf16[128,32,768]{2,0,1:T(8,128)(2,1)} async-done(((bf16[128,32,768]{2,0,1:T(8,128)(2,1)}), bf16[128,32,768]{2,0,1:T(8,128)(2,1)}, u32[]{:S(2)}, u32[]{:S(2)}) %all-to-all-start.1) | async-done | bytes 6291488 | tf_op jit(solution)/shard_map/all_to_all | solution.py:140
  439.7 3.6 convert_reduce_fusion
  443.4 0.9 copy.62
  444.2 0.0 copy-start.1
  444.2 2.0 gather_fusion.1
  446.3 1.1 select_convert_fusion
  447.4 0.0 copy-done.1
  (16 shorter events, 0.1 us)
Async XLA Ops:
  6.5 3.6 copy-start
  6.5 68.6 %all-gather.3.cloned.1.call-start = ((), (), s32[]{:S(2)}) async-start(), calls=%async_computation.2 | async-start | bytes 3932160 | tf_op jit(solution)/shard_map/all_gather | solution.py:77
  89.9 24.7 %all-to-all-start = ((bf16[128,8,768]{2,0,1:T(8,128)(2,1)}), bf16[128,8,768]{2,0,1:T(8,128)(2,1)S(1)}, u32[]{:S(2)}, u32[]{:S(2)}) async-start(bf16[128,8,768]{2,0,1:T(8,128)(2,1)} %copy.44), calls=%async_computation | async-start | bytes 3145728 | tf_op jit(solution)/shard_map/all_to_all | solution.py:93
  93.5 98.4 %all-gather.5.cloned.1.call-start = ((), (), s32[]{:S(2)}) async-start(), calls=%async_computation.3 | async-start | bytes 4915200 | tf_op jit(solution)/shard_map/all_gather | solution.py:103
  113.5 3.8 copy-start.3
  216.6 1.5 copy-start.2
  218.2 42.7 %slice-start = ((s8[4718592]{0:T(1024)(128)(4,1)}), s8[4194304]{0:T(1024)(128)(4,1)S(1)}, s32[]{:S(2)}) async-start(s8[4718592]{0:T(1024)(128)(4,1)} %bitcast.66), calls=%async_computation.4 | async-start | bytes 8388608
  226.4 34.4 %slice-start.1 = ((s8[4718592]{0:T(1024)(128)(4,1)}), s8[524288]{0:T(1024)(128)(4,1)S(1)}, s32[]{:S(2)}) async-start(s8[4718592]{0:T(1024)(128)(4,1)} %bitcast.66), calls=%async_computation.5 | async-start | bytes 1048576
  299.2 140.5 %all-to-all-start.1 = ((bf16[128,32,768]{2,0,1:T(8,128)(2,1)}), bf16[128,32,768]{2,0,1:T(8,128)(2,1)}, u32[]{:S(2)}, u32[]{:S(2)}) async-start(bf16[128,32,768]{2,0,1:T(8,128)(2,1)} %copy_select_fusion), calls=%async_computation.1 | async-start | bytes 12582912 | tf_op jit(solution)/shard_map/all_to_all | solution.py:140
  444.2 3.1 copy-start.1
Sparse Core Ops, SparseCore 0:
  8.9 66.1 all-gather.2
  117.4 74.5 all-gather.4
where the time goes:
time: 457 us; the launch traced here: 454 us
  waiting for transfers between devices  277 us (61%)
  local copies, waits for them, and re-layouts  58.9 us (13%)
  matrix products  51.7 us (11%)
  other arithmetic  45.1 us (10%)
  between operations  13.7 us (3%)
  starting transfers between devices  7.31 us (2%)
    all_to_all x1, waiting for transfers between devices, body(): lax.all_to_all(back_rows, ('dp', 'bag'), split_axis=1, concat_axis=1, til...  137 us
    all_gather x1, waiting for transfers between devices, body(): lax.all_gather(packed_part, 'bag', axis=1, tiled=True)  73.8 us
    all_gather x1, waiting for transfers between devices, body(): pieces = lax.all_gather(home_tokens, 'bag', axis=1, tiled=True)  64.9 us
    sub x1, other arithmetic, attend(): raised = jnp.exp(scores - row_max)  26 us
    gather x2, local copies, waits for them, and re-layouts, body(): jnp.take(partial_low, slot_table, axis=0, mode='fill', fill_value=0)  25.5 us
    scatter x1, local copies, waits for them, and re-layouts, body(): jnp.full((send_slots,), pack_size, jnp.int32).at[recv_index]  15.5 us
    dot_general x1, matrix products, body(): jnp.einsum('pn,knh->kph', lax.all_gather(packed_part, 'bag', axis=1, tile...  13.4 us
  transfers between devices with their start and end apart: 4, of which 4 were waited for; matrix products, arithmetic and copies ran while one was open for 5% of the time, Pallas kernels for 0%

commit v1 on v0

v1 whole, which is shorter than its diff:
```python
import functools

import jax
import jax.numpy as jnp
from jax import lax
from jax.experimental import pallas as pl
from jax.experimental.pallas import tpu as pltpu
from jax.sharding import PartitionSpec as P

HD = 64
EPSILON = 1e-06
VMEM_LIMIT = 56 * 1024 * 1024
BF16 = jnp.bfloat16
F32 = jnp.float32


def params():
    return pltpu.CompilerParams(vmem_limit_bytes=VMEM_LIMIT)


def up16(count):
    return (count + 15) // 16 * 16


def iota(shape, dim):
    return lax.broadcasted_iota(jnp.int32, shape, dim)


def dot(left, right):
    return jnp.dot(left, right, preferred_element_type=F32)


def dot_nt(left, right):
    return lax.dot_general(left, right, (((1,), (1,)), ((), ())), preferred_element_type=F32)


def total(mask, axis):
    return jnp.sum(jnp.where(mask, 1.0, 0.0), axis=axis, keepdims=True).astype(jnp.int32)


def bag_numbers(plan, bags, pack):
    number = jnp.zeros_like(plan)
    for bag in range(1, bags):
        number += (plan >= bag * pack).astype(jnp.int32)
    return number


def order_kernel(bags, pack, plan_col, plan_row, tokens, even, odd, order_even, order_odd, where_row, where_col):
    count = plan_row.shape[1]
    bag_col = bag_numbers(plan_col[...], bags, pack)
    bag_row = bag_numbers(plan_row[...], bags, pack)
    same = bag_col == bag_row
    above = iota((count, count), 0) < iota((count, count), 1)
    below = iota((count, count), 0) > iota((count, count), 1)
    place_col = total(same & below, 1)
    place_row = total(same & above, 0)
    part_col = place_col & 1
    part_row = place_row & 1
    for part, (ordered, order) in enumerate(((even, order_even), (odd, order_odd))):
        rank_row = total(above & (part_col == part), 0)
        rows = ordered.shape[0]
        onehot = ((iota((rows, count), 0) == rank_row) & (part_row == part)).astype(F32).astype(BF16)
        order[...] = onehot
        ordered[...] = dot(onehot, tokens[...]).astype(BF16)
    where_row[...] = bag_row * 65536 + place_row
    where_col[...] = bag_col * 65536 + place_col


def send_kernel(bags, pack, half, ends, modality, plan_row, where_row, where_col, order_even, order_odd,
                send_even, send_odd, kind_even, kind_odd, final):
    count = plan_row.shape[1]
    slots = bags * half
    bag_row = where_row[...] >> 16
    place_row = where_row[...] & 65535
    bag_col = where_col[...] >> 16
    place_col = where_col[...] & 65535
    plan = plan_row[...]
    kind = jnp.zeros((1, count), F32)
    for bag in range(bags):
        begin = bag * pack
        for sample in range(ends.shape[1]):
            end = bag * pack + ends[bag, sample]
            inside = (plan >= begin) & (plan < end)
            kind = jnp.where(inside, modality[bag, sample].astype(F32), kind)
            begin = end
    slot_row = bag_row * half + (place_row >> 1)
    for part, (order, send, kinds) in enumerate(((order_even, send_even, kind_even), (order_odd, send_odd, kind_odd))):
        target = (iota((slots, count), 0) == slot_row) & ((place_row & 1) == part)
        send[...] = dot_nt(target.astype(F32).astype(BF16), order[...]).astype(BF16)
        picked = jnp.sum(order[...].astype(F32) * kind, axis=1, keepdims=True)
        kinds[...] = jnp.broadcast_to(picked, kinds.shape)
    back_col = bag_col * (2 * half) + (place_col & 1) * half + (place_col >> 1)
    final[...] = (iota(final.shape, 1) == back_col).astype(F32).astype(BF16)


def bag_kernel(pack, half, me, ends, plan, pack_even, pack_odd, back, samples, held):
    homes, count = plan.shape
    slot = plan[...] - me[0] * pack
    mine = (slot >= 0) & (slot < pack)
    ahead = (iota((count, count), 0) < iota((count, count), 1)).astype(F32).astype(BF16)
    place = dot(mine.astype(F32).astype(BF16), ahead).astype(jnp.int32)
    place = jnp.where(mine, place, -1)
    filled = total(mine, 1)
    first = 0
    for part, packer in enumerate((pack_even, pack_odd)):
        rows, slots = packer.shape
        lanes = iota((1, slots), 1)
        shift = jnp.zeros((1, slots), jnp.int32)
        limit = jnp.zeros((1, slots), jnp.int32)
        start = jnp.zeros((1, 1), jnp.int32)
        for home in range(homes):
            here = (filled[home:home + 1, :] + (1 - part)) >> 1
            of_home = (lanes >= home * half) & (lanes < (home + 1) * half)
            shift = jnp.where(of_home, start - home * half, shift)
            limit = jnp.where(of_home, here + home * half, limit)
            down = iota((half, back.shape[1]), 0)
            across = iota((half, back.shape[1]), 1)
            block = ((across == down + start + first) & (down < here)).astype(F32).astype(BF16)
            at = (home * 2 + part) * half
            back[at:at + half, :] = block
            chosen = place[home:home + 1, :] == iota((half, count), 0) * 2 + part
            slot_here = jnp.sum(jnp.where(chosen, slot[home:home + 1, :].astype(F32), 0.0), axis=1, keepdims=True)
            slot_here = slot_here.astype(jnp.int32)
            number = jnp.ones((half, 1), jnp.int32)
            for sample in range(ends.shape[1]):
                number += (slot_here >= ends[me[0], sample]).astype(jnp.int32)
            held[home * half:(home + 1) * half, :] = jnp.broadcast_to(number.astype(F32), (half, held.shape[1])).astype(BF16)
            start = start + here
        onehot = ((iota((rows, slots), 0) == lanes + shift) & (lanes < limit)).astype(F32).astype(BF16)
        packer[...] = onehot
        samples[first:first + rows, :] = dot(onehot, held[...])
        first += rows


def project_kernel(rows_in, kinds, weight, send, out):
    rows = rows_in[...]
    image = dot(rows, weight[0])
    video = dot(rows, weight[1])
    projected = jnp.where(kinds[:, :1] == 0.0, image, video).astype(BF16)
    out[...] = dot(send[...], projected).astype(BF16)


def project(rows_in, kinds, weight, send):
    rows, depth = rows_in.shape
    width = weight.shape[2]
    step = 256 if width % 256 == 0 else width
    slots = send.shape[0]
    return pl.pallas_call(
        project_kernel,
        grid=(width // step,),
        in_specs=[
            pl.BlockSpec((rows, depth), lambda i: (0, 0)),
            pl.BlockSpec(kinds.shape, lambda i: (0, 0)),
            pl.BlockSpec((2, depth, step), lambda i: (0, 0, i)),
            pl.BlockSpec(send.shape, lambda i: (0, 0)),
        ],
        out_specs=pl.BlockSpec((slots, step), lambda i: (0, i)),
        out_shape=jax.ShapeDtypeStruct((slots, width), BF16),
        compiler_params=params(),
        cost_estimate=pl.CostEstimate(
            flops=4 * rows * depth * width, bytes_accessed=weight.size * 2, transcendentals=0
        ),
        name="project",
    )(rows_in, kinds, weight, send)


def split_dot(value, square):
    high = value.astype(BF16)
    low = (value - high.astype(F32)).astype(BF16)
    return dot(high, square) + dot(low, square)


def qkv_kernel(rows_in, weight, gain, queries, keys, values):
    rows = rows_in[...]
    step = weight.shape[2]
    square = (iota((step, step), 0) // HD == iota((step, step), 1) // HD).astype(F32) * (1.0 / HD)
    square = square.astype(BF16)
    for index, (out, scale) in enumerate(((queries, HD ** -0.5), (keys, 1.0))):
        raw = dot(rows, weight[index])
        shifted = raw - split_dot(raw, square)
        spread = split_dot(shifted * shifted, square)
        out[...] = (shifted * lax.rsqrt(spread + EPSILON) * gain[index:index + 1, :] * scale).astype(BF16)
    values[...] = dot(rows, weight[2]).astype(BF16)


def make_qkv(rows_in, weight, gain):
    rows, depth = rows_in.shape
    width = weight.shape[2]
    step = 256 if width % 256 == 0 else 128
    part = pl.BlockSpec((rows, step), lambda i: (0, i))
    shape = jax.ShapeDtypeStruct((rows, width), BF16)
    return pl.pallas_call(
        qkv_kernel,
        grid=(width // step,),
        in_specs=[
            pl.BlockSpec((rows, depth), lambda i: (0, 0)),
            pl.BlockSpec((3, depth, step), lambda i: (0, 0, i)),
            pl.BlockSpec((2, step), lambda i: (0, i)),
        ],
        out_specs=[part] * 3,
        out_shape=[shape] * 3,
        compiler_params=params(),
        cost_estimate=pl.CostEstimate(
            flops=6 * rows * depth * width, bytes_accessed=weight.size * 2, transcendentals=0
        ),
        name="qkv",
    )(rows_in, weight, gain)


def attend_kernel(sample_col, sample_row, qa, ka, va, qb, kb, vb, out, bias, keys, values):
    first = qa.shape[0]
    second = qb.shape[0]

    @pl.when(pl.program_id(0) == 0)
    def _():
        bias[...] = jnp.where(sample_col[:, :1] == sample_row[...], 0.0, -1e30)

    keys[:first, :] = ka[...]
    keys[first:, :] = kb[...]
    values[:first, :] = va[...]
    values[first:, :] = vb[...]
    width = qa.shape[1]
    for part, begin, rows in ((qa, 0, first), (qb, first, second)):
        count = 3 if rows % 48 == 0 else 2
        step = rows // count
        for block in range(count):
            low = block * step
            query = part[low:low + step, :]
            lanes = iota((step, width), 1)
            result = jnp.zeros((step, width), F32)
            for head in range(width // HD):
                own = (lanes >= head * HD) & (lanes < (head + 1) * HD)
                masked = jnp.where(own, query, jnp.zeros_like(query))
                scores = dot_nt(masked, keys[...]) + bias[begin + low:begin + low + step, :]
                top = jnp.max(scores, axis=1, keepdims=True)
                raised = jnp.exp(scores - top)
                weight = jnp.sum(raised, axis=1, keepdims=True)
                mixed = dot(raised.astype(BF16), values[...]) / weight
                result = jnp.where(own, mixed, result)
            out[begin + low:begin + low + step, :] = result.astype(BF16)


def attend(sample_col, sample_row, parts_a, parts_b):
    first, width = parts_a[0].shape
    second = parts_b[0].shape[0]
    rows = first + second
    step = 2 * HD
    spec_a = pl.BlockSpec((first, step), lambda i: (0, i))
    spec_b = pl.BlockSpec((second, step), lambda i: (0, i))
    return pl.pallas_call(
        attend_kernel,
        grid=(width // step,),
        in_specs=[
            pl.BlockSpec(sample_col.shape, lambda i: (0, 0)),
            pl.BlockSpec(sample_row.shape, lambda i: (0, 0)),
        ] + [spec_a] * 3 + [spec_b] * 3,
        out_specs=pl.BlockSpec((rows, step), lambda i: (0, i)),
        out_shape=jax.ShapeDtypeStruct((rows, width), BF16),
        scratch_shapes=[
            pltpu.VMEM((rows, rows), F32),
            pltpu.VMEM((rows, step), BF16),
            pltpu.VMEM((rows, step), BF16),
        ],
        compiler_params=params(),
        cost_estimate=pl.CostEstimate(
            flops=4 * rows * rows * width, bytes_accessed=8 * rows * width, transcendentals=rows * rows * width // HD
        ),
        name="attend",
    )(sample_col, sample_row, *parts_a, *parts_b)


def line_sum(partial, width):
    members = lax.axis_size("bag")
    mine = lax.axis_index("bag")

    def piece(index):
        index = jnp.clip(index, 0, members - 1)
        return lax.dynamic_slice_in_dim(partial, index * width, width, 1).astype(F32)

    up = down = None
    for step in range(1, members):
        to_up = piece(members - step + mine)
        to_down = piece(mine + step - members)
        if step > 1:
            to_up = to_up + up.astype(F32)
            to_down = to_down + down.astype(F32)
        up = lax.ppermute(to_up.astype(BF16), "bag", [(i, i + 1) for i in range(step)])
        down = lax.ppermute(to_down.astype(BF16), "bag", [(i, i - 1) for i in range(members - step, members)])
    return (piece(mine) + up.astype(F32) + down.astype(F32)).astype(BF16)


def body(
    home_tokens,
    mod_weight,
    qkv_weight,
    norm_gain,
    output_weight,
    row_plan,
    sample_lengths,
    modality,
):
    bags = lax.axis_size("dp")
    me = lax.axis_index("dp")
    count, width = home_tokens.shape
    pack = count + count // 4
    capacity = 2 * count // bags
    half = capacity // 2
    slots = bags * half
    home_rows = (up16(count // 2 + bags // 2), up16(count // 2))
    bag_rows = (up16(pack // 2 + bags // 2), up16(pack // 2))
    rows = sum(bag_rows)
    vmem = pl.BlockSpec(memory_space=pltpu.VMEM)
    smem = pl.BlockSpec(memory_space=pltpu.SMEM)
    ends = jnp.cumsum(sample_lengths, axis=1)

    own_plan = lax.dynamic_slice_in_dim(row_plan, me * count, count, 0)
    plan_row = own_plan.reshape(1, count)
    plan_col = own_plan.reshape(count, 1)
    orders = [jax.ShapeDtypeStruct((size, count), BF16) for size in home_rows]
    ordered = [jax.ShapeDtypeStruct((size, width), BF16) for size in home_rows]
    even, odd, order_even, order_odd, where_row, where_col = pl.pallas_call(
        functools.partial(order_kernel, bags, pack),
        in_specs=[vmem] * 3,
        out_specs=[vmem] * 6,
        out_shape=ordered + orders + [
            jax.ShapeDtypeStruct((1, count), jnp.int32),
            jax.ShapeDtypeStruct((count, 1), jnp.int32),
        ],
        compiler_params=params(),
        name="order",
    )(plan_col, plan_row, home_tokens)
    full_even = lax.all_gather(even, "bag", axis=1, tiled=True)
    full_odd = lax.all_gather(odd, "bag", axis=1, tiled=True)

    send_even, send_odd, kind_even, kind_odd, final = pl.pallas_call(
        functools.partial(send_kernel, bags, pack, half),
        in_specs=[smem, smem] + [vmem] * 5,
        out_specs=[vmem] * 5,
        out_shape=[jax.ShapeDtypeStruct((slots, size), BF16) for size in home_rows]
        + [jax.ShapeDtypeStruct((size, 128), F32) for size in home_rows]
        + [jax.ShapeDtypeStruct((count, 2 * slots), BF16)],
        compiler_params=params(),
        name="send_plan",
    )(ends, modality, plan_row, where_row, where_col, order_even, order_odd)
    pack_even, pack_odd, back, samples = pl.pallas_call(
        functools.partial(bag_kernel, pack, half),
        in_specs=[smem, smem, vmem],
        out_specs=[vmem] * 4,
        out_shape=[jax.ShapeDtypeStruct((size, slots), BF16) for size in bag_rows]
        + [jax.ShapeDtypeStruct((2 * slots, rows), BF16), jax.ShapeDtypeStruct((rows, 128), F32)],
        scratch_shapes=[pltpu.VMEM((slots, 128), BF16)],
        compiler_params=params(),
        name="bag_plan",
    )(me.reshape(1).astype(jnp.int32), ends, row_plan.reshape(bags, count))
    sample_row = samples[:, 0].reshape(1, rows)

    def to_bag(full, kinds, send, packer):
        outgoing = project(full, kinds, mod_weight, send).reshape(bags, half, width)
        arrived = lax.all_to_all(outgoing, "dp", split_axis=0, concat_axis=0, tiled=True)
        packed = dot(packer, arrived.reshape(slots, width)).astype(BF16)
        return lax.all_gather(packed, "bag", axis=1, tiled=True)

    bag_even = to_bag(full_even, kind_even, send_even, pack_even)
    bag_odd = to_bag(full_odd, kind_odd, send_odd, pack_odd)
    parts_even = make_qkv(bag_even, qkv_weight, norm_gain)
    parts_odd = make_qkv(bag_odd, qkv_weight, norm_gain)
    attended = attend(samples, sample_row, parts_even, parts_odd)
    partial = dot(attended, output_weight).astype(BF16)
    summed = line_sum(partial, width)
    outgoing = dot(back, summed).astype(BF16).reshape(bags, capacity, width)
    returned = lax.all_to_all(outgoing, "dp", split_axis=0, concat_axis=0, tiled=True)
    return dot(final, returned.reshape(bags * capacity, width)).astype(BF16)


def solution(mesh):
    in_specs = (
        P("dp", "bag"),
        P(None, None, "bag"),
        P(None, None, "bag"),
        P(None, "bag"),
        P("bag", None),
        P(),
        P(),
        P(),
    )
    return jax.shard_map(body, mesh=mesh, in_specs=in_specs, out_specs=P("dp", "bag"), check_vma=False)
```

time: 457 us -> 368 us (0.81)
  waiting for transfers between devices: 277 us -> 186 us
  Pallas kernels: 0 us -> 78.9 us
  local copies, waits for them, and re-layouts: 58.9 us -> 5.68 us
  blocking collectives: 0 us -> 40.8 us
  matrix products: 51.7 us -> 14.6 us
  other arithmetic: 45.1 us -> 8.15 us
  starting transfers between devices: 7.31 us -> 19.7 us
    all_to_all x2 -> x1, waiting for transfers between devices: 138 us -> 8.2 us  [to_bag(): lax.all_to_all(outgoing, 'dp', split_axis=0, concat_axis=0, tiled=True)]
    ppermute x0 -> x6, waiting for transfers between devices: none -> 80.2 us  [the longest x3 56 us: line_sum(): lax.ppermute(to_up.astype(BF16), 'bag', [(i, i + 1) for i in range(step)])]
    pallas_call x0 -> x8, Pallas kernels: none -> 78.9 us  [the longest x2 29.2 us: make_qkv(): pl.pallas_call(qkv_kernel, grid=(width // step,), in_specs=[pl.BlockSpec(...]
    all_gather x2 -> x4, waiting for transfers between devices: 139 us -> 96.6 us  [the longest x2 49.1 us: to_bag(): return lax.all_gather(packed, 'bag', axis=1, tiled=True)]
    all_to_all x0 -> x2, blocking collectives: none -> 40.8 us  [the longest x1 24.5 us: body(): lax.all_to_all(outgoing, 'dp', split_axis=0, concat_axis=0, tiled=True)]
    dot_general x10 -> x5, matrix products: 51.7 us -> 14.6 us  [dot(): return jnp.dot(left, right, preferred_element_type=F32)]
    gather x3 -> x0, local copies, waits for them, and re-layouts: 27.5 us -> none  [the longest x2 25.5 us: body(): jnp.take(partial_low, slot_table, axis=0, mode='fill', fill_value=0)]
    sub x1 -> x0, other arithmetic: 26 us -> none  [attend(): raised = jnp.exp(scores - row_max)]
  transfers between devices with their start and end apart: 4 -> 11, of which waited for: 4 -> 9; matrix products, arithmetic and copies ran while one was open for 5% -> 3% of each run, Pallas kernels for 0% -> 10%
where the time goes in v1:
time: 368 us; the launch traced here: 367 us
  waiting for transfers between devices  186 us (51%)
  Pallas kernels  78.9 us (21%)
  blocking collectives  40.8 us (11%)
  starting transfers between devices  19.7 us (5%)
  matrix products  14.6 us (4%)
  between operations  13.3 us (4%)
  other arithmetic  8.15 us (2%)
  local copies, waits for them, and re-layouts  5.68 us (2%)
    ppermute x3, waiting for transfers between devices, line_sum(): lax.ppermute(to_up.astype(BF16), 'bag', [(i, i + 1) for i in range(step)])  56 us
    all_gather x2, waiting for transfers between devices, to_bag(): return lax.all_gather(packed, 'bag', axis=1, tiled=True)  49.1 us
    all_gather x1, waiting for transfers between devices, body(): full_odd = lax.all_gather(odd, 'bag', axis=1, tiled=True)  34.7 us
    pallas_call x2, Pallas kernels, make_qkv(): pl.pallas_call(qkv_kernel, grid=(width // step,), in_specs=[pl.BlockSpec(...  29.2 us
    all_to_all x1, blocking collectives, body(): lax.all_to_all(outgoing, 'dp', split_axis=0, concat_axis=0, tiled=True)  24.5 us
    ppermute x3, waiting for transfers between devices, line_sum(): lax.ppermute(to_down.astype(BF16), 'bag', [(i, i - 1) for i in range(memb...  24.2 us
    pallas_call x1, Pallas kernels, attend(): pl.pallas_call(attend_kernel, grid=(width // step,), in_specs=[pl.BlockSp...  24.1 us
    all_to_all x1, blocking collectives, to_bag(): lax.all_to_all(outgoing, 'dp', split_axis=0, concat_axis=0, tiled=True)  16.3 us
  transfers between devices with their start and end apart: 11, of which 9 were waited for; matrix products, arithmetic and copies ran while one was open for 3% of the time, Pallas kernels for 10%

profile of v1, /device:TPU:0, one launch (start us, length us, event | category | flops | bytes accessed | tf_op | source)
XLA Modules:
  0.0 367.0 jit_solution(179712126993853325)
XLA Ops:
  6.5 0.0 copy-start.5
  6.5 0.0 all-gather.9.cloned.1.call-start
  6.5 0.8 dynamic_slice.24
  7.3 0.9 copy.12.plan_col
  8.2 0.0 copy-done.3
  8.2 3.3 order.1
  11.4 0.0 all-gather.9.cloned.1.call-update
  11.5 0.0 all-gather.5.cloned.1.call-start
  11.5 0.7 all-gather.5.cloned.1.call-update
  12.2 0.0 copy-done.5
  12.2 0.1 copy.11
  12.3 0.7 reduce_window_sum.11.ends
  13.1 0.0 copy-done.6
  13.1 0.7 copy.13.modality
  13.7 3.0 send_plan.1
  16.8 34.7 %all-gather.9.cloned.1.call-done.rows_in = bf16[256,3072]{1,0:T(8,128)(2,1)} async-done(((bf16[256,768]{1,0:T(8,128)(2,1)}), bf16[256,3072]{1,0:T(8,128)(2,1)}) %all-gather.9.cloned.1.call-update) | async-done | bytes 1572880 | tf_op jit(solution)/shard_map/all_gather | solution.py:333
  51.4 7.7 %project.3 = bf16[512,768]{1,0:T(8,128)(2,1)} custom-call(bf16[256,3072]{1,0:T(8,128)(2,1)} %all-gather.9.cloned.1.call-done.rows_in, f32[256,128]{1,0:T(8,128)} %get-tuple-element.42.kinds, bf16[2,3072,768]{2,1,0:T(8,128)(2,1)} %weight.6, bf16[512,256]{1,0:T(8,128)(2,1)} %get-tuple-element.43.send), custom_call_target="tpu_custom_call" | custom-call | flops 2415919104 | bytes 9437184 | tf_op jit(solution)/shard_map/project/pallas_call | solution.py:148
  59.2 3.7 all-to-all-start.1
  62.8 0.0 all-gather.11.cloned.1.call-start
  62.9 0.0 copy-done.4
  62.9 0.6 reshape.33.plan
  63.5 3.7 %bag_plan.1 = (bf16[336,512]{1,0:T(8,128)(2,1)}, bf16[320,512]{1,0:T(8,128)(2,1)}, bf16[1024,656]{1,0:T(8,128)(2,1)}, f32[656,128]{1,0:T(8,128)}) custom-call(s32[1]{0:T(128)} %bitcast.2.me, s32[8,4]{1,0:T(8,128)} %reduce_window_sum.11.ends, s32[8,512]{1,0:T(8,128)} %reshape.33.plan), custom_call_target="tpu_custom_call" | custom-call | tf_op jit(solution)/shard_map/bag_plan/pallas_call | solution.py:345
  67.2 8.2 %all-to-all-done.1 = bf16[8,64,768]{2,1,0:T(8,128)(2,1)S(1)} async-done(((bf16[8,64,768]{2,1,0:T(8,128)(2,1)}), bf16[8,64,768]{2,1,0:T(8,128)(2,1)S(1)}, u32[]{:S(2)}, u32[]{:S(2)}) %all-to-all-start.1) | async-done | bytes 786464 | tf_op jit(solution)/shard_map/all_to_all | solution.py:359
  75.4 2.2 convolution_convert_fusion.4
  77.6 0.0 all-gather.11.cloned.1.call-update
  77.6 0.0 all-gather.7.cloned.1.call-start
  77.7 12.9 %all-gather.5.cloned.1.call-done.rows_in = bf16[272,3072]{1,0:T(8,128)(2,1)} async-done(((bf16[272,768]{1,0:T(8,128)(2,1)}), bf16[272,3072]{1,0:T(8,128)(2,1)}) %all-gather.5.cloned.1.call-update) | async-done | bytes 1671184 | tf_op jit(solution)/shard_map/all_gather | solution.py:332
  90.6 7.8 %project.2 = bf16[512,768]{1,0:T(8,128)(2,1)} custom-call(bf16[272,3072]{1,0:T(8,128)(2,1)} %all-gather.5.cloned.1.call-done.rows_in, f32[272,128]{1,0:T(8,128)} %get-tuple-element.35.kinds, bf16[2,3072,768]{2,1,0:T(8,128)(2,1)} %weight.6, bf16[512,272]{1,0:T(8,128)(2,1)} %get-tuple-element.36.send), custom_call_target="tpu_custom_call" | custom-call | flops 2566914048 | bytes 9437184 | tf_op jit(solution)/shard_map/project/pallas_call | solution.py:148
  98.4 16.3 %all_to_all.15 = bf16[8,64,768]{2,1,0:T(8,128)(2,1)S(1)} all-to-all(bf16[8,64,768]{2,1,0:T(8,128)(2,1)} %bitcast.21), channel_id=1, replica_groups=mesh['dp'=8,'bag'=4] {'dp'}, dimensions={0} | all-to-all | bytes 1572864 | tf_op jit(solution)/shard_map/all_to_all | solution.py:359
  114.8 0.0 copy-done.1
  114.8 1.2 convolution_convert_fusion.3
  116.0 0.0 all-gather.7.cloned.1.call-update
  116.0 0.0 copy-done.2
  116.0 0.2 slice_reduce_fusion
  116.2 0.6 reshape_squeeze.3.sample_row
  116.8 17.8 %all-gather.11.cloned.1.call-done.rows_in = bf16[320,3072]{1,0:T(8,128)(2,1)} async-done(((bf16[320,768]{1,0:T(8,128)(2,1)}), bf16[320,3072]{1,0:T(8,128)(2,1)}) %all-gather.11.cloned.1.call-update) | async-done | bytes 1966096 | tf_op jit(solution)/shard_map/all_gather | solution.py:361
  134.6 14.4 %qkv.3 = (bf16[320,768]{1,0:T(8,128)(2,1)}, bf16[320,768]{1,0:T(8,128)(2,1)}, bf16[320,768]{1,0:T(8,128)(2,1)}) custom-call(bf16[320,3072]{1,0:T(8,128)(2,1)} %all-gather.11.cloned.1.call-done.rows_in, bf16[3,3072,768]{2,1,0:T(8,128)(2,1)} %weight.7, f32[2,768]{1,0:T(2,128)} %gain.3), custom_call_target="tpu_custom_call" | custom-call | flops 4529848320 | bytes 14155776 | tf_op jit(solution)/shard_map/qkv/pallas_call | solution.py:192
  149.0 31.2 %all-gather.7.cloned.1.call-done.rows_in = bf16[336,3072]{1,0:T(8,128)(2,1)} async-done(((bf16[336,768]{1,0:T(8,128)(2,1)}), bf16[336,3072]{1,0:T(8,128)(2,1)}) %all-gather.7.cloned.1.call-update) | async-done | bytes 2064400 | tf_op jit(solution)/shard_map/all_gather | solution.py:361
  180.2 14.8 %qkv.2 = (bf16[336,768]{1,0:T(8,128)(2,1)}, bf16[336,768]{1,0:T(8,128)(2,1)}, bf16[336,768]{1,0:T(8,128)(2,1)}) custom-call(bf16[336,3072]{1,0:T(8,128)(2,1)} %all-gather.7.cloned.1.call-done.rows_in, bf16[3,3072,768]{2,1,0:T(8,128)(2,1)} %weight.7, f32[2,768]{1,0:T(2,128)} %gain.3), custom_call_target="tpu_custom_call" | custom-call | flops 4756340736 | bytes 14155776 | tf_op jit(solution)/shard_map/qkv/pallas_call | solution.py:192
  195.1 24.1 %attend.1 = bf16[656,768]{1,0:T(8,128)(2,1)} custom-call(f32[656,128]{1,0:T(8,128)} %get-tuple-element.32.sample_col, f32[1,656]{1,0:T(1,128)} %reshape_squeeze.3.sample_row, bf16[336,768]{1,0:T(8,128)(2,1)} %get-tuple-element.37.qa, bf16[336,768]{1,0:T(8,128)(2,1)} %get-tuple-element.38.ka, bf16[336,768]{1,0:T(8,128)(2,1)} %get-tuple-element.39.va, ...), custom_call_target="tpu_custom_call" | custom-call | flops 1321992192 | bytes 4030464 | tf_op jit(solution)/shard_map/attend/pallas_call | solution.py:250
  219.2 5.9 %convolution_convert_fusion = bf16[656,3072]{1,0:T(8,128)(2,1)S(1)} fusion(bf16[656,768]{1,0:T(8,128)(2,1)} %attend.1, bf16[768,3072]{1,0:T(8,128)(2,1)} %param.12), kind=kOutput, calls=%fused_computation | convolution fusion | flops 3097411584 | bytes 9756672 | tf_op jit(solution)/shard_map/dot_general | solution.py:30
  225.1 0.0 copy-start
  225.2 0.2 constant_dynamic-slice_fusion.1
  225.4 1.7 copy-done
  227.1 2.8 collective-permute-start
  229.9 0.7 collective-permute-start.3
  230.6 19.6 %collective-permute-done = bf16[656,768]{1,0:T(8,128)(2,1)} collective-permute-done((bf16[656,768]{1,0:T(8,128)(2,1)S(1)}, bf16[656,768]{1,0:T(8,128)(2,1)}, u32[]{:S(2)}, u32[]{:S(2)}) %collective-permute-start) | collective-permute-done | bytes 1007648 | tf_op jit(solution)/shard_map/ppermute | solution.py:287
  250.2 2.8 add_convert_fusion.4
  253.0 4.5 %collective-permute-start.1 = (bf16[656,768]{1,0:T(8,128)(2,1)}, bf16[656,768]{1,0:T(8,128)(2,1)S(1)}, u32[]{:S(2)}, u32[]{:S(2)}) collective-permute-start(bf16[656,768]{1,0:T(8,128)(2,1)} %add_convert_fusion.4), channel_id=1, source_target_pairs={{0,1},{1,2},{4,5},{5,6},{8,9},{9,10},{12,13},{13,14},{16,17},{17,1... | collective-permute-start | bytes 3022856 | tf_op jit(solution)/shard_map/ppermute | solution.py:287
  257.6 0.0 collective-permute-done.3
  257.6 20.7 %collective-permute-done.1 = bf16[656,768]{1,0:T(8,128)(2,1)S(1)} collective-permute-done((bf16[656,768]{1,0:T(8,128)(2,1)}, bf16[656,768]{1,0:T(8,128)(2,1)S(1)}, u32[]{:S(2)}, u32[]{:S(2)}) %collective-permute-start.1) | collective-permute-done | bytes 1007648 | tf_op jit(solution)/shard_map/ppermute | solution.py:287
  278.2 3.1 add_convert_fusion.3
  281.3 0.7 collective-permute-start.4
  282.1 5.8 %collective-permute-start.2 = (bf16[656,768]{1,0:T(8,128)(2,1)S(1)}, bf16[656,768]{1,0:T(8,128)(2,1)}, u32[]{:S(2)}, u32[]{:S(2)}) collective-permute-start(bf16[656,768]{1,0:T(8,128)(2,1)S(1)} %get-tuple-element.47), channel_id=1, source_target_pairs={{0,1},{1,2},{2,3},{4,5},{5,6},{6,7},{8,9},{9,10},{10,11},{12,13},{... | collective-permute-start | bytes 3022856 | tf_op jit(solution)/shard_map/ppermute | solution.py:287
  287.9 0.0 collective-permute-done.4
  287.9 1.5 add_convert_fusion.1
  289.4 1.3 collective-permute-start.5
  290.7 15.7 %collective-permute-done.2 = bf16[656,768]{1,0:T(8,128)(2,1)} collective-permute-done((bf16[656,768]{1,0:T(8,128)(2,1)S(1)}, bf16[656,768]{1,0:T(8,128)(2,1)}, u32[]{:S(2)}, u32[]{:S(2)}) %collective-permute-start.2) | collective-permute-done | bytes 1007648 | tf_op jit(solution)/shard_map/ppermute | solution.py:287
  306.4 24.2 %collective-permute-done.5 = bf16[656,768]{1,0:T(8,128)(2,1)S(1)} collective-permute-done((bf16[656,768]{1,0:T(8,128)(2,1)S(1)}, bf16[656,768]{1,0:T(8,128)(2,1)S(1)}, u32[]{:S(2)}, u32[]{:S(2)}) %collective-permute-start.5) | collective-permute-done | bytes 1007648 | tf_op jit(solution)/shard_map/ppermute | solution.py:288
  330.6 3.5 convolution_convert_fusion.1
  334.1 0.0 copy-start.7
  334.1 24.5 %all_to_all.16 = bf16[8,128,768]{2,1,0:T(8,128)(2,1)S(1)} all-to-all(bf16[8,128,768]{2,1,0:T(8,128)(2,1)S(1)} %bitcast.22), channel_id=1, replica_groups=mesh['dp'=8,'bag'=4] {'dp'}, dimensions={0} | all-to-all | bytes 3145728 | tf_op jit(solution)/shard_map/all_to_all | solution.py:371
  358.6 0.0 copy-done.7
  358.6 1.9 convolution_convert_fusion.2
  (5 shorter events, 0.0 us)
Async XLA Ops:
  6.5 5.7 %copy-start.5 = (s32[8,4]{0,1:T(4,128)S(1)}, s32[8,4]{0,1:T(4,128)}, u32[]{:S(2)}) copy-start(s32[8,4]{0,1:T(4,128)} %param.14) | copy-start | bytes 388
  6.5 6.5 %copy-start.6 = (s32[8,4]{0,1:T(4,128)S(1)}, s32[8,4]{0,1:T(4,128)}, u32[]{:S(2)}) copy-start(s32[8,4]{0,1:T(4,128)} %param.15) | copy-start | bytes 388
  6.5 44.9 %all-gather.9.cloned.1.call-start = ((), (), s32[]{:S(2)}) async-start(), calls=%async_computation.5 | async-start | bytes 1966080 | tf_op jit(solution)/shard_map/all_gather | solution.py:333
  7.3 0.9 copy-start.3
  11.5 79.1 %all-gather.5.cloned.1.call-start = ((), (), s32[]{:S(2)}) async-start(), calls=%async_computation.3 | async-start | bytes 2088960 | tf_op jit(solution)/shard_map/all_gather | solution.py:332
  51.4 11.4 %copy-start.4 = (s32[4096]{0:T(1024)S(1)}, s32[4096]{0:T(1024)}, u32[]{:S(2)}) copy-start(s32[4096]{0:T(1024)} %param.13) | copy-start | bytes 49156
  59.2 16.3 %all-to-all-start.1 = ((bf16[8,64,768]{2,1,0:T(8,128)(2,1)}), bf16[8,64,768]{2,1,0:T(8,128)(2,1)S(1)}, u32[]{:S(2)}, u32[]{:S(2)}) async-start(bf16[8,64,768]{2,1,0:T(8,128)(2,1)} %bitcast.18), calls=%async_computation.1 | async-start | bytes 1572864 | tf_op jit(solution)/shard_map/all_to_all | solution.py:359
  62.8 71.8 %all-gather.11.cloned.1.call-start = ((), (), s32[]{:S(2)}) async-start(), calls=%async_computation.6 | async-start | bytes 2457600 | tf_op jit(solution)/shard_map/all_gather | solution.py:361
  77.6 102.6 %all-gather.7.cloned.1.call-start = ((), (), s32[]{:S(2)}) async-start(), calls=%async_computation.4 | async-start | bytes 2580480 | tf_op jit(solution)/shard_map/all_gather | solution.py:361
  90.6 24.2 %copy-start.1 = (bf16[336,512]{1,0:T(8,128)(2,1)S(1)}, bf16[336,512]{1,0:T(8,128)(2,1)}, u32[]{:S(2)}) copy-start(bf16[336,512]{1,0:T(8,128)(2,1)} %get-tuple-element.33) | copy-start | bytes 1032196
  98.4 17.6 %copy-start.2 = (f32[656,128]{1,0:T(8,128)S(1)}, f32[656,128]{1,0:T(8,128)}, u32[]{:S(2)}) copy-start(f32[656,128]{1,0:T(8,128)} %get-tuple-element.32.sample_col) | copy-start | bytes 1007620
  225.1 1.9 copy-start
  227.1 23.2 %collective-permute-start = (bf16[656,768]{1,0:T(8,128)(2,1)S(1)}, bf16[656,768]{1,0:T(8,128)(2,1)}, u32[]{:S(2)}, u32[]{:S(2)}) collective-permute-start(bf16[656,768]{1,0:T(8,128)(2,1)S(1)} %get-tuple-element.49), channel_id=1, source_target_pairs={{0,1},{4,5},{8,9},{12,13},{16,17},{20,21},{24,25},{28,29}} | collective-permute-start | bytes 3022856 | tf_op jit(solution)/shard_map/ppermute | solution.py:287
  229.9 27.7 %collective-permute-start.3 = (bf16[656,768]{1,0:T(8,128)(2,1)S(1)}, bf16[656,768]{1,0:T(8,128)(2,1)S(1)}, u32[]{:S(2)}, u32[]{:S(2)}) collective-permute-start(bf16[656,768]{1,0:T(8,128)(2,1)S(1)} %get-tuple-element.50), channel_id=1, source_target_pairs={{3,2},{7,6},{11,10},{15,14},{19,18},{23,22},{27,26},{31,30}} | collective-permute-start | bytes 3022856 | tf_op jit(solution)/shard_map/ppermute | solution.py:288
  253.0 25.2 %collective-permute-start.1 = (bf16[656,768]{1,0:T(8,128)(2,1)}, bf16[656,768]{1,0:T(8,128)(2,1)S(1)}, u32[]{:S(2)}, u32[]{:S(2)}) collective-permute-start(bf16[656,768]{1,0:T(8,128)(2,1)} %add_convert_fusion.4), channel_id=1, source_target_pairs={{0,1},{1,2},{4,5},{5,6},{8,9},{9,10},{12,13},{13,14},{16,17},{17,1... | collective-permute-start | bytes 3022856 | tf_op jit(solution)/shard_map/ppermute | solution.py:287
  281.3 6.5 %collective-permute-start.4 = (bf16[656,768]{1,0:T(8,128)(2,1)}, bf16[656,768]{1,0:T(8,128)(2,1)S(1)}, u32[]{:S(2)}, u32[]{:S(2)}) collective-permute-start(bf16[656,768]{1,0:T(8,128)(2,1)} %get-tuple-element.48), channel_id=1, source_target_pairs={{2,1},{3,2},{6,5},{7,6},{10,9},{11,10},{14,13},{15,14},{18,17},{19... | collective-permute-start | bytes 3022856 | tf_op jit(solution)/shard_map/ppermute | solution.py:288
  282.1 24.4 %collective-permute-start.2 = (bf16[656,768]{1,0:T(8,128)(2,1)S(1)}, bf16[656,768]{1,0:T(8,128)(2,1)}, u32[]{:S(2)}, u32[]{:S(2)}) collective-permute-start(bf16[656,768]{1,0:T(8,128)(2,1)S(1)} %get-tuple-element.47), channel_id=1, source_target_pairs={{0,1},{1,2},{2,3},{4,5},{5,6},{6,7},{8,9},{9,10},{10,11},{12,13},{... | collective-permute-start | bytes 3022856 | tf_op jit(solution)/shard_map/ppermute | solution.py:287
  289.4 41.3 %collective-permute-start.5 = (bf16[656,768]{1,0:T(8,128)(2,1)S(1)}, bf16[656,768]{1,0:T(8,128)(2,1)S(1)}, u32[]{:S(2)}, u32[]{:S(2)}) collective-permute-start(bf16[656,768]{1,0:T(8,128)(2,1)S(1)} %add_convert_fusion.1), channel_id=1, source_target_pairs={{1,0},{2,1},{3,2},{5,4},{6,5},{7,6},{9,8},{10,9},{11,10},{13,12},{... | collective-permute-start | bytes 3022856 | tf_op jit(solution)/shard_map/ppermute | solution.py:288
  334.1 24.5 %copy-start.7 = (bf16[512,1024]{1,0:T(8,128)(2,1)S(1)}, bf16[512,1024]{1,0:T(8,128)(2,1)}, u32[]{:S(2)}) copy-start(bf16[512,1024]{1,0:T(8,128)(2,1)} %get-tuple-element.30) | copy-start | bytes 3145732
Sparse Core Ops, SparseCore 0:
  11.6 39.7 all-gather.8
  53.0 37.5 all-gather.4
  92.2 42.4 all-gather.10
  136.0 44.1 all-gather.6

commit v2 on v1

--- a/solution.py
+++ b/solution.py
@@ -67,7 +67,7 @@
 
 
 def send_kernel(bags, pack, half, ends, modality, plan_row, where_row, where_col, order_even, order_odd,
-                send_even, send_odd, kind_even, kind_odd, final):
+                send_even, send_odd, kind_even, kind_odd, final_even, final_odd):
     count = plan_row.shape[1]
     slots = bags * half
     bag_row = where_row[...] >> 16
@@ -89,11 +89,13 @@
         send[...] = dot_nt(target.astype(F32).astype(BF16), order[...]).astype(BF16)
         picked = jnp.sum(order[...].astype(F32) * kind, axis=1, keepdims=True)
         kinds[...] = jnp.broadcast_to(picked, kinds.shape)
-    back_col = bag_col * (2 * half) + (place_col & 1) * half + (place_col >> 1)
-    final[...] = (iota(final.shape, 1) == back_col).astype(F32).astype(BF16)
-
-
-def bag_kernel(pack, half, me, ends, plan, pack_even, pack_odd, back, samples, held):
+    slot_col = bag_col * half + (place_col >> 1)
+    for part, final in enumerate((final_even, final_odd)):
+        match = (iota((count, slots), 1) == slot_col) & ((place_col & 1) == part)
+        final[...] = match.astype(F32).astype(BF16)
+
+
+def bag_kernel(pack, half, me, ends, plan, pack_even, pack_odd, back_even, back_odd, samples, held):
     homes, count = plan.shape
     slot = plan[...] - me[0] * pack
     mine = (slot >= 0) & (slot < pack)
@@ -102,7 +104,7 @@
     place = jnp.where(mine, place, -1)
     filled = total(mine, 1)
     first = 0
-    for part, packer in enumerate((pack_even, pack_odd)):
+    for part, (packer, back) in enumerate(((pack_even, back_even), (pack_odd, back_odd))):
         rows, slots = packer.shape
         lanes = iota((1, slots), 1)
         shift = jnp.zeros((1, slots), jnp.int32)
@@ -115,9 +117,8 @@
             limit = jnp.where(of_home, here + home * half, limit)
             down = iota((half, back.shape[1]), 0)
             across = iota((half, back.shape[1]), 1)
-            block = ((across == down + start + first) & (down < here)).astype(F32).astype(BF16)
-            at = (home * 2 + part) * half
-            back[at:at + half, :] = block
+            block = ((across == down + start) & (down < here)).astype(F32).astype(BF16)
+            back[home * half:(home + 1) * half, :] = block
             chosen = place[home:home + 1, :] == iota((half, count), 0) * 2 + part
             slot_here = jnp.sum(jnp.where(chosen, slot[home:home + 1, :].astype(F32), 0.0), axis=1, keepdims=True)
             slot_here = slot_here.astype(jnp.int32)
@@ -175,12 +176,13 @@
     step = weight.shape[2]
     square = (iota((step, step), 0) // HD == iota((step, step), 1) // HD).astype(F32) * (1.0 / HD)
     square = square.astype(BF16)
-    for index, (out, scale) in enumerate(((queries, HD ** -0.5), (keys, 1.0))):
-        raw = dot(rows, weight[index])
+    raw_queries = dot(rows, weight[0])
+    raw_keys = dot(rows, weight[1])
+    values[...] = dot(rows, weight[2]).astype(BF16)
+    for index, (raw, out, scale) in enumerate(((raw_queries, queries, HD ** -0.5), (raw_keys, keys, 1.0))):
         shifted = raw - split_dot(raw, square)
         spread = split_dot(shifted * shifted, square)
-        out[...] = (shifted * lax.rsqrt(spread + EPSILON) * gain[index:index + 1, :] * scale).astype(BF16)
-    values[...] = dot(rows, weight[2]).astype(BF16)
+        out[...] = (shifted * lax.rsqrt(spread + EPSILON) * gain[0, index:index + 1, :] * scale).astype(BF16)
 
 
 def make_qkv(rows_in, weight, gain):
@@ -195,7 +197,7 @@
         in_specs=[
             pl.BlockSpec((rows, depth), lambda i: (0, 0)),
             pl.BlockSpec((3, depth, step), lambda i: (0, 0, i)),
-            pl.BlockSpec((2, step), lambda i: (0, i)),
+            pl.BlockSpec((1, 2, step), lambda i: (i, 0, 0)),
         ],
         out_specs=[part] * 3,
         out_shape=[shape] * 3,
@@ -204,12 +206,12 @@
             flops=6 * rows * depth * width, bytes_accessed=weight.size * 2, transcendentals=0
         ),
         name="qkv",
-    )(rows_in, weight, gain)
-
-
-def attend_kernel(sample_col, sample_row, qa, ka, va, qb, kb, vb, out, bias, keys, values):
-    first = qa.shape[0]
-    second = qb.shape[0]
+    )(rows_in, weight, gain.reshape(2, width // step, step).transpose(1, 0, 2))
+
+
+def attend_kernel(sample_col, sample_row, query, ka, va, kb, vb, out, bias, keys, values):
+    first = ka.shape[0]
+    count, width = query.shape
 
     @pl.when(pl.program_id(0) == 0)
     def _():
@@ -219,32 +221,26 @@
     keys[first:, :] = kb[...]
     values[:first, :] = va[...]
     values[first:, :] = vb[...]
-    width = qa.shape[1]
-    for part, begin, rows in ((qa, 0, first), (qb, first, second)):
-        count = 3 if rows % 48 == 0 else 2
-        step = rows // count
-        for block in range(count):
-            low = block * step
-            query = part[low:low + step, :]
-            lanes = iota((step, width), 1)
-            result = jnp.zeros((step, width), F32)
-            for head in range(width // HD):
-                own = (lanes >= head * HD) & (lanes < (head + 1) * HD)
-                masked = jnp.where(own, query, jnp.zeros_like(query))
-                scores = dot_nt(masked, keys[...]) + bias[begin + low:begin + low + step, :]
-                top = jnp.max(scores, axis=1, keepdims=True)
-                raised = jnp.exp(scores - top)
-                weight = jnp.sum(raised, axis=1, keepdims=True)
-                mixed = dot(raised.astype(BF16), values[...]) / weight
-                result = jnp.where(own, mixed, result)
-            out[begin + low:begin + low + step, :] = result.astype(BF16)
-
-
-def attend(sample_col, sample_row, parts_a, parts_b):
-    first, width = parts_a[0].shape
+    lanes = iota((count, width), 1)
+    result = jnp.zeros((count, width), F32)
+    for head in range(width // HD):
+        own = (lanes >= head * HD) & (lanes < (head + 1) * HD)
+        masked = jnp.where(own, query[...], jnp.zeros_like(query))
+        scores = dot_nt(masked, keys[...]) + bias[...]
+        top = jnp.max(scores, axis=1, keepdims=True)
+        raised = jnp.exp(scores - top)
+        weight = jnp.sum(raised, axis=1, keepdims=True)
+        mixed = dot(raised.astype(BF16), values[...]) / weight
+        result = jnp.where(own, mixed, result)
+    out[...] = result.astype(BF16)
+
+
+def attend(sample_col, sample_row, query, parts_a, parts_b):
+    count, width = query.shape
+    first = parts_a[0].shape[0]
     second = parts_b[0].shape[0]
     rows = first + second
-    step = 2 * HD
+    step = 256 if width % 256 == 0 else 128
     spec_a = pl.BlockSpec((first, step), lambda i: (0, i))
     spec_b = pl.BlockSpec((second, step), lambda i: (0, i))
     return pl.pallas_call(
@@ -253,29 +249,30 @@
         in_specs=[
             pl.BlockSpec(sample_col.shape, lambda i: (0, 0)),
             pl.BlockSpec(sample_row.shape, lambda i: (0, 0)),
-        ] + [spec_a] * 3 + [spec_b] * 3,
-        out_specs=pl.BlockSpec((rows, step), lambda i: (0, i)),
-        out_shape=jax.ShapeDtypeStruct((rows, width), BF16),
+            pl.BlockSpec((count, step), lambda i: (0, i)),
+        ] + [spec_a] * 2 + [spec_b] * 2,
+        out_specs=pl.BlockSpec((count, step), lambda i: (0, i)),
+        out_shape=jax.ShapeDtypeStruct((count, width), BF16),
         scratch_shapes=[
-            pltpu.VMEM((rows, rows), F32),
+            pltpu.VMEM((count, rows), F32),
             pltpu.VMEM((rows, step), BF16),
             pltpu.VMEM((rows, step), BF16),
         ],
         compiler_params=params(),
         cost_estimate=pl.CostEstimate(
-            flops=4 * rows * rows * width, bytes_accessed=8 * rows * width, transcendentals=rows * rows * width // HD
+            flops=4 * count * rows * width * 2, bytes_accessed=8 * rows * width, transcendentals=count * rows * width // HD
         ),
         name="attend",
-    )(sample_col, sample_row, *parts_a, *parts_b)
-
-
-def line_sum(partial, width):
+    )(sample_col, sample_row, query, *parts_a, *parts_b)
+
+
+def line_sum(partial):
     members = lax.axis_size("bag")
     mine = lax.axis_index("bag")
 
     def piece(index):
         index = jnp.clip(index, 0, members - 1)
-        return lax.dynamic_slice_in_dim(partial, index * width, width, 1).astype(F32)
+        return lax.dynamic_index_in_dim(partial, index, 0, keepdims=False).astype(F32)
 
     up = down = None
     for step in range(1, members):
@@ -284,9 +281,34 @@
         if step > 1:
             to_up = to_up + up.astype(F32)
             to_down = to_down + down.astype(F32)
-        up = lax.ppermute(to_up.astype(BF16), "bag", [(i, i + 1) for i in range(step)])
-        down = lax.ppermute(to_down.astype(BF16), "bag", [(i, i - 1) for i in range(members - step, members)])
+        to_up, to_down = lax.optimization_barrier((to_up.astype(BF16), to_down.astype(BF16)))
+        up = lax.ppermute(to_up, "bag", [(i, i + 1) for i in range(step)])
+        down = lax.ppermute(to_down, "bag", [(i, i - 1) for i in range(members - step, members)])
+        up, down = lax.optimization_barrier((up, down))
     return (piece(mine) + up.astype(F32) + down.astype(F32)).astype(BF16)
+
+
+def own_columns(weight):
+    bags = lax.axis_size("dp")
+    members = lax.axis_size("bag")
+    me = lax.axis_index("dp")
+    depth = weight.shape[0]
+    width = weight.shape[1] // members
+    share = depth // bags
+    part = lax.dynamic_slice_in_dim(weight, me * share, share, 0)
+    part = part.reshape(share, members, width).transpose(1, 0, 2)
+    part = lax.all_to_all(part, "bag", split_axis=0, concat_axis=0, tiled=True)
+    shape = (members,)
+    bit = bags // 2
+    while bit:
+        other = lax.ppermute(part, "dp", [(i, i ^ bit) for i in range(bags)])
+        high = (me & bit) != 0
+        low_part = jnp.where(high, other, part)
+        high_part = jnp.where(high, part, other)
+        part = jnp.stack([low_part, high_part], axis=len(shape))
+        shape = shape + (2,)
+        bit //= 2
+    return part.reshape(members * depth, width)
 
 
 def body(
@@ -329,25 +351,28 @@
         compiler_params=params(),
         name="order",
     )(plan_col, plan_row, home_tokens)
+    early_weight, even = lax.optimization_barrier((output_weight, even))
     full_even = lax.all_gather(even, "bag", axis=1, tiled=True)
+    columns = own_columns(early_weight)
     full_odd = lax.all_gather(odd, "bag", axis=1, tiled=True)
 
-    send_even, send_odd, kind_even, kind_odd, final = pl.pallas_call(
+    send_even, send_odd, kind_even, kind_odd, final_even, final_odd = pl.pallas_call(
         functools.partial(send_kernel, bags, pack, half),
         in_specs=[smem, smem] + [vmem] * 5,
-        out_specs=[vmem] * 5,
+        out_specs=[vmem] * 6,
         out_shape=[jax.ShapeDtypeStruct((slots, size), BF16) for size in home_rows]
         + [jax.ShapeDtypeStruct((size, 128), F32) for size in home_rows]
-        + [jax.ShapeDtypeStruct((count, 2 * slots), BF16)],
+        + [jax.ShapeDtypeStruct((count, slots), BF16)] * 2,
         compiler_params=params(),
         name="send_plan",
     )(ends, modality, plan_row, where_row, where_col, order_even, order_odd)
-    pack_even, pack_odd, back, samples = pl.pallas_call(
+    pack_even, pack_odd, back_even, back_odd, samples = pl.pallas_call(
         functools.partial(bag_kernel, pack, half),
         in_specs=[smem, smem, vmem],
-        out_specs=[vmem] * 4,
+        out_specs=[vmem] * 5,
         out_shape=[jax.ShapeDtypeStruct((size, slots), BF16) for size in bag_rows]
-        + [jax.ShapeDtypeStruct((2 * slots, rows), BF16), jax.ShapeDtypeStruct((rows, 128), F32)],
+        + [jax.ShapeDtypeStruct((slots, size), BF16) for size in bag_rows]
+        + [jax.ShapeDtypeStruct((rows, 128), F32)],
         scratch_shapes=[pltpu.VMEM((slots, 128), BF16)],
         compiler_params=params(),
         name="bag_plan",
@@ -364,12 +389,25 @@
     bag_odd = to_bag(full_odd, kind_odd, send_odd, pack_odd)
     parts_even = make_qkv(bag_even, qkv_weight, norm_gain)
     parts_odd = make_qkv(bag_odd, qkv_weight, norm_gain)
-    attended = attend(samples, sample_row, parts_even, parts_odd)
-    partial = dot(attended, output_weight).astype(BF16)
-    summed = line_sum(partial, width)
-    outgoing = dot(back, summed).astype(BF16).reshape(bags, capacity, width)
-    returned = lax.all_to_all(outgoing, "dp", split_axis=0, concat_axis=0, tiled=True)
-    return dot(final, returned.reshape(bags * capacity, width)).astype(BF16)
+    first, second = bag_rows
+    attended_even = attend(samples[:first], sample_row, parts_even[0], parts_even[1:], parts_odd[1:])
+    gathered = lax.all_gather(attended_even, "bag", axis=1, tiled=True)
+    attended_odd = attend(samples[first:], sample_row, parts_odd[0], parts_even[1:], parts_odd[1:])
+    members = lax.axis_size("bag")
+    partial = jnp.stack(
+        [dot(attended_odd, output_weight[:, i * width:(i + 1) * width]).astype(BF16) for i in range(members)]
+    )
+    summed_odd = line_sum(partial)
+    summed_even = dot(gathered, columns).astype(BF16)
+
+    def to_home(summed, back):
+        outgoing = dot(back, summed).astype(BF16).reshape(bags, half, width)
+        returned = lax.all_to_all(outgoing, "dp", split_axis=0, concat_axis=0, tiled=True)
+        return returned.reshape(slots, width)
+
+    home_odd = to_home(summed_odd, back_odd)
+    home_even = to_home(summed_even, back_even)
+    return (dot(final_even, home_even) + dot(final_odd, home_odd)).astype(BF16)
 
 
 def solution(mesh):

time: 368 us -> 323 us (0.88)
  blocking collectives: 40.8 us -> 0 us
  waiting for transfers between devices: 186 us -> 162 us
  starting transfers between devices: 19.7 us -> 38.7 us
  Pallas kernels: 78.9 us -> 62 us
  matrix products: 14.6 us -> 23.4 us
  other arithmetic: 8.15 us -> 12.7 us
  local copies, waits for them, and re-layouts: 5.68 us -> 9.58 us
    all_to_all x2 -> x0, blocking collectives: 40.8 us -> none  [the longest x1 24.5 us: body(): lax.all_to_all(outgoing, 'dp', split_axis=0, concat_axis=0, tiled=True)]
    all_gather x2, waiting for transfers between devices: 49.1 us -> 10.1 us  [to_bag(): return lax.all_gather(packed, 'bag', axis=1, tiled=True)]
    all_to_all x0 -> x3, waiting for transfers between devices: none -> 18.3 us  [the longest x2 18.3 us: to_home(): lax.all_to_all(outgoing, 'dp', split_axis=0, concat_axis=0, tiled=True)]
    ppermute x6 -> x9, waiting for transfers between devices: 80.2 us -> 66 us  [the longest x3 35.1 us: own_columns(): other = lax.ppermute(part, 'dp', [(i, i ^ bit) for i in range(bags)])]
    all_to_all x1 -> x2, waiting for transfers between devices: 8.2 us -> 19.5 us  [to_bag(): lax.all_to_all(outgoing, 'dp', split_axis=0, concat_axis=0, tiled=True)]
    all_to_all x0 -> x3, starting transfers between devices: none -> 10.7 us  [the longest x2 7.2 us: to_home(): lax.all_to_all(outgoing, 'dp', split_axis=0, concat_axis=0, tiled=True)]
    another operation x0 -> x7, other arithmetic: none -> 9.33 us  [the longest x6 9.08 us: own_columns(): part = jnp.stack([low_part, high_part], axis=len(shape))]
    dot_general x5 -> x10, matrix products: 14.6 us -> 23.4 us  [dot(): return jnp.dot(left, right, preferred_element_type=F32)]
  transfers between devices with their start and end apart: 11 -> 19, of which waited for: 9 -> 12; matrix products, arithmetic and copies ran while one was open for 3% -> 13% of each run, Pallas kernels for 10% -> 18%
where the time goes in v2:
time: 323 us; the launch traced here: 322 us
  waiting for transfers between devices  162 us (50%)
  Pallas kernels  62 us (19%)
  starting transfers between devices  38.7 us (12%)
  matrix products  23.4 us (7%)
  between operations  13.4 us (4%)
  other arithmetic  12.7 us (4%)
  local copies, waits for them, and re-layouts  9.58 us (3%)
    ppermute x3, waiting for transfers between devices, own_columns(): other = lax.ppermute(part, 'dp', [(i, i ^ bit) for i in range(bags)])  35.1 us
    all_gather x1, waiting for transfers between devices, body(): full_odd = lax.all_gather(odd, 'bag', axis=1, tiled=True)  34.7 us
    ppermute x3, waiting for transfers between devices, line_sum(): up = lax.ppermute(to_up, 'bag', [(i, i + 1) for i in range(step)])  28.6 us
    dot_general x10, matrix products, dot(): return jnp.dot(left, right, preferred_element_type=F32)  23.4 us
    pallas_call x2, Pallas kernels, make_qkv(): pl.pallas_call(qkv_kernel, grid=(width // step,), in_specs=[pl.BlockSpec(...  21.3 us
    all_to_all x2, waiting for transfers between devices, to_bag(): lax.all_to_all(outgoing, 'dp', split_axis=0, concat_axis=0, tiled=True)  19.5 us
    all_to_all x2, waiting for transfers between devices, to_home(): lax.all_to_all(outgoing, 'dp', split_axis=0, concat_axis=0, tiled=True)  18.3 us
    pallas_call x2, Pallas kernels, attend(): pl.pallas_call(attend_kernel, grid=(width // step,), in_specs=[pl.BlockSp...  15.7 us
  transfers between devices with their start and end apart: 19, of which 12 were waited for; matrix products, arithmetic and copies ran while one was open for 13% of the time, Pallas kernels for 18%

profile of v2, /device:TPU:0, one launch (start us, length us, event | category | flops | bytes accessed | tf_op | source)
XLA Modules:
  0.0 321.7 jit_solution(6712973147421614993)
XLA Ops:
  6.5 0.8 dynamic_slice.28
  7.3 0.9 copy.22.plan_col
  8.2 3.3 %order.1 = (bf16[272,768]{1,0:T(8,128)(2,1)}, bf16[256,768]{1,0:T(8,128)(2,1)}, bf16[272,512]{1,0:T(8,128)(2,1)}, bf16[256,512]{1,0:T(8,128)(2,1)}, s32[1,512]{1,0:T(1,128)}, /*index=5*/s32[512,1]{1,0:T(8,128)}) custom-call(s32[512,1]{1,0:T(8,128)} %copy.22.plan_col, s32[1,512]{1,0:T(1,128)} %bitcast.91, bf16[512,768]{1,0:T(8,128)(2,1)} %tokens.1), custom_call_target="tpu_custom_call" | custom-call | tf_op jit(solution)/shard_map/order/pallas_call | solution.py:343
  11.5 0.7 all-gather.6.cloned.1.call-update
  12.3 0.7 reduce_window_sum.11.ends
  13.1 0.7 copy.23.modality
  13.8 3.0 send_plan.1
  16.8 34.7 %all-gather.10.cloned.1.call-done.rows_in = bf16[256,3072]{1,0:T(8,128)(2,1)} async-done(((bf16[256,768]{1,0:T(8,128)(2,1)}), bf16[256,3072]{1,0:T(8,128)(2,1)}) %all-gather.10.cloned.1.call-update) | async-done | bytes 1572880 | tf_op jit(solution)/shard_map/all_gather | solution.py:357
  51.4 7.7 %project.3 = bf16[512,768]{1,0:T(8,128)(2,1)} custom-call(bf16[256,3072]{1,0:T(8,128)(2,1)} %all-gather.10.cloned.1.call-done.rows_in, f32[256,128]{1,0:T(8,128)} %get-tuple-element.59.kinds, bf16[2,3072,768]{2,1,0:T(8,128)(2,1)} %weight.6, bf16[512,256]{1,0:T(8,128)(2,1)} %get-tuple-element.60.send), custom_call_target="tpu_custom_call" | custom-call | flops 2415919104 | bytes 9437184 | tf_op jit(solution)/shard_map/project/pallas_call | solution.py:149
  59.2 3.7 %all-to-all-start.1 = ((bf16[8,64,768]{2,1,0:T(8,128)(2,1)}), bf16[8,64,768]{2,1,0:T(8,128)(2,1)S(1)}, u32[]{:S(2)}, u32[]{:S(2)}) async-start(bf16[8,64,768]{2,1,0:T(8,128)(2,1)} %bitcast.81), calls=%async_computation.1 | async-start | bytes 1572864 | tf_op jit(solution)/shard_map/all_to_all | solution.py:384
  62.9 0.6 reshape.59.plan
  63.5 3.1 bag_plan.1
  66.6 8.8 %all-to-all-done.1 = bf16[8,64,768]{2,1,0:T(8,128)(2,1)S(1)} async-done(((bf16[8,64,768]{2,1,0:T(8,128)(2,1)}), bf16[8,64,768]{2,1,0:T(8,128)(2,1)S(1)}, u32[]{:S(2)}, u32[]{:S(2)}) %all-to-all-start.1) | async-done | bytes 786464 | tf_op jit(solution)/shard_map/all_to_all | solution.py:384
  75.4 2.2 convolution_convert_fusion.4
  77.7 1.1 constant_dynamic-slice_fusion
  79.2 0.9 copy.24
  80.1 3.5 %all-to-all-start.2 = ((bf16[4,96,768]{2,1,0:T(8,128)(2,1)}), bf16[4,96,768]{2,1,0:T(8,128)(2,1)S(1)}, u32[]{:S(2)}, u32[]{:S(2)}) async-start(bf16[4,96,768]{2,1,0:T(8,128)(2,1)} %copy.24), calls=%async_computation.2 | async-start | bytes 1179648 | tf_op jit(solution)/shard_map/all_to_all | solution.py:300
  83.6 12.8 %all-gather.6.cloned.1.call-done.rows_in = bf16[272,3072]{1,0:T(8,128)(2,1)} async-done(((bf16[272,768]{1,0:T(8,128)(2,1)}), bf16[272,3072]{1,0:T(8,128)(2,1)}) %all-gather.6.cloned.1.call-update) | async-done | bytes 1671184 | tf_op jit(solution)/shard_map/all_gather | solution.py:355
  96.3 7.8 %project.2 = bf16[512,768]{1,0:T(8,128)(2,1)} custom-call(bf16[272,3072]{1,0:T(8,128)(2,1)} %all-gather.6.cloned.1.call-done.rows_in, f32[272,128]{1,0:T(8,128)} %get-tuple-element.52.kinds, bf16[2,3072,768]{2,1,0:T(8,128)(2,1)} %weight.6, bf16[512,272]{1,0:T(8,128)(2,1)} %get-tuple-element.53.send), custom_call_target="tpu_custom_call" | custom-call | flops 2566914048 | bytes 9437184 | tf_op jit(solution)/shard_map/project/pallas_call | solution.py:149
  104.2 3.6 %all-to-all-start = ((bf16[8,64,768]{2,1,0:T(8,128)(2,1)}), bf16[8,64,768]{2,1,0:T(8,128)(2,1)S(1)}, u32[]{:S(2)}, u32[]{:S(2)}) async-start(bf16[8,64,768]{2,1,0:T(8,128)(2,1)} %bitcast.87), calls=%async_computation | async-start | bytes 1572864 | tf_op jit(solution)/shard_map/all_to_all | solution.py:384
  107.8 2.0 collective-permute-start
  109.8 10.7 %all-to-all-done = bf16[8,64,768]{2,1,0:T(8,128)(2,1)S(1)} async-done(((bf16[8,64,768]{2,1,0:T(8,128)(2,1)}), bf16[8,64,768]{2,1,0:T(8,128)(2,1)S(1)}, u32[]{:S(2)}, u32[]{:S(2)}) %all-to-all-start) | async-done | bytes 786464 | tf_op jit(solution)/shard_map/all_to_all | solution.py:384
  120.4 1.2 convolution_convert_fusion.2
  121.9 10.2 %collective-permute-done = bf16[4,96,768]{2,1,0:T(8,128)(2,1)} collective-permute-done((bf16[4,96,768]{2,1,0:T(8,128)(2,1)S(1)}, bf16[4,96,768]{2,1,0:T(8,128)(2,1)}, u32[]{:S(2)}, u32[]{:S(2)}) %collective-permute-start) | collective-permute-done | bytes 589856 | tf_op jit(solution)/shard_map/ppermute | solution.py:304
  132.1 1.1 select_bitcast_fusion.5
  133.4 1.5 collective-permute-start.1
  134.9 0.7 slice.21.sample_col
  135.8 0.6 reshape_squeeze.3.sample_row
  136.4 24.9 %collective-permute-done.1 = bf16[4,2,96,768]{3,2,1,0:T(8,128)(2,1)} collective-permute-done((bf16[4,2,96,768]{3,2,1,0:T(8,128)(2,1)S(1)}, bf16[4,2,96,768]{3,2,1,0:T(8,128)(2,1)}, u32[]{:S(2)}, u32[]{:S(2)}) %collective-permute-start.1) | collective-permute-done | bytes 1179680 | tf_op jit(solution)/shard_map/ppermute | solution.py:304
  161.2 1.4 select_bitcast_fusion.3
  162.7 1.8 pad_maximum_fusion.1
  164.5 10.6 %qkv.3 = (bf16[320,768]{1,0:T(8,128)(2,1)}, bf16[320,768]{1,0:T(8,128)(2,1)}, bf16[320,768]{1,0:T(8,128)(2,1)}) custom-call(bf16[320,3072]{1,0:T(8,128)(2,1)} %all-gather.12.cloned.1.call-done.rows_in, bf16[3,3072,768]{2,1,0:T(8,128)(2,1)} %weight.7, f32[3,2,256]{2,1,0:T(2,128)} %bitcast.93), custom_call_target="tpu_custom_call" | custom-call | flops 4529848320 | bytes 14155776 | tf_op jit(solution)/shard_map/qkv/pallas_call | solution.py:194
  175.1 10.1 %all-gather.8.cloned.1.call-done.rows_in = bf16[336,3072]{1,0:T(8,128)(2,1)} async-done(((bf16[336,768]{1,0:T(8,128)(2,1)}), bf16[336,3072]{1,0:T(8,128)(2,1)}) %all-gather.8.cloned.1.call-update) | async-done | bytes 2064400 | tf_op jit(solution)/shard_map/all_gather | solution.py:386
  185.1 10.7 %qkv.2 = (bf16[336,768]{1,0:T(8,128)(2,1)}, bf16[336,768]{1,0:T(8,128)(2,1)}, bf16[336,768]{1,0:T(8,128)(2,1)}) custom-call(bf16[336,3072]{1,0:T(8,128)(2,1)} %all-gather.8.cloned.1.call-done.rows_in, bf16[3,3072,768]{2,1,0:T(8,128)(2,1)} %weight.7, f32[3,2,256]{2,1,0:T(2,128)} %bitcast.94), custom_call_target="tpu_custom_call" | custom-call | flops 4756340736 | bytes 14155776 | tf_op jit(solution)/shard_map/qkv/pallas_call | solution.py:194
  195.9 8.0 %attend.2 = bf16[336,768]{1,0:T(8,128)(2,1)} custom-call(f32[336,128]{1,0:T(8,128)} %slice.21.sample_col, f32[1,656]{1,0:T(1,128)} %reshape_squeeze.3.sample_row, bf16[336,768]{1,0:T(8,128)(2,1)} %get-tuple-element.54.query, bf16[336,768]{1,0:T(8,128)(2,1)} %get-tuple-element.55.ka, bf16[336,768]{1,0:T(8,128)(2,1)} %get-tuple-element.56.va, ...), custom_call_target="tpu_custom_call" | custom-call | flops 1354235904 | bytes 4030464 | tf_op jit(solution)/shard_map/attend/pallas_call | solution.py:246
  203.9 0.7 slice.23.sample_col
  204.6 7.7 %attend.3 = bf16[320,768]{1,0:T(8,128)(2,1)} custom-call(f32[320,128]{1,0:T(8,128)} %slice.23.sample_col, f32[1,656]{1,0:T(1,128)} %reshape_squeeze.3.sample_row, bf16[320,768]{1,0:T(8,128)(2,1)} %get-tuple-element.66.query, bf16[336,768]{1,0:T(8,128)(2,1)} %get-tuple-element.55.ka, bf16[336,768]{1,0:T(8,128)(2,1)} %get-tuple-element.56.va, ...), custom_call_target="tpu_custom_call" | custom-call | flops 1289748480 | bytes 4030464 | tf_op jit(solution)/shard_map/attend/pallas_call | solution.py:246
  212.3 2.0 fusion.3
  214.3 1.8 fusion.2
  216.2 1.8 fusion.1
  218.0 1.8 fusion
  220.1 1.1 dynamic-slice_bitcast_fusion
  221.2 2.8 collective-permute-start.3
  224.0 1.5 collective-permute-start.4
  225.4 19.7 %collective-permute-done.3 = bf16[320,768]{1,0:T(8,128)(2,1)} collective-permute-done((bf16[320,768]{1,0:T(8,128)(2,1)}, bf16[320,768]{1,0:T(8,128)(2,1)}, u32[]{:S(2)}, u32[]{:S(2)}) %collective-permute-start.3) | collective-permute-done | bytes 491552 | tf_op jit(solution)/shard_map/ppermute | solution.py:285
  245.1 1.4 fusion.9
  246.5 4.4 %collective-permute-start.5 = (bf16[320,768]{1,0:T(8,128)(2,1)S(1)}, bf16[320,768]{1,0:T(8,128)(2,1)S(1)}, u32[]{:S(2)}, u32[]{:S(2)}) collective-permute-start(bf16[320,768]{1,0:T(8,128)(2,1)S(1)} %get-tuple-element.71), channel_id=1, source_target_pairs={{0,1},{1,2},{4,5},{5,6},{8,9},{9,10},{12,13},{13,14},{16,17},{17,1... | collective-permute-start | bytes 1474568 | tf_op jit(solution)/shard_map/ppermute | solution.py:285
  250.9 0.9 collective-permute-start.6
  251.9 2.0 select_bitcast_fusion.1
  253.9 2.6 pad_maximum_fusion
  256.5 8.9 %collective-permute-done.5 = bf16[320,768]{1,0:T(8,128)(2,1)S(1)} collective-permute-done((bf16[320,768]{1,0:T(8,128)(2,1)S(1)}, bf16[320,768]{1,0:T(8,128)(2,1)S(1)}, u32[]{:S(2)}, u32[]{:S(2)}) %collective-permute-start.5) | collective-permute-done | bytes 491552 | tf_op jit(solution)/shard_map/ppermute | solution.py:285
  265.4 1.2 fusion.8
  266.6 6.1 %collective-permute-start.7 = (bf16[320,768]{1,0:T(8,128)(2,1)}, bf16[320,768]{1,0:T(8,128)(2,1)}, u32[]{:S(2)}, u32[]{:S(2)}) collective-permute-start(bf16[320,768]{1,0:T(8,128)(2,1)} %get-tuple-element.75), channel_id=1, source_target_pairs={{0,1},{1,2},{2,3},{4,5},{5,6},{6,7},{8,9},{9,10},{10,11},{12,13},{... | collective-permute-start | bytes 1474568 | tf_op jit(solution)/shard_map/ppermute | solution.py:285
  272.8 1.3 collective-permute-start.8
  274.1 6.4 %convolution_convert_fusion.1 = bf16[512,768]{1,0:T(8,128)(2,1)} fusion(bf16[512,336]{1,0:T(8,128)(2,1)S(1)} %copy-done.11, bf16[336,3072]{1,0:T(8,128)(2,1)} %all-gather.14.cloned.1.call-done, bf16[3072,768]{1,0:T(8,128)(2,1)} %bitcast.80), kind=kOutput, calls=%fused_computation.7 | convolution fusion | flops 1850339328 | bytes 7913472 | tf_op jit(solution)/shard_map/dot_general | solution.py:30
  280.5 3.7 %all-to-all-start.3 = ((bf16[8,64,768]{2,1,0:T(8,128)(2,1)}), bf16[8,64,768]{2,1,0:T(8,128)(2,1)S(1)}, u32[]{:S(2)}, u32[]{:S(2)}) async-start(bf16[8,64,768]{2,1,0:T(8,128)(2,1)} %bitcast.89), calls=%async_computation.3 | async-start | bytes 1572864 | tf_op jit(solution)/shard_map/all_to_all | solution.py:405
  284.2 2.3 collective-permute-done.8
  286.5 2.7 convolution_convert_fusion
  289.1 7.6 %all-to-all-done.3 = bf16[8,64,768]{2,1,0:T(8,128)(2,1)S(1)} async-done(((bf16[8,64,768]{2,1,0:T(8,128)(2,1)}), bf16[8,64,768]{2,1,0:T(8,128)(2,1)S(1)}, u32[]{:S(2)}, u32[]{:S(2)}) %all-to-all-start.3) | async-done | bytes 786464 | tf_op jit(solution)/shard_map/all_to_all | solution.py:405
  296.8 0.9 copy-done.2
  297.7 3.5 %all-to-all-start.4 = ((bf16[8,64,768]{2,1,0:T(8,128)(2,1)}), bf16[8,64,768]{2,1,0:T(8,128)(2,1)S(1)}, u32[]{:S(2)}, u32[]{:S(2)}) async-start(bf16[8,64,768]{2,1,0:T(8,128)(2,1)} %bitcast.86), calls=%async_computation.4 | async-start | bytes 1572864 | tf_op jit(solution)/shard_map/all_to_all | solution.py:405
  301.2 1.9 fusion.18
  303.1 10.7 %all-to-all-done.4 = bf16[8,64,768]{2,1,0:T(8,128)(2,1)S(1)} async-done(((bf16[8,64,768]{2,1,0:T(8,128)(2,1)}), bf16[8,64,768]{2,1,0:T(8,128)(2,1)S(1)}, u32[]{:S(2)}, u32[]{:S(2)}) %all-to-all-start.4) | async-done | bytes 786464 | tf_op jit(solution)/shard_map/all_to_all | solution.py:405
  313.7 1.5 add_convert_fusion
  (47 shorter events, 1.5 us)
Async XLA Ops:
  6.5 5.7 %copy-start.9 = (s32[8,4]{0,1:T(4,128)S(1)}, s32[8,4]{0,1:T(4,128)}, u32[]{:S(2)}) copy-start(s32[8,4]{0,1:T(4,128)} %param.14) | copy-start | bytes 388
  6.5 6.5 %copy-start.10 = (s32[8,4]{0,1:T(4,128)S(1)}, s32[8,4]{0,1:T(4,128)}, u32[]{:S(2)}) copy-start(s32[8,4]{0,1:T(4,128)} %param.15) | copy-start | bytes 388
  6.5 44.9 %all-gather.10.cloned.1.call-start = ((), (), s32[]{:S(2)}) async-start(), calls=%async_computation.7 | async-start | bytes 1966080 | tf_op jit(solution)/shard_map/all_gather | solution.py:357
  7.3 0.9 copy-start.7
  11.5 84.9 %all-gather.6.cloned.1.call-start = ((), (), s32[]{:S(2)}) async-start(), calls=%async_computation.5 | async-start | bytes 2088960 | tf_op jit(solution)/shard_map/all_gather | solution.py:355
  51.4 11.4 %copy-start.8 = (s32[4096]{0:T(1024)S(1)}, s32[4096]{0:T(1024)}, u32[]{:S(2)}) copy-start(s32[4096]{0:T(1024)} %param.13) | copy-start | bytes 49156
  59.2 16.3 %all-to-all-start.1 = ((bf16[8,64,768]{2,1,0:T(8,128)(2,1)}), bf16[8,64,768]{2,1,0:T(8,128)(2,1)S(1)}, u32[]{:S(2)}, u32[]{:S(2)}) async-start(bf16[8,64,768]{2,1,0:T(8,128)(2,1)} %bitcast.81), calls=%async_computation.1 | async-start | bytes 1572864 | tf_op jit(solution)/shard_map/all_to_all | solution.py:384
  62.8 101.7 %all-gather.12.cloned.1.call-start = ((), (), s32[]{:S(2)}) async-start(), calls=%async_computation.8 | async-start | bytes 2457600 | tf_op jit(solution)/shard_map/all_gather | solution.py:386
  80.1 24.1 %all-to-all-start.2 = ((bf16[4,96,768]{2,1,0:T(8,128)(2,1)}), bf16[4,96,768]{2,1,0:T(8,128)(2,1)S(1)}, u32[]{:S(2)}, u32[]{:S(2)}) async-start(bf16[4,96,768]{2,1,0:T(8,128)(2,1)} %copy.24), calls=%async_computation.2 | async-start | bytes 1179648 | tf_op jit(solution)/shard_map/all_to_all | solution.py:300
  96.3 24.1 %copy-start.6 = (bf16[336,512]{1,0:T(8,128)(2,1)S(1)}, bf16[336,512]{1,0:T(8,128)(2,1)}, u32[]{:S(2)}) copy-start(bf16[336,512]{1,0:T(8,128)(2,1)} %get-tuple-element.49) | copy-start | bytes 1032196
  104.2 16.3 %all-to-all-start = ((bf16[8,64,768]{2,1,0:T(8,128)(2,1)}), bf16[8,64,768]{2,1,0:T(8,128)(2,1)S(1)}, u32[]{:S(2)}, u32[]{:S(2)}) async-start(bf16[8,64,768]{2,1,0:T(8,128)(2,1)} %bitcast.87), calls=%async_computation | async-start | bytes 1572864 | tf_op jit(solution)/shard_map/all_to_all | solution.py:384
  107.7 77.4 %all-gather.8.cloned.1.call-start = ((), (), s32[]{:S(2)}) async-start(), calls=%async_computation.6 | async-start | bytes 2580480 | tf_op jit(solution)/shard_map/all_gather | solution.py:386
  107.8 24.3 %collective-permute-start = (bf16[4,96,768]{2,1,0:T(8,128)(2,1)S(1)}, bf16[4,96,768]{2,1,0:T(8,128)(2,1)}, u32[]{:S(2)}, u32[]{:S(2)}) collective-permute-start(bf16[4,96,768]{2,1,0:T(8,128)(2,1)S(1)} %all-to-all-done.2), channel_id=1, source_target_pairs={{0,16},{4,20},{8,24},{12,28},{16,0},{20,4},{24,8},{28,12},{1,17},{... | collective-permute-start | bytes 1769480 | tf_op jit(solution)/shard_map/ppermute | solution.py:304
  121.7 152.4 %all-gather.14.cloned.1.call-start = ((), (), s32[]{:S(2)}) async-start(), calls=%async_computation.9 | async-start | bytes 2580480 | tf_op jit(solution)/shard_map/all_gather | solution.py:394
  121.9 13.0 %copy-start.3 = (f32[656,128]{1,0:T(8,128)S(1)}, f32[656,128]{1,0:T(8,128)}, u32[]{:S(2)}) copy-start(f32[656,128]{1,0:T(8,128)} %get-tuple-element.48) | copy-start | bytes 1007620
  133.4 27.8 %collective-permute-start.1 = (bf16[4,2,96,768]{3,2,1,0:T(8,128)(2,1)S(1)}, bf16[4,2,96,768]{3,2,1,0:T(8,128)(2,1)}, u32[]{:S(2)}, u32[]{:S(2)}) collective-permute-start(bf16[4,2,96,768]{3,2,1,0:T(8,128)(2,1)S(1)} %pad_maximum_fusion.3), channel_id=1, source_target_pairs={{0,8},{4,12},{8,0},{12,4},{16,24},{20,28},{24,16},{28,20},{1,9},{5... | collective-permute-start | bytes 3538952 | tf_op jit(solution)/shard_map/ppermute | solution.py:304
  162.7 1.8 copy-start
  164.5 87.4 %collective-permute-start.2 = (bf16[4,2,2,96,768]{4,3,2,1,0:T(8,128)(2,1)}, bf16[4,2,2,96,768]{4,3,2,1,0:T(8,128)(2,1)}, u32[]{:S(2)}, u32[]{:S(2)}) collective-permute-start(bf16[4,2,2,96,768]{4,3,2,1,0:T(8,128)(2,1)} %pad_maximum_fusion.1), channel_id=1, source_target_pairs={{0,4},{4,0},{8,12},{12,8},{16,20},{20,16},{24,28},{28,24},{1,5},{5... | collective-permute-start | bytes 7077896 | tf_op jit(solution)/shard_map/ppermute | solution.py:304
  212.3 2.0 copy-start.12
  221.2 23.9 %collective-permute-start.3 = (bf16[320,768]{1,0:T(8,128)(2,1)}, bf16[320,768]{1,0:T(8,128)(2,1)}, u32[]{:S(2)}, u32[]{:S(2)}) collective-permute-start(bf16[320,768]{1,0:T(8,128)(2,1)} %get-tuple-element.67), channel_id=1, source_target_pairs={{0,1},{4,5},{8,9},{12,13},{16,17},{20,21},{24,25},{28,29}} | collective-permute-start | bytes 1474568 | tf_op jit(solution)/shard_map/ppermute | solution.py:285
  224.0 21.1 %collective-permute-start.4 = (bf16[320,768]{1,0:T(8,128)(2,1)}, bf16[320,768]{1,0:T(8,128)(2,1)}, u32[]{:S(2)}, u32[]{:S(2)}) collective-permute-start(bf16[320,768]{1,0:T(8,128)(2,1)} %get-tuple-element.68), channel_id=1, source_target_pairs={{3,2},{7,6},{11,10},{15,14},{19,18},{23,22},{27,26},{31,30}} | collective-permute-start | bytes 1474568 | tf_op jit(solution)/shard_map/ppermute | solution.py:286
  225.4 26.5 %copy-start.1 = (bf16[4,2,1,96,768]{4,3,2,1,0:T(8,128)(2,1)S(1)}, bf16[4,2,1,96,768]{4,3,2,1,0:T(8,128)(2,1)}, u32[]{:S(2)}) copy-start(bf16[4,2,1,96,768]{4,3,2,1,0:T(8,128)(2,1)} %copy-done) | copy-start | bytes 3538948
  246.5 18.9 %collective-permute-start.5 = (bf16[320,768]{1,0:T(8,128)(2,1)S(1)}, bf16[320,768]{1,0:T(8,128)(2,1)S(1)}, u32[]{:S(2)}, u32[]{:S(2)}) collective-permute-start(bf16[320,768]{1,0:T(8,128)(2,1)S(1)} %get-tuple-element.71), channel_id=1, source_target_pairs={{0,1},{1,2},{4,5},{5,6},{8,9},{9,10},{12,13},{13,14},{16,17},{17,1... | collective-permute-start | bytes 1474568 | tf_op jit(solution)/shard_map/ppermute | solution.py:285
  250.9 14.5 %collective-permute-start.6 = (bf16[320,768]{1,0:T(8,128)(2,1)S(1)}, bf16[320,768]{1,0:T(8,128)(2,1)S(1)}, u32[]{:S(2)}, u32[]{:S(2)}) collective-permute-start(bf16[320,768]{1,0:T(8,128)(2,1)S(1)} %get-tuple-element.72), channel_id=1, source_target_pairs={{2,1},{3,2},{6,5},{7,6},{10,9},{11,10},{14,13},{15,14},{18,17},{19... | collective-permute-start | bytes 1474568 | tf_op jit(solution)/shard_map/ppermute | solution.py:286
  256.5 17.6 %copy-start.11 = (bf16[512,336]{1,0:T(8,128)(2,1)S(1)}, bf16[512,336]{1,0:T(8,128)(2,1)}, u32[]{:S(2)}) copy-start(bf16[512,336]{1,0:T(8,128)(2,1)} %get-tuple-element.47) | copy-start | bytes 1032196
  266.6 17.6 %collective-permute-start.7 = (bf16[320,768]{1,0:T(8,128)(2,1)}, bf16[320,768]{1,0:T(8,128)(2,1)}, u32[]{:S(2)}, u32[]{:S(2)}) collective-permute-start(bf16[320,768]{1,0:T(8,128)(2,1)} %get-tuple-element.75), channel_id=1, source_target_pairs={{0,1},{1,2},{2,3},{4,5},{5,6},{6,7},{8,9},{9,10},{10,11},{12,13},{... | collective-permute-start | bytes 1474568 | tf_op jit(solution)/shard_map/ppermute | solution.py:285
  272.8 13.7 %collective-permute-start.8 = (bf16[320,768]{1,0:T(8,128)(2,1)}, bf16[320,768]{1,0:T(8,128)(2,1)}, u32[]{:S(2)}, u32[]{:S(2)}) collective-permute-start(bf16[320,768]{1,0:T(8,128)(2,1)} %get-tuple-element.76), channel_id=1, source_target_pairs={{1,0},{2,1},{3,2},{5,4},{6,5},{7,6},{9,8},{10,9},{11,10},{13,12},{... | collective-permute-start | bytes 1474568 | tf_op jit(solution)/shard_map/ppermute | solution.py:286
  274.1 12.4 %copy-start.5 = (bf16[512,320]{1,0:T(8,128)(2,1)S(1)}, bf16[512,320]{1,0:T(8,128)(2,1)}, u32[]{:S(2)}) copy-start(bf16[512,320]{1,0:T(8,128)(2,1)} %get-tuple-element.65) | copy-start | bytes 983044
  280.5 16.3 %all-to-all-start.3 = ((bf16[8,64,768]{2,1,0:T(8,128)(2,1)}), bf16[8,64,768]{2,1,0:T(8,128)(2,1)S(1)}, u32[]{:S(2)}, u32[]{:S(2)}) async-start(bf16[8,64,768]{2,1,0:T(8,128)(2,1)} %bitcast.89), calls=%async_computation.3 | async-start | bytes 1572864 | tf_op jit(solution)/shard_map/all_to_all | solution.py:405
  296.8 0.9 copy-start.2
  296.8 17.0 %copy-start.4 = (bf16[512,512]{1,0:T(8,128)(2,1)S(1)}, bf16[512,512]{1,0:T(8,128)(2,1)}, u32[]{:S(2)}) copy-start(bf16[512,512]{1,0:T(8,128)(2,1)} %get-tuple-element.64) | copy-start | bytes 1572868
  297.7 16.1 %all-to-all-start.4 = ((bf16[8,64,768]{2,1,0:T(8,128)(2,1)}), bf16[8,64,768]{2,1,0:T(8,128)(2,1)S(1)}, u32[]{:S(2)}, u32[]{:S(2)}) async-start(bf16[8,64,768]{2,1,0:T(8,128)(2,1)} %bitcast.86), calls=%async_computation.4 | async-start | bytes 1572864 | tf_op jit(solution)/shard_map/all_to_all | solution.py:405
Sparse Core Ops, SparseCore 0:
  11.6 39.7 all-gather.9
  53.0 43.2 all-gather.5
  97.9 41.5 all-gather.11
  141.0 44.1 all-gather.7
  204.0 55.3 all-gather.13

commit v3 on v2

v3 whole, which is shorter than its diff:
```python
import functools

import jax
import jax.numpy as jnp
from jax import lax
from jax.experimental import pallas as pl
from jax.experimental.pallas import tpu as pltpu
from jax.sharding import PartitionSpec as P

HD = 64
EPSILON = 1e-06
PERIOD = 8
FIRST = 5
SMALL_BYTES = 240 * 1024
VMEM_LIMIT = 56 * 1024 * 1024
BF16 = jnp.bfloat16
F32 = jnp.float32


def params():
    return pltpu.CompilerParams(vmem_limit_bytes=VMEM_LIMIT)


def up16(count):
    return (count + 15) // 16 * 16


def iota(shape, dim):
    return lax.broadcasted_iota(jnp.int32, shape, dim)


def dot(left, right):
    return jnp.dot(left, right, preferred_element_type=F32)


def dot_nt(left, right):
    return lax.dot_general(left, right, (((1,), (1,)), ((), ())), preferred_element_type=F32)


def total(mask, axis):
    return jnp.sum(jnp.where(mask, 1.0, 0.0), axis=axis, keepdims=True).astype(jnp.int32)


def part_place(place, part):
    cycle, within = place // PERIOD, place % PERIOD
    if part == 0:
        return jnp.where(within < FIRST, cycle * FIRST + within, -1)
    return jnp.where(within >= FIRST, cycle * (PERIOD - FIRST) + within - FIRST, -1)


def part_sizes(rows, groups):
    spare = groups * FIRST * (PERIOD - FIRST)
    first = up16((rows * FIRST + spare + PERIOD - 1) // PERIOD)
    return first, up16((rows * (PERIOD - FIRST) + PERIOD - 1) // PERIOD)


def bag_numbers(plan, bags, pack):
    number = jnp.zeros_like(plan)
    for bag in range(1, bags):
        number += (plan >= bag * pack).astype(jnp.int32)
    return number


def order_onehot(part, place_row, place_col, rows):
    count = place_row.shape[1]
    above = iota((count, count), 0) < iota((count, count), 1)
    rank_row = total(above & (part_place(place_col, part) >= 0), 0)
    chosen = part_place(place_row, part) >= 0
    return ((iota((rows, count), 0) == rank_row) & chosen).astype(F32).astype(BF16)


def order_kernel(bags, pack, plan_row, tokens, even, odd, order_even, order_odd, where_row, where_col):
    count = plan_row.shape[1]
    diagonal = iota((count, count), 0) == iota((count, count), 1)
    plan_col = jnp.sum(jnp.where(diagonal, plan_row[...].astype(F32), 0.0), axis=1, keepdims=True).astype(jnp.int32)
    bag_col = bag_numbers(plan_col, bags, pack)
    bag_row = bag_numbers(plan_row[...], bags, pack)
    same = bag_col == bag_row
    above = iota((count, count), 0) < iota((count, count), 1)
    below = iota((count, count), 0) > iota((count, count), 1)
    place_col = total(same & below, 1)
    place_row = total(same & above, 0)
    for part, (ordered, order) in enumerate(((even, order_even), (odd, order_odd))):
        onehot = order_onehot(part, place_row, place_col, ordered.shape[0])
        order[...] = onehot
        ordered[...] = dot(onehot, tokens[...]).astype(BF16)
    where_row[...] = bag_row * 65536 + place_row
    where_col[...] = bag_col * 65536 + place_col


def move_kernel(onehot, rows, *refs):
    refs[-1][...] = dot(onehot[...], rows[...]).astype(BF16)


def move_rows(name, onehot, rows, after):
    vmem = pl.BlockSpec(memory_space=pltpu.VMEM)
    return pl.pallas_call(
        move_kernel,
        in_specs=[vmem] * 2 + [pl.BlockSpec(memory_space=pl.ANY)] * len(after),
        out_specs=vmem,
        out_shape=jax.ShapeDtypeStruct((onehot.shape[0], rows.shape[1]), BF16),
        compiler_params=params(),
        name=name,
    )(onehot, rows, *after)


def send_kernel(bags, pack, caps, ends, modality, plan_row, where_row, where_col, order_even, order_odd,
                send_even, send_odd, kind_even, kind_odd, final_even, final_odd):
    count = plan_row.shape[1]
    bag_row = where_row[...] >> 16
    place_row = where_row[...] & 65535
    bag_col = where_col[...] >> 16
    place_col = where_col[...] & 65535
    plan = plan_row[...]
    kind = jnp.zeros((1, count), F32)
    for bag in range(bags):
        begin = bag * pack
        for sample in range(ends.shape[1]):
            end = bag * pack + ends[bag, sample]
            inside = (plan >= begin) & (plan < end)
            kind = jnp.where(inside, modality[bag, sample].astype(F32), kind)
            begin = end
    for part, (order, send, kinds) in enumerate(((order_even, send_even, kind_even), (order_odd, send_odd, kind_odd))):
        own_place = part_place(place_row, part)
        target = (iota((bags * caps[part], count), 0) == bag_row * caps[part] + own_place) & (own_place >= 0)
        send[...] = dot_nt(target.astype(F32).astype(BF16), order[...]).astype(BF16)
        picked = jnp.sum(order[...].astype(F32) * kind, axis=1, keepdims=True)
        kinds[...] = jnp.broadcast_to(picked, kinds.shape)
    for part, final in enumerate((final_even, final_odd)):
        own_place = part_place(place_col, part)
        match = (iota((count, bags * caps[part]), 1) == bag_col * caps[part] + own_place) & (own_place >= 0)
        final[...] = match.astype(F32).astype(BF16)


def bag_kernel(pack, caps, me, ends, plan, pack_even, pack_odd, back_even, back_odd, samples, held):
    homes, count = plan.shape
    slot = plan[...] - me[0] * pack
    mine = (slot >= 0) & (slot < pack)
    ahead = (iota((count, count), 0) < iota((count, count), 1)).astype(F32).astype(BF16)
    place = dot(mine.astype(F32).astype(BF16), ahead).astype(jnp.int32)
    place = jnp.where(mine, place, -PERIOD)
    filled = total(mine, 1)
    first = 0
    for part, (packer, back) in enumerate(((pack_even, back_even), (pack_odd, back_odd))):
        rows, slots = packer.shape
        half = caps[part]
        own_place = part_place(place, part)
        whole = filled // PERIOD * FIRST + jnp.minimum(filled % PERIOD, FIRST)
        heres = whole if part == 0 else filled - whole
        lanes = iota((1, slots), 1)
        shift = jnp.zeros((1, slots), jnp.int32)
        limit = jnp.zeros((1, slots), jnp.int32)
        start = jnp.zeros((1, 1), jnp.int32)
        for home in range(homes):
            here = heres[home:home + 1, :]
            of_home = (lanes >= home * half) & (lanes < (home + 1) * half)
            shift = jnp.where(of_home, start - home * half, shift)
            limit = jnp.where(of_home, here + home * half, limit)
            down = iota((half, back.shape[1]), 0)
            across = iota((half, back.shape[1]), 1)
            block = ((across == down + start) & (down < here)).astype(F32).astype(BF16)
            back[home * half:(home + 1) * half, :] = block
            chosen = own_place[home:home + 1, :] == iota((half, count), 0)
            slot_here = jnp.sum(jnp.where(chosen, slot[home:home + 1, :].astype(F32), 0.0), axis=1, keepdims=True)
            slot_here = slot_here.astype(jnp.int32)
            number = jnp.ones((half, 1), jnp.int32)
            for sample in range(ends.shape[1]):
                number += (slot_here >= ends[me[0], sample]).astype(jnp.int32)
            held[home * half:(home + 1) * half, :] = jnp.broadcast_to(number.astype(F32), (half, held.shape[1])).astype(BF16)
            start = start + here
        onehot = ((iota((rows, slots), 0) == lanes + shift) & (lanes < limit)).astype(F32).astype(BF16)
        packer[...] = onehot
        samples[first:first + rows, :] = dot(onehot, held[:slots, :])
        first += rows


def project_kernel(rows_in, kinds, weight, send, *refs):
    out = refs[-1]
    rows = rows_in[...]
    product = dot(rows, weight[0])
    if weight.shape[0] == 2:
        product = jnp.where(kinds[:, :1] == 0.0, product, dot(rows, weight[1]))
    out[...] = dot(send[...], product.astype(BF16)).astype(BF16)


def project(name, rows_in, kinds, weight, send, after=()):
    rows, depth = rows_in.shape
    width = weight.shape[2]
    step = 256 if width % 256 == 0 else width
    slots = send.shape[0]
    return pl.pallas_call(
        project_kernel,
        grid=(width // step,),
        in_specs=[
            pl.BlockSpec((rows, depth), lambda i: (0, 0)),
            pl.BlockSpec(kinds.shape, lambda i: (0, 0)),
            pl.BlockSpec((weight.shape[0], depth, step), lambda i: (0, 0, i)),
            pl.BlockSpec(send.shape, lambda i: (0, 0)),
        ] + [pl.BlockSpec(memory_space=pl.ANY)] * len(after),
        out_specs=pl.BlockSpec((slots, step), lambda i: (0, i)),
        out_shape=jax.ShapeDtypeStruct((slots, width), BF16),
        compiler_params=params(),
        cost_estimate=pl.CostEstimate(
            flops=2 * rows * weight.size, bytes_accessed=weight.size * 2, transcendentals=0
        ),
        name=name,
    )(rows_in, kinds, weight, send, *after)


def split_dot(value, square):
    high = value.astype(BF16)
    low = (value - high.astype(F32)).astype(BF16)
    return dot(high, square) + dot(low, square)


def qkv_kernel(which, rows_in, gain, *refs):
    weights, outs = refs[:len(which)], refs[-len(which):]
    rows = rows_in[...]
    step = gain.shape[2]
    square = (iota((step, step), 0) // HD == iota((step, step), 1) // HD).astype(F32) * (1.0 / HD)
    square = square.astype(BF16)
    raws = [dot(rows, weight[0]) for weight in weights]
    for index, raw, out in zip(which, raws, outs):
        if index == 2:
            out[...] = raw.astype(BF16)
            continue
        shifted = raw - split_dot(raw, square)
        spread = split_dot(shifted * shifted, square)
        scale = HD ** -0.5 if index == 0 else 1.0
        out[...] = (shifted * lax.rsqrt(spread + EPSILON) * gain[0, index:index + 1, :] * scale).astype(BF16)


def make_qkv(rows_in, weight, gain, which, after=()):
    rows, depth = rows_in.shape
    width = weight.shape[2]
    step = 256 if width % 256 == 0 else 128
    part = pl.BlockSpec((rows, step), lambda i: (0, i))
    shape = jax.ShapeDtypeStruct((rows, width), BF16)
    return pl.pallas_call(
        functools.partial(qkv_kernel, which),
        grid=(width // step,),
        in_specs=[
            pl.BlockSpec((rows, depth), lambda i: (0, 0)),
            pl.BlockSpec((1, 2, step), lambda i: (i, 0, 0)),
        ] + [pl.BlockSpec((1, depth, step), lambda i, index=index: (index, 0, i)) for index in which]
        + [pl.BlockSpec(memory_space=pl.ANY)] * len(after),
        out_specs=[part] * len(which),
        out_shape=[shape] * len(which),
        compiler_params=params(),
        cost_estimate=pl.CostEstimate(
            flops=2 * len(which) * rows * depth * width,
            bytes_accessed=2 * len(which) * depth * width,
            transcendentals=0,
        ),
        name="qkv",
    )(rows_in, gain.reshape(2, width // step, step).transpose(1, 0, 2), *[weight] * len(which), *after)


def attend_kernel(counts, sample_col, sample_row, *refs):
    query_count, key_count = counts
    queries, refs = refs[:query_count], refs[query_count:]
    keys_in, refs = refs[:key_count], refs[key_count:]
    values_in, refs = refs[:key_count], refs[key_count:]
    out, bias, query, keys, values = refs[-5:]

    @pl.when(pl.program_id(0) == 0)
    def _():
        bias[...] = jnp.where(sample_col[:, :1] == sample_row[...], 0.0, -1e30)

    for parts, held in ((queries, query), (keys_in, keys), (values_in, values)):
        at = 0
        for part in parts:
            held[at:at + part.shape[0], :] = part[...]
            at += part.shape[0]
    count, width = query.shape
    lanes = iota((count, width), 1)
    result = jnp.zeros((count, width), F32)
    for head in range(width // HD):
        own = (lanes >= head * HD) & (lanes < (head + 1) * HD)
        masked = jnp.where(own, query[...], jnp.zeros_like(query))
        scores = dot_nt(masked, keys[...]) + bias[...]
        top = jnp.max(scores, axis=1, keepdims=True)
        raised = jnp.exp(scores - top)
        weight = jnp.sum(raised, axis=1, keepdims=True)
        mixed = dot(raised.astype(BF16), values[...]) / weight
        result = jnp.where(own, mixed, result)
    out[...] = result.astype(BF16)


def attend(sample_col, sample_row, queries, keys, values, after=()):
    width = queries[0].shape[1]
    count = sum(part.shape[0] for part in queries)
    rows = sum(part.shape[0] for part in keys)
    step = 256 if width % 256 == 0 else 128
    parts = [*queries, *keys, *values]
    return pl.pallas_call(
        functools.partial(attend_kernel, (len(queries), len(keys))),
        grid=(width // step,),
        in_specs=[
            pl.BlockSpec(sample_col.shape, lambda i: (0, 0)),
            pl.BlockSpec(sample_row.shape, lambda i: (0, 0)),
        ] + [pl.BlockSpec((part.shape[0], step), lambda i: (0, i)) for part in parts]
        + [pl.BlockSpec(memory_space=pl.ANY)] * len(after),
        out_specs=pl.BlockSpec((count, step), lambda i: (0, i)),
        out_shape=jax.ShapeDtypeStruct((count, width), BF16),
        scratch_shapes=[
            pltpu.VMEM((count, rows), F32),
            pltpu.VMEM((count, step), BF16),
            pltpu.VMEM((rows, step), BF16),
            pltpu.VMEM((rows, step), BF16),
        ],
        compiler_params=params(),
        cost_estimate=pl.CostEstimate(
            flops=8 * count * rows * width, bytes_accessed=8 * rows * width, transcendentals=count * rows * width // HD
        ),
        name="attend",
    )(sample_col, sample_row, *parts, *after)


def gather(rows):
    return lax.all_gather(rows, "bag", axis=1, tiled=True)


def small_rows(width):
    return SMALL_BYTES // (2 * width) // 16 * 16


def gather_small(rows):
    count, width = rows.shape
    number = -(-count // small_rows(width))
    step = up16(-(-count // number))
    return jnp.concatenate([gather(rows[at:min(at + step, count)]) for at in range(0, count, step)])


def term_kernel(rows, weight, out):
    out[...] = dot(rows[...], weight[...]).astype(BF16)


def terms(rows, weight):
    count, depth = rows.shape
    width = weight.shape[1]
    step = 512
    return pl.pallas_call(
        term_kernel,
        grid=(width // step,),
        in_specs=[
            pl.BlockSpec((count, depth), lambda i: (0, 0)),
            pl.BlockSpec((depth, step), lambda i: (0, i)),
        ],
        out_specs=pl.BlockSpec((count, step), lambda i: (0, i)),
        out_shape=jax.ShapeDtypeStruct((count, width), BF16),
        compiler_params=params(),
        cost_estimate=pl.CostEstimate(
            flops=2 * count * depth * width, bytes_accessed=2 * depth * width, transcendentals=0
        ),
        name="terms",
    )(rows, weight)


def body(
    home_tokens,
    mod_weight,
    qkv_weight,
    norm_gain,
    output_weight,
    row_plan,
    sample_lengths,
    modality,
):
    bags = lax.axis_size("dp")
    me = lax.axis_index("dp")
    count, width = home_tokens.shape
    pack = count + count // 4
    capacity = 2 * count // bags
    caps = (capacity // PERIOD * FIRST, capacity // PERIOD * (PERIOD - FIRST))
    slots = tuple(bags * cap for cap in caps)
    home_rows = part_sizes(count, bags)
    bag_rows = part_sizes(pack, bags)
    rows = sum(bag_rows)
    vmem = pl.BlockSpec(memory_space=pltpu.VMEM)
    smem = pl.BlockSpec(memory_space=pltpu.SMEM)
    ends = jnp.cumsum(sample_lengths, axis=1)

    own_plan = lax.dynamic_slice_in_dim(row_plan, me * count, count, 0)
    plan_row = own_plan.reshape(1, count)
    even, odd, order_even, order_odd, where_row, where_col = pl.pallas_call(
        functools.partial(order_kernel, bags, pack),
        in_specs=[vmem] * 2,
        out_specs=[vmem] * 6,
        out_shape=[jax.ShapeDtypeStruct((size, width), BF16) for size in home_rows]
        + [jax.ShapeDtypeStruct((size, count), BF16) for size in home_rows]
        + [
            jax.ShapeDtypeStruct((1, count), jnp.int32),
            jax.ShapeDtypeStruct((count, 1), jnp.int32),
        ],
        compiler_params=params(),
        name="order",
    )(plan_row, home_tokens)
    full_even = gather(even)
    full_odd = gather_small(odd)
    send_even, send_odd, kind_even, kind_odd, final_even, final_odd = pl.pallas_call(
        functools.partial(send_kernel, bags, pack, caps),
        in_specs=[smem, smem] + [vmem] * 5,
        out_specs=[vmem] * 6,
        out_shape=[jax.ShapeDtypeStruct(shape, BF16) for shape in zip(slots, home_rows)]
        + [jax.ShapeDtypeStruct((size, 128), F32) for size in home_rows]
        + [jax.ShapeDtypeStruct((count, size), BF16) for size in slots],
        compiler_params=params(),
        name="send_plan",
    )(ends, modality, plan_row, where_row, where_col, order_even, order_odd)
    pack_even, pack_odd, back_even, back_odd, samples = pl.pallas_call(
        functools.partial(bag_kernel, pack, caps),
        in_specs=[smem, smem, vmem],
        out_specs=[vmem] * 5,
        out_shape=[jax.ShapeDtypeStruct(shape, BF16) for shape in zip(bag_rows, slots)]
        + [jax.ShapeDtypeStruct(shape, BF16) for shape in zip(slots, bag_rows)]
        + [jax.ShapeDtypeStruct((rows, 128), F32)],
        scratch_shapes=[pltpu.VMEM((max(slots), 128), BF16)],
        compiler_params=params(),
        name="bag_plan",
    )(me.reshape(1).astype(jnp.int32), ends, row_plan.reshape(bags, count))
    sample_row = samples[:, 0].reshape(1, rows)

    def exchange(outgoing):
        arrived = lax.all_to_all(outgoing.reshape(bags, -1, width), "dp", split_axis=0, concat_axis=0, tiled=True)
        return arrived.reshape(-1, width)

    outgoing_odd = project("project", full_odd, kind_odd, mod_weight, send_odd)
    arrived_odd = exchange(outgoing_odd)
    outgoing_even = project("project", full_even, kind_even, mod_weight, send_even, [outgoing_odd])
    arrived_even = exchange(outgoing_even)
    bag_odd = gather(move_rows("pack", pack_odd, arrived_odd, [outgoing_even]))
    packed_even = move_rows("pack", pack_even, arrived_even, [])
    small = small_rows(width)
    bag_late = gather(packed_even[small:])
    bag_early = gather(packed_even[:small])
    every = (0, 1, 2)
    odd = make_qkv(bag_odd, qkv_weight, norm_gain, every)
    early = make_qkv(bag_early, qkv_weight, norm_gain, every)
    late = make_qkv(bag_late, qkv_weight, norm_gain, every, [odd[0], early[0]])
    keys = early[1], late[1], odd[1]
    values = early[2], late[2], odd[2]
    first = bag_rows[0]
    def to_home(rows, back):
        summed = lax.psum_scatter(terms(rows, output_weight), "bag", scatter_dimension=1, tiled=True)
        return exchange(dot(back, summed).astype(BF16))

    attended_even = attend(samples[:first], sample_row, (early[0], late[0]), keys, values)
    home_even = to_home(attended_even, back_even)
    attended_odd = attend(samples[first:], sample_row, (odd[0],), keys, values, [attended_even])
    home_odd = to_home(attended_odd, back_odd)
    return (dot(final_even, home_even) + dot(final_odd, home_odd)).astype(BF16)


def solution(mesh):
    in_specs = (
        P("dp", "bag"),
        P(None, None, "bag"),
        P(None, None, "bag"),
        P(None, "bag"),
        P("bag", None),
        P(),
        P(),
        P(),
    )
    return jax.shard_map(body, mesh=mesh, in_specs=in_specs, out_specs=P("dp", "bag"), check_vma=False)
```

time: 323 us -> 318 us (0.985)
  blocking collectives: 0 us -> 97 us
  waiting for transfers between devices: 162 us -> 84 us
  Pallas kernels: 62 us -> 91.1 us
  starting transfers between devices: 38.7 us -> 11.3 us
  matrix products: 23.4 us -> 8.17 us
  other arithmetic: 12.7 us -> 1.86 us
    all_gather x0 -> x3, blocking collectives: none -> 78.3 us  [gather(): return lax.all_gather(rows, 'bag', axis=1, tiled=True)]
    ppermute x9 -> x0, waiting for transfers between devices: 66 us -> none  [the longest x3 35.1 us: own_columns(): other = lax.ppermute(part, 'dp', [(i, i ^ bit) for i in range(bags)])]
    reduce_scatter x0 -> x2, waiting for transfers between devices: none -> 64 us  [to_home(): lax.psum_scatter(terms(rows, output_weight), 'bag', scatter_dimension=1,...]
    all_gather x5 -> x3, waiting for transfers between devices: 57.5 us -> 11.4 us  [gather(): return lax.all_gather(rows, 'bag', axis=1, tiled=True)]
    all_to_all x5 -> x3, waiting for transfers between devices: 37.8 us -> 8.53 us  [exchange(): lax.all_to_all(outgoing.reshape(bags, -1, width), 'dp', split_axis=0, con...]
    pallas_call x6 -> x11, Pallas kernels: 43.2 us -> 71.9 us  [the longest x3 29.6 us: make_qkv(): pl.pallas_call(functools.partial(qkv_kernel, which), grid=(width // step,...]
    ppermute x9 -> x0, starting transfers between devices: 20.5 us -> none  [the longest x3 13.3 us: line_sum(): up = lax.ppermute(to_up, 'bag', [(i, i + 1) for i in range(step)])]
    all_to_all x0 -> x1, blocking collectives: none -> 18.7 us  [exchange(): lax.all_to_all(outgoing.reshape(bags, -1, width), 'dp', split_axis=0, con...]
  transfers between devices with their start and end apart: 19 -> 8, of which waited for: 12 -> 4; matrix products, arithmetic and copies ran while one was open for 13% -> 5% of each run, Pallas kernels for 18% -> 19%
where the time goes in v3:
time: 318 us; the launch traced here: 317 us
  blocking collectives  97 us (31%)
  Pallas kernels  91.1 us (29%)
  waiting for transfers between devices  84 us (26%)
  between operations  13.2 us (4%)
  starting transfers between devices  11.3 us (4%)
  local copies, waits for them, and re-layouts  9.88 us (3%)
  matrix products  8.17 us (3%)
    all_gather x3, blocking collectives, gather(): return lax.all_gather(rows, 'bag', axis=1, tiled=True)  78.3 us
    reduce_scatter x2, waiting for transfers between devices, to_home(): lax.psum_scatter(terms(rows, output_weight), 'bag', scatter_dimension=1,...  64 us
    pallas_call x3, Pallas kernels, make_qkv(): pl.pallas_call(functools.partial(qkv_kernel, which), grid=(width // step,...  29.6 us
    all_to_all x1, blocking collectives, exchange(): lax.all_to_all(outgoing.reshape(bags, -1, width), 'dp', split_axis=0, con...  18.7 us
    pallas_call x2, Pallas kernels, attend(): pl.pallas_call(functools.partial(attend_kernel, (len(queries), len(keys))...  17.3 us
    pallas_call x2, Pallas kernels, project(): pl.pallas_call(project_kernel, grid=(width // step,), in_specs=[pl.BlockS...  15.6 us
    pallas_call x2, Pallas kernels, terms(): pl.pallas_call(term_kernel, grid=(width // step,), in_specs=[pl.BlockSpec...  13.3 us
    all_gather x3, waiting for transfers between devices, gather(): return lax.all_gather(rows, 'bag', axis=1, tiled=True)  11.4 us
  transfers between devices with their start and end apart: 8, of which 4 were waited for; matrix products, arithmetic and copies ran while one was open for 5% of the time, Pallas kernels for 19%

profile of v3, /device:TPU:0, one launch (start us, length us, event | category | flops | bytes accessed | tf_op | source)
XLA Modules:
  0.0 316.6 jit_solution(18340663898013340411)
XLA Ops:
  6.5 0.0 all-gather.4.cloned.1.call-start
  6.5 1.4 dynamic_slice.3
  7.9 3.7 %order.1 = (bf16[336,768]{1,0:T(8,128)(2,1)}, bf16[192,768]{1,0:T(8,128)(2,1)}, bf16[336,512]{1,0:T(8,128)(2,1)}, bf16[192,512]{1,0:T(8,128)(2,1)}, s32[1,512]{1,0:T(1,128)}, /*index=5*/s32[512,1]{1,0:T(8,128)}) custom-call(s32[1,512]{1,0:T(1,128)} %bitcast.30, bf16[512,768]{1,0:T(8,128)(2,1)} %tokens.1), custom_call_target="tpu_custom_call" | custom-call | tf_op jit(solution)/shard_map/order/pallas_call | solution.py:386
  11.5 0.0 all-gather.4.cloned.1.call-update
  11.6 0.8 copy.11
  12.3 0.7 reduce_window_sum.11.ends
  13.1 1.3 copy.12.modality
  14.4 3.3 %send_plan.1 = (bf16[640,336]{1,0:T(8,128)(2,1)}, bf16[384,192]{1,0:T(8,128)(2,1)}, f32[336,128]{1,0:T(8,128)}, f32[192,128]{1,0:T(8,128)}, bf16[512,640]{1,0:T(8,128)(2,1)}, /*index=5*/bf16[512,384]{1,0:T(8,128)(2,1)}) custom-call(s32[8,4]{1,0:T(8,128)} %reduce_window_sum.11.ends, s32[8,4]{1,0:T(8,128)} %copy.12.modality, s32[1,512]{1,0:T(1,128)} %bitcast.31, ...), custom_call_target="tpu_custom_call" | custom-call | tf_op jit(solution)/shard_map/send_plan/pallas_call | solution.py:401
  17.7 1.0 fusion
  18.7 25.8 %all_gather.19 = bf16[96,3072]{1,0:T(8,128)(2,1)S(1)} all-gather(bf16[96,768]{1,0:T(8,128)(2,1)S(1)} %get-tuple-element.57), channel_id=1, replica_groups=mesh['dp'=8,'bag'=4] {'bag'}, dimensions={1}, use_global_device_ids=true | all-gather | bytes 737280 | tf_op jit(solution)/shard_map/all_gather | solution.py:321
  44.5 24.5 %all_gather.20 = bf16[96,3072]{1,0:T(8,128)(2,1)S(1)} all-gather(bf16[96,768]{1,0:T(8,128)(2,1)S(1)} %get-tuple-element.58), channel_id=1, replica_groups=mesh['dp'=8,'bag'=4] {'bag'}, dimensions={1}, use_global_device_ids=true | all-gather | bytes 737280 | tf_op jit(solution)/shard_map/all_gather | solution.py:321
  69.0 1.1 pad_maximum_fusion.rows_in
  70.1 0.0 copy-start.5
  70.1 7.1 %project.2.refs_0_ = bf16[384,768]{1,0:T(8,128)(2,1)} custom-call(bf16[192,3072]{1,0:T(8,128)(2,1)} %pad_maximum_fusion.rows_in, f32[192,128]{1,0:T(8,128)} %get-tuple-element.43.kinds, bf16[2,3072,768]{2,1,0:T(8,128)(2,1)} %weight.5, bf16[384,192]{1,0:T(8,128)(2,1)} %get-tuple-element.44.send), custom_call_target="tpu_custom_call" | custom-call | flops 1811939328 | bytes 9437184 | tf_op jit(solution)/shard_map/project/pallas_call | solution.py:191
  77.2 3.7 %all-to-all-start.1 = ((bf16[8,48,768]{2,1,0:T(8,128)(2,1)}), bf16[8,48,768]{2,1,0:T(8,128)(2,1)S(1)}, u32[]{:S(2)}, u32[]{:S(2)}) async-start(bf16[8,48,768]{2,1,0:T(8,128)(2,1)} %bitcast.22), calls=%async_computation.1 | async-start | bytes 1179648 | tf_op jit(solution)/shard_map/all_to_all | solution.py:425
  80.9 0.0 all-gather.8.cloned.1.call-start
  80.9 0.0 copy-done.5
  81.0 0.6 reshape.40.plan
  81.6 3.2 %bag_plan.1 = (bf16[416,640]{1,0:T(8,128)(2,1)}, bf16[240,384]{1,0:T(8,128)(2,1)}, bf16[640,416]{1,0:T(8,128)(2,1)}, bf16[384,240]{1,0:T(8,128)(2,1)}, f32[656,128]{1,0:T(8,128)}) custom-call(s32[1]{0:T(128)} %bitcast.1.me, s32[8,4]{1,0:T(8,128)} %reduce_window_sum.11.ends, s32[8,512]{1,0:T(8,128)} %reshape.40.plan), custom_call_target="tpu_custom_call" | custom-call | tf_op jit(solution)/shard_map/bag_plan/pallas_call | solution.py:411
  84.7 0.0 all-gather.4.cloned.1.call-done.rows_in
  84.8 8.5 %project.3.refs_0_ = bf16[640,768]{1,0:T(8,128)(2,1)} custom-call(bf16[336,3072]{1,0:T(8,128)(2,1)} %all-gather.4.cloned.1.call-done.rows_in, f32[336,128]{1,0:T(8,128)} %get-tuple-element.40.kinds, bf16[2,3072,768]{2,1,0:T(8,128)(2,1)} %weight.5, bf16[640,336]{1,0:T(8,128)(2,1)} %get-tuple-element.41.send, bf16[384,768]{1,0:T(8,128)(2,1)} %project.2.refs_0_), custom_call_target="tpu_custom_call" | custom-call | flops 3170893824 | bytes 9437184 | tf_op jit(solution)/shard_map/project/pallas_call | solution.py:191
  93.3 0.0 copy-start
  93.3 0.0 all-to-all-done.1
  93.3 0.8 copy-done.1
  94.1 2.3 pack.3
  96.3 0.0 all-gather.8.cloned.1.call-update
  96.4 0.0 all-gather.6.cloned.1.call-start
  96.4 0.0 copy-done
  96.4 18.7 %all_to_all.20 = bf16[8,80,768]{2,1,0:T(8,128)(2,1)} all-to-all(bf16[8,80,768]{2,1,0:T(8,128)(2,1)S(1)} %bitcast.21), channel_id=1, replica_groups=mesh['dp'=8,'bag'=4] {'dp'}, dimensions={0} | all-to-all | bytes 1966080 | tf_op jit(solution)/shard_map/all_to_all | solution.py:425
  115.1 2.9 pack.2
  118.0 1.8 slice.29
  119.9 0.0 all-gather.6.cloned.1.call-update
  119.9 0.0 reduce-scatter.3.cloned.1.call-start
  119.9 0.0 copy-done.2
  119.9 0.7 slice.21.sample_col
  120.6 0.2 slice_reduce_fusion
  120.8 0.6 reshape_squeeze.3.sample_row
  121.4 0.0 slice-done
  121.4 28.0 %all_gather.21.rows_in = bf16[160,3072]{1,0:T(8,128)(2,1)} all-gather(bf16[160,768]{1,0:T(8,128)(2,1)S(1)} %slice-done), channel_id=1, replica_groups=mesh['dp'=8,'bag'=4] {'bag'}, dimensions={1}, use_global_device_ids=true | all-gather | bytes 1228800 | tf_op jit(solution)/shard_map/all_gather | solution.py:321
  149.5 9.2 %qkv.3 = (bf16[160,768]{1,0:T(8,128)(2,1)}, bf16[160,768]{1,0:T(8,128)(2,1)}, bf16[160,768]{1,0:T(8,128)(2,1)}) custom-call(bf16[160,3072]{1,0:T(8,128)(2,1)} %all_gather.21.rows_in, f32[3,2,256]{2,1,0:T(2,128)} %bitcast.27, bf16[3,3072,768]{2,1,0:T(8,128)(2,1)} %refs_2_.5, bf16[3,3072,768]{2,1,0:T(8,128)(2,1)} %refs_2_.5, bf16[3,3072,768]{2,1,0:T(8,128)(2,1)} %refs_2_.5), custom_call_target="tpu_custom_call" | custom-call | flops 2264924160 | bytes 14155776 | tf_op jit(solution)/shard_map/qkv/pallas_call | solution.py:239
  158.7 10.1 %qkv.4 = (bf16[240,768]{1,0:T(8,128)(2,1)}, bf16[240,768]{1,0:T(8,128)(2,1)}, bf16[240,768]{1,0:T(8,128)(2,1)}) custom-call(bf16[240,3072]{1,0:T(8,128)(2,1)} %all-gather.8.cloned.1.call-done.rows_in, f32[3,2,256]{2,1,0:T(2,128)} %bitcast.28, bf16[3,3072,768]{2,1,0:T(8,128)(2,1)} %refs_2_.5, bf16[3,3072,768]{2,1,0:T(8,128)(2,1)} %refs_2_.5, ...), custom_call_target="tpu_custom_call" | custom-call | flops 3397386240 | bytes 14155776 | tf_op jit(solution)/shard_map/qkv/pallas_call | solution.py:239
  168.8 11.4 %all-gather.6.cloned.1.call-done.rows_in = bf16[256,3072]{1,0:T(8,128)(2,1)} async-done(((bf16[256,768]{1,0:T(8,128)(2,1)}), bf16[256,3072]{1,0:T(8,128)(2,1)}) %all-gather.6.cloned.1.call-update) | async-done | bytes 1572880 | tf_op jit(solution)/shard_map/all_gather | solution.py:321
  180.2 10.3 %qkv.5 = (bf16[256,768]{1,0:T(8,128)(2,1)}, bf16[256,768]{1,0:T(8,128)(2,1)}, bf16[256,768]{1,0:T(8,128)(2,1)}) custom-call(bf16[256,3072]{1,0:T(8,128)(2,1)} %all-gather.6.cloned.1.call-done.rows_in, f32[3,2,256]{2,1,0:T(2,128)} %bitcast.29, bf16[3,3072,768]{2,1,0:T(8,128)(2,1)} %refs_2_.5, bf16[3,3072,768]{2,1,0:T(8,128)(2,1)} %refs_2_.5, ...), custom_call_target="tpu_custom_call" | custom-call | flops 3623878656 | bytes 14155776 | tf_op jit(solution)/shard_map/qkv/pallas_call | solution.py:239
  190.5 9.0 %attend.2.rows.refs_7_ = bf16[416,768]{1,0:T(8,128)(2,1)} custom-call(f32[416,128]{1,0:T(8,128)} %slice.21.sample_col, f32[1,656]{1,0:T(1,128)} %reshape_squeeze.3.sample_row, bf16[160,768]{1,0:T(8,128)(2,1)} %get-tuple-element.45.refs_4_.refs_0_, bf16[256,768]{1,0:T(8,128)(2,1)} %get-tuple-element.48.refs_1_, ...), custom_call_target="tpu_custom_call" | custom-call | flops 1676673024 | bytes 4030464 | tf_op jit(solution)/shard_map/attend/pallas_call | solution.py:296
  199.6 7.0 %terms.2 = bf16[416,3072]{1,0:T(8,128)(2,1)} custom-call(bf16[416,768]{1,0:T(8,128)(2,1)} %attend.2.rows.refs_7_, bf16[768,3072]{1,0:T(8,128)(2,1)} %weight.7), custom_call_target="tpu_custom_call" | custom-call | flops 1962934272 | bytes 4718592 | tf_op jit(solution)/shard_map/terms/pallas_call | solution.py:343
  206.5 0.0 reduce-scatter.3.cloned.1.call-update
  206.6 0.0 reduce-scatter.5.cloned.1.call-start
  206.6 0.7 slice.27.sample_col
  207.3 8.3 %attend.3.rows = bf16[240,768]{1,0:T(8,128)(2,1)} custom-call(f32[240,128]{1,0:T(8,128)} %slice.27.sample_col, f32[1,656]{1,0:T(1,128)} %reshape_squeeze.3.sample_row, bf16[240,768]{1,0:T(8,128)(2,1)} %get-tuple-element.47.refs_3_.refs_0_, bf16[160,768]{1,0:T(8,128)(2,1)} %get-tuple-element.49.refs_2_.refs_1_, ...), custom_call_target="tpu_custom_call" | custom-call | flops 967311360 | bytes 4030464 | tf_op jit(solution)/shard_map/attend/pallas_call | solution.py:296
  215.6 6.3 %terms.3 = bf16[240,3072]{1,0:T(8,128)(2,1)} custom-call(bf16[240,768]{1,0:T(8,128)(2,1)} %attend.3.rows, bf16[768,3072]{1,0:T(8,128)(2,1)} %weight.7), custom_call_target="tpu_custom_call" | custom-call | flops 1132462080 | bytes 4718592 | tf_op jit(solution)/shard_map/terms/pallas_call | solution.py:343
  221.9 0.0 reduce-scatter.5.cloned.1.call-update
  221.9 34.8 %reduce-scatter.3.cloned.1.call-done = bf16[416,768]{1,0:T(8,128)(2,1)} async-done(((bf16[416,3072]{1,0:T(8,128)(2,1)}), bf16[416,768]{1,0:T(8,128)(2,1)}) %reduce-scatter.3.cloned.1.call-update) | async-done | bytes 638992 | tf_op jit(solution)/shard_map/reduce_scatter | solution.py:445
  256.7 0.0 copy-done.6
  256.7 2.7 convolution_convert_fusion
  259.4 3.8 %all-to-all-start.2 = ((bf16[8,80,768]{2,1,0:T(8,128)(2,1)}), bf16[8,80,768]{2,1,0:T(8,128)(2,1)S(1)}, u32[]{:S(2)}, u32[]{:S(2)}) async-start(bf16[8,80,768]{2,1,0:T(8,128)(2,1)} %bitcast.9), calls=%async_computation.3 | async-start | bytes 1966080 | tf_op jit(solution)/shard_map/all_to_all | solution.py:425
  263.2 29.2 %reduce-scatter.5.cloned.1.call-done = bf16[240,768]{1,0:T(8,128)(2,1)} async-done(((bf16[240,3072]{1,0:T(8,128)(2,1)}), bf16[240,768]{1,0:T(8,128)(2,1)}) %reduce-scatter.5.cloned.1.call-update) | async-done | bytes 368656 | tf_op jit(solution)/shard_map/reduce_scatter | solution.py:445
  292.4 0.0 copy-done.4
  292.4 2.1 convolution_convert_fusion.1
  294.5 0.0 all-to-all-done.2
  294.5 3.7 %all-to-all-start.3 = ((bf16[8,48,768]{2,1,0:T(8,128)(2,1)}), bf16[8,48,768]{2,1,0:T(8,128)(2,1)S(1)}, u32[]{:S(2)}, u32[]{:S(2)}) async-start(bf16[8,48,768]{2,1,0:T(8,128)(2,1)} %bitcast.11), calls=%async_computation.5 | async-start | bytes 1179648 | tf_op jit(solution)/shard_map/all_to_all | solution.py:425
  298.1 1.9 fusion.1
  300.1 8.5 %all-to-all-done.3 = bf16[8,48,768]{2,1,0:T(8,128)(2,1)S(1)} async-done(((bf16[8,48,768]{2,1,0:T(8,128)(2,1)}), bf16[8,48,768]{2,1,0:T(8,128)(2,1)S(1)}, u32[]{:S(2)}, u32[]{:S(2)}) %all-to-all-start.3) | async-done | bytes 589856 | tf_op jit(solution)/shard_map/all_to_all | solution.py:425
  308.6 0.0 copy-done.3
  308.6 1.5 add_convert_fusion
  (7 shorter events, 0.0 us)
Async XLA Ops:
  6.5 78.2 %all-gather.4.cloned.1.call-start = ((), (), s32[]{:S(2)}) async-start(), calls=%async_computation.6 | async-start | bytes 2580480 | tf_op jit(solution)/shard_map/all_gather | solution.py:321
  70.1 10.8 %copy-start.5 = (s32[4096]{0:T(1024)S(1)}, s32[4096]{0:T(1024)}, u32[]{:S(2)}) copy-start(s32[4096]{0:T(1024)} %param.13) | copy-start | bytes 49156
  77.2 16.1 %all-to-all-start.1 = ((bf16[8,48,768]{2,1,0:T(8,128)(2,1)}), bf16[8,48,768]{2,1,0:T(8,128)(2,1)S(1)}, u32[]{:S(2)}, u32[]{:S(2)}) async-start(bf16[8,48,768]{2,1,0:T(8,128)(2,1)} %bitcast.22), calls=%async_computation.1 | async-start | bytes 1179648 | tf_op jit(solution)/shard_map/all_to_all | solution.py:425
  80.9 77.8 %all-gather.8.cloned.1.call-start = ((), (), s32[]{:S(2)}) async-start(), calls=%async_computation.8 | async-start | bytes 1843200 | tf_op jit(solution)/shard_map/all_gather | solution.py:321
  93.3 3.2 copy-start
  93.3 0.8 copy-start.1
  96.4 83.9 %all-gather.6.cloned.1.call-start = ((), (), s32[]{:S(2)}) async-start(), calls=%async_computation.7 | async-start | bytes 1966080 | tf_op jit(solution)/shard_map/all_gather | solution.py:321
  115.1 4.8 %copy-start.2 = (f32[656,128]{1,0:T(8,128)S(1)}, f32[656,128]{1,0:T(8,128)}, u32[]{:S(2)}) copy-start(f32[656,128]{1,0:T(8,128)} %get-tuple-element.37) | copy-start | bytes 1007620
  118.0 3.4 %slice-start = ((bf16[416,768]{1,0:T(8,128)(2,1)}), bf16[160,768]{1,0:T(8,128)(2,1)S(1)}, s32[]{:S(2)}) async-start(bf16[416,768]{1,0:T(8,128)(2,1)} %pack.2), calls=%async_computation.11 | async-start | bytes 491520 | tf_op jit(solution)/shard_map/slice | solution.py:436
  119.9 136.8 %reduce-scatter.3.cloned.1.call-start = ((), (), s32[]{:S(2)}) async-start(), calls=%async_computation.9 | async-start | bytes 3194880 | tf_op jit(solution)/shard_map/reduce_scatter | solution.py:445
  206.6 85.8 %reduce-scatter.5.cloned.1.call-start = ((), (), s32[]{:S(2)}) async-start(), calls=%async_computation.10 | async-start | bytes 1843200 | tf_op jit(solution)/shard_map/reduce_scatter | solution.py:445
  215.6 41.1 %copy-start.6 = (bf16[640,416]{1,0:T(8,128)(2,1)S(1)}, bf16[640,416]{1,0:T(8,128)(2,1)}, u32[]{:S(2)}) copy-start(bf16[640,416]{1,0:T(8,128)(2,1)} %get-tuple-element.36) | copy-start | bytes 1597444
  259.4 33.0 %copy-start.4 = (bf16[384,240]{1,0:T(8,128)(2,1)S(1)}, bf16[384,240]{1,0:T(8,128)(2,1)}, u32[]{:S(2)}) copy-start(bf16[384,240]{1,0:T(8,128)(2,1)} %get-tuple-element.56) | copy-start | bytes 552964
  259.4 35.1 %all-to-all-start.2 = ((bf16[8,80,768]{2,1,0:T(8,128)(2,1)}), bf16[8,80,768]{2,1,0:T(8,128)(2,1)S(1)}, u32[]{:S(2)}, u32[]{:S(2)}) async-start(bf16[8,80,768]{2,1,0:T(8,128)(2,1)} %bitcast.9), calls=%async_computation.3 | async-start | bytes 1966080 | tf_op jit(solution)/shard_map/all_to_all | solution.py:425
  294.5 14.1 %all-to-all-start.3 = ((bf16[8,48,768]{2,1,0:T(8,128)(2,1)}), bf16[8,48,768]{2,1,0:T(8,128)(2,1)S(1)}, u32[]{:S(2)}, u32[]{:S(2)}) async-start(bf16[8,48,768]{2,1,0:T(8,128)(2,1)} %bitcast.11), calls=%async_computation.5 | async-start | bytes 1179648 | tf_op jit(solution)/shard_map/all_to_all | solution.py:425
  298.1 10.4 %copy-start.3 = (bf16[512,384]{1,0:T(8,128)(2,1)S(1)}, bf16[512,384]{1,0:T(8,128)(2,1)}, u32[]{:S(2)}) copy-start(bf16[512,384]{1,0:T(8,128)(2,1)} %get-tuple-element.55) | copy-start | bytes 1179652
Sparse Core Ops, SparseCore 0:
  11.7 66.1 all-gather.3
  96.5 43.8 all-gather.7
  142.0 38.2 all-gather.5
  206.7 49.9 reduce-scatter.2
  259.0 33.3 reduce-scatter.4

commit v4 on v3

--- a/solution.py
+++ b/solution.py
@@ -13,12 +13,13 @@
 FIRST = 5
 SMALL_BYTES = 240 * 1024
 VMEM_LIMIT = 56 * 1024 * 1024
+SMALL_LIMIT = 24 * 1024 * 1024
 BF16 = jnp.bfloat16
 F32 = jnp.float32
 
 
-def params():
-    return pltpu.CompilerParams(vmem_limit_bytes=VMEM_LIMIT)
+def params(limit=VMEM_LIMIT):
+    return pltpu.CompilerParams(vmem_limit_bytes=limit)
 
 
 def up16(count):
@@ -69,7 +70,7 @@
     return ((iota((rows, count), 0) == rank_row) & chosen).astype(F32).astype(BF16)
 
 
-def order_kernel(bags, pack, plan_row, tokens, even, odd, order_even, order_odd, where_row, where_col):
+def order_kernel(bags, pack, plan_row, tokens, order_even, order_odd, where_row, where_col, even, *odds):
     count = plan_row.shape[1]
     diagonal = iota((count, count), 0) == iota((count, count), 1)
     plan_col = jnp.sum(jnp.where(diagonal, plan_row[...].astype(F32), 0.0), axis=1, keepdims=True).astype(jnp.int32)
@@ -80,31 +81,39 @@
     below = iota((count, count), 0) > iota((count, count), 1)
     place_col = total(same & below, 1)
     place_row = total(same & above, 0)
-    for part, (ordered, order) in enumerate(((even, order_even), (odd, order_odd))):
-        onehot = order_onehot(part, place_row, place_col, ordered.shape[0])
+    for part, (outs, order) in enumerate((((even,), order_even), (odds, order_odd))):
+        onehot = order_onehot(part, place_row, place_col, order.shape[0])
         order[...] = onehot
-        ordered[...] = dot(onehot, tokens[...]).astype(BF16)
+        ordered = dot(onehot, tokens[...]).astype(BF16)
+        at = 0
+        for out in outs:
+            out[...] = ordered[at:at + out.shape[0], :]
+            at += out.shape[0]
     where_row[...] = bag_row * 65536 + place_row
     where_col[...] = bag_col * 65536 + place_col
 
 
-def move_kernel(onehot, rows, *refs):
-    refs[-1][...] = dot(onehot[...], rows[...]).astype(BF16)
-
-
-def move_rows(name, onehot, rows, after):
+def move_kernel(number, onehot, rows, *refs):
+    moved = dot(onehot[...], rows[...]).astype(BF16)
+    at = 0
+    for out in refs[-number:]:
+        out[...] = moved[at:at + out.shape[0], :]
+        at += out.shape[0]
+
+
+def move_rows(name, onehot, rows, sizes, after=()):
     vmem = pl.BlockSpec(memory_space=pltpu.VMEM)
     return pl.pallas_call(
-        move_kernel,
+        functools.partial(move_kernel, len(sizes)),
         in_specs=[vmem] * 2 + [pl.BlockSpec(memory_space=pl.ANY)] * len(after),
-        out_specs=vmem,
-        out_shape=jax.ShapeDtypeStruct((onehot.shape[0], rows.shape[1]), BF16),
+        out_specs=[vmem] * len(sizes),
+        out_shape=[jax.ShapeDtypeStruct((size, rows.shape[1]), BF16) for size in sizes],
         compiler_params=params(),
         name=name,
     )(onehot, rows, *after)
 
 
-def send_kernel(bags, pack, caps, ends, modality, plan_row, where_row, where_col, order_even, order_odd,
+def send_kernel(bags, pack, caps, lengths, modality, plan_row, where_row, where_col, order_even, order_odd,
                 send_even, send_odd, kind_even, kind_odd, final_even, final_odd):
     count = plan_row.shape[1]
     bag_row = where_row[...] >> 16
@@ -115,8 +124,8 @@
     kind = jnp.zeros((1, count), F32)
     for bag in range(bags):
         begin = bag * pack
-        for sample in range(ends.shape[1]):
-            end = bag * pack + ends[bag, sample]
+        for sample in range(lengths.shape[1]):
+            end = begin + lengths[bag, sample]
             inside = (plan >= begin) & (plan < end)
             kind = jnp.where(inside, modality[bag, sample].astype(F32), kind)
             begin = end
@@ -132,79 +141,102 @@
         final[...] = match.astype(F32).astype(BF16)
 
 
-def bag_kernel(pack, caps, me, ends, plan, pack_even, pack_odd, back_even, back_odd, samples, held):
-    homes, count = plan.shape
+def bag_counts(pack, me, plan, part):
     slot = plan[...] - me[0] * pack
     mine = (slot >= 0) & (slot < pack)
-    ahead = (iota((count, count), 0) < iota((count, count), 1)).astype(F32).astype(BF16)
-    place = dot(mine.astype(F32).astype(BF16), ahead).astype(jnp.int32)
-    place = jnp.where(mine, place, -PERIOD)
     filled = total(mine, 1)
-    first = 0
-    for part, (packer, back) in enumerate(((pack_even, back_even), (pack_odd, back_odd))):
+    whole = filled // PERIOD * FIRST + jnp.minimum(filled % PERIOD, FIRST)
+    return slot, mine, whole if part == 0 else filled - whole
+
+
+def pack_plan_kernel(pack, caps, me, plan, pack_even, pack_odd):
+    for part, packer in enumerate((pack_even, pack_odd)):
+        heres = bag_counts(pack, me, plan, part)[2]
         rows, slots = packer.shape
-        half = caps[part]
-        own_place = part_place(place, part)
-        whole = filled // PERIOD * FIRST + jnp.minimum(filled % PERIOD, FIRST)
-        heres = whole if part == 0 else filled - whole
         lanes = iota((1, slots), 1)
         shift = jnp.zeros((1, slots), jnp.int32)
         limit = jnp.zeros((1, slots), jnp.int32)
         start = jnp.zeros((1, 1), jnp.int32)
+        for home in range(plan.shape[0]):
+            here = heres[home:home + 1, :]
+            base = home * caps[part]
+            of_home = (lanes >= base) & (lanes < base + caps[part])
+            shift = jnp.where(of_home, start - base, shift)
+            limit = jnp.where(of_home, here + base, limit)
+            start = start + here
+        packer[...] = ((iota((rows, slots), 0) == lanes + shift) & (lanes < limit)).astype(F32).astype(BF16)
+
+
+def bag_kernel(pack, caps, me, lengths, plan, pack_even, pack_odd, back_even, back_odd, samples, held):
+    homes, count = plan.shape
+    first = 0
+    for part, (packer, back) in enumerate(((pack_even, back_even), (pack_odd, back_odd))):
+        slot, mine, heres = bag_counts(pack, me, plan, part)
+        ahead = (iota((count, count), 0) < iota((count, count), 1)).astype(F32).astype(BF16)
+        place = dot(mine.astype(F32).astype(BF16), ahead).astype(jnp.int32)
+        own_place = part_place(jnp.where(mine, place, -PERIOD), part)
+        rows, slots = packer.shape
+        cap = caps[part]
+        start = jnp.zeros((1, 1), jnp.int32)
         for home in range(homes):
             here = heres[home:home + 1, :]
-            of_home = (lanes >= home * half) & (lanes < (home + 1) * half)
-            shift = jnp.where(of_home, start - home * half, shift)
-            limit = jnp.where(of_home, here + home * half, limit)
-            down = iota((half, back.shape[1]), 0)
-            across = iota((half, back.shape[1]), 1)
-            block = ((across == down + start) & (down < here)).astype(F32).astype(BF16)
-            back[home * half:(home + 1) * half, :] = block
-            chosen = own_place[home:home + 1, :] == iota((half, count), 0)
+            down = iota((cap, rows), 0)
+            block = ((iota((cap, rows), 1) == down + start) & (down < here)).astype(F32).astype(BF16)
+            back[home * cap:(home + 1) * cap, :] = block
+            chosen = own_place[home:home + 1, :] == iota((cap, count), 0)
             slot_here = jnp.sum(jnp.where(chosen, slot[home:home + 1, :].astype(F32), 0.0), axis=1, keepdims=True)
             slot_here = slot_here.astype(jnp.int32)
-            number = jnp.ones((half, 1), jnp.int32)
-            for sample in range(ends.shape[1]):
-                number += (slot_here >= ends[me[0], sample]).astype(jnp.int32)
-            held[home * half:(home + 1) * half, :] = jnp.broadcast_to(number.astype(F32), (half, held.shape[1])).astype(BF16)
+            number = jnp.ones((cap, 1), jnp.int32)
+            end = 0
+            for sample in range(lengths.shape[1]):
+                end = end + lengths[me[0], sample]
+                number += (slot_here >= end).astype(jnp.int32)
+            held[home * cap:(home + 1) * cap, :] = jnp.broadcast_to(number.astype(F32), (cap, held.shape[1])).astype(BF16)
             start = start + here
-        onehot = ((iota((rows, slots), 0) == lanes + shift) & (lanes < limit)).astype(F32).astype(BF16)
-        packer[...] = onehot
-        samples[first:first + rows, :] = dot(onehot, held[:slots, :])
+        samples[first:first + rows, :] = dot(packer[...], held[:slots, :])
         first += rows
 
 
-def project_kernel(rows_in, kinds, weight, send, *refs):
-    out = refs[-1]
-    rows = rows_in[...]
+def project_kernel(number, kinds, weight, send, *refs):
+    out, held = refs[-2:]
+
+    @pl.when(pl.program_id(0) == 0)
+    def _():
+        at = 0
+        for part in refs[:number]:
+            held[at:at + part.shape[0], :] = part[...]
+            at += part.shape[0]
+
+    rows = held[...]
     product = dot(rows, weight[0])
     if weight.shape[0] == 2:
         product = jnp.where(kinds[:, :1] == 0.0, product, dot(rows, weight[1]))
     out[...] = dot(send[...], product.astype(BF16)).astype(BF16)
 
 
-def project(name, rows_in, kinds, weight, send, after=()):
-    rows, depth = rows_in.shape
+def project(name, parts, kinds, weight, send, after=()):
+    rows = sum(part.shape[0] for part in parts)
+    depth = parts[0].shape[1]
     width = weight.shape[2]
     step = 256 if width % 256 == 0 else width
     slots = send.shape[0]
     return pl.pallas_call(
-        project_kernel,
+        functools.partial(project_kernel, len(parts)),
         grid=(width // step,),
         in_specs=[
-            pl.BlockSpec((rows, depth), lambda i: (0, 0)),
             pl.BlockSpec(kinds.shape, lambda i: (0, 0)),
             pl.BlockSpec((weight.shape[0], depth, step), lambda i: (0, 0, i)),
             pl.BlockSpec(send.shape, lambda i: (0, 0)),
-        ] + [pl.BlockSpec(memory_space=pl.ANY)] * len(after),
+        ] + [pl.BlockSpec(part.shape, lambda i: (0, 0)) for part in parts] + [pl.BlockSpec(memory_space=pl.ANY)] * len(after),
         out_specs=pl.BlockSpec((slots, step), lambda i: (0, i)),
         out_shape=jax.ShapeDtypeStruct((slots, width), BF16),
+        scratch_shapes=[pltpu.VMEM((rows, depth), BF16)],
         compiler_params=params(),
         cost_estimate=pl.CostEstimate(
             flops=2 * rows * weight.size, bytes_accessed=weight.size * 2, transcendentals=0
         ),
         name=name,
-    )(rows_in, kinds, weight, send, *after)
+    )(kinds, weight, send, *parts, *after)
 
 
 def split_dot(value, square):
@@ -325,11 +357,10 @@
     return SMALL_BYTES // (2 * width) // 16 * 16
 
 
-def gather_small(rows):
-    count, width = rows.shape
+def small_pieces(count, width):
     number = -(-count // small_rows(width))
     step = up16(-(-count // number))
-    return jnp.concatenate([gather(rows[at:min(at + step, count)]) for at in range(0, count, step)])
+    return [min(step, count - at) for at in range(0, count, step)]
 
 
 def term_kernel(rows, weight, out):
@@ -349,7 +380,7 @@
         ],
         out_specs=pl.BlockSpec((count, step), lambda i: (0, i)),
         out_shape=jax.ShapeDtypeStruct((count, width), BF16),
-        compiler_params=params(),
+        compiler_params=params(SMALL_LIMIT),
         cost_estimate=pl.CostEstimate(
             flops=2 * count * depth * width, bytes_accessed=2 * depth * width, transcendentals=0
         ),
@@ -376,28 +407,28 @@
     slots = tuple(bags * cap for cap in caps)
     home_rows = part_sizes(count, bags)
     bag_rows = part_sizes(pack, bags)
+    odd_pieces = small_pieces(home_rows[1], width)
     rows = sum(bag_rows)
     vmem = pl.BlockSpec(memory_space=pltpu.VMEM)
     smem = pl.BlockSpec(memory_space=pltpu.SMEM)
-    ends = jnp.cumsum(sample_lengths, axis=1)
 
     own_plan = lax.dynamic_slice_in_dim(row_plan, me * count, count, 0)
     plan_row = own_plan.reshape(1, count)
-    even, odd, order_even, order_odd, where_row, where_col = pl.pallas_call(
+    order_even, order_odd, where_row, where_col, even, *odds = pl.pallas_call(
         functools.partial(order_kernel, bags, pack),
         in_specs=[vmem] * 2,
-        out_specs=[vmem] * 6,
-        out_shape=[jax.ShapeDtypeStruct((size, width), BF16) for size in home_rows]
-        + [jax.ShapeDtypeStruct((size, count), BF16) for size in home_rows]
+        out_specs=[vmem] * (5 + len(odd_pieces)),
+        out_shape=[jax.ShapeDtypeStruct((size, count), BF16) for size in home_rows]
         + [
             jax.ShapeDtypeStruct((1, count), jnp.int32),
             jax.ShapeDtypeStruct((count, 1), jnp.int32),
-        ],
+        ]
+        + [jax.ShapeDtypeStruct((size, width), BF16) for size in (home_rows[0], *odd_pieces)],
         compiler_params=params(),
         name="order",
     )(plan_row, home_tokens)
     full_even = gather(even)
-    full_odd = gather_small(odd)
+    full_odds = [gather(odd) for odd in odds]
     send_even, send_odd, kind_even, kind_odd, final_even, final_odd = pl.pallas_call(
         functools.partial(send_kernel, bags, pack, caps),
         in_specs=[smem, smem] + [vmem] * 5,
@@ -407,33 +438,43 @@
         + [jax.ShapeDtypeStruct((count, size), BF16) for size in slots],
         compiler_params=params(),
         name="send_plan",
-    )(ends, modality, plan_row, where_row, where_col, order_even, order_odd)
-    pack_even, pack_odd, back_even, back_odd, samples = pl.pallas_call(
+    )(sample_lengths, modality, plan_row, where_row, where_col, order_even, order_odd)
+    home = me.reshape(1).astype(jnp.int32)
+    plan = row_plan.reshape(bags, count)
+    pack_even, pack_odd = pl.pallas_call(
+        functools.partial(pack_plan_kernel, pack, caps),
+        in_specs=[smem, vmem],
+        out_specs=[vmem] * 2,
+        out_shape=[jax.ShapeDtypeStruct(shape, BF16) for shape in zip(bag_rows, slots)],
+        compiler_params=params(),
+        name="pack_plan",
+    )(home, plan)
+    back_even, back_odd, samples = pl.pallas_call(
         functools.partial(bag_kernel, pack, caps),
-        in_specs=[smem, smem, vmem],
-        out_specs=[vmem] * 5,
-        out_shape=[jax.ShapeDtypeStruct(shape, BF16) for shape in zip(bag_rows, slots)]
-        + [jax.ShapeDtypeStruct(shape, BF16) for shape in zip(slots, bag_rows)]
+        in_specs=[smem, smem] + [vmem] * 3,
+        out_specs=[vmem] * 3,
+        out_shape=[jax.ShapeDtypeStruct(shape, BF16) for shape in zip(slots, bag_rows)]
         + [jax.ShapeDtypeStruct((rows, 128), F32)],
         scratch_shapes=[pltpu.VMEM((max(slots), 128), BF16)],
         compiler_params=params(),
         name="bag_plan",
-    )(me.reshape(1).astype(jnp.int32), ends, row_plan.reshape(bags, count))
+    )(home, sample_lengths, plan, pack_even, pack_odd)
     sample_row = samples[:, 0].reshape(1, rows)
 
     def exchange(outgoing):
         arrived = lax.all_to_all(outgoing.reshape(bags, -1, width), "dp", split_axis=0, concat_axis=0, tiled=True)
         return arrived.reshape(-1, width)
 
-    outgoing_odd = project("project", full_odd, kind_odd, mod_weight, send_odd)
+    outgoing_odd = project("project", full_odds, kind_odd, mod_weight, send_odd)
     arrived_odd = exchange(outgoing_odd)
-    outgoing_even = project("project", full_even, kind_even, mod_weight, send_even, [outgoing_odd])
+    outgoing_even = project("project", [full_even], kind_even, mod_weight, send_even, [outgoing_odd])
     arrived_even = exchange(outgoing_even)
-    bag_odd = gather(move_rows("pack", pack_odd, arrived_odd, [outgoing_even]))
-    packed_even = move_rows("pack", pack_even, arrived_even, [])
+    packed_odd, = move_rows("pack", pack_odd, arrived_odd, bag_rows[1:], [outgoing_even])
+    bag_odd = gather(packed_odd)
     small = small_rows(width)
-    bag_late = gather(packed_even[small:])
-    bag_early = gather(packed_even[:small])
+    packed_early, packed_late = move_rows("pack", pack_even, arrived_even, (small, bag_rows[0] - small))
+    bag_late = gather(packed_late)
+    bag_early = gather(packed_early)
     every = (0, 1, 2)
     odd = make_qkv(bag_odd, qkv_weight, norm_gain, every)
     early = make_qkv(bag_early, qkv_weight, norm_gain, every)

time: 318 us -> 310 us (0.975)
  waiting for transfers between devices: 84 us -> 78.5 us
  local copies, waits for them, and re-layouts: 9.88 us -> 14.8 us
    unnamed x16 -> x28, local copies, waits for them, and re-layouts: 2.94 us -> 7.97 us
    pallas_call x2, Pallas kernels: 13.3 us -> 8.55 us  [terms(): pl.pallas_call(term_kernel, grid=(width // step,), in_specs=[pl.BlockSpec...]
    all_gather x3, waiting for transfers between devices: 11.4 us -> 7.75 us  [gather(): return lax.all_gather(rows, 'bag', axis=1, tiled=True)]
    pallas_call x4 -> x5, Pallas kernels: 20.7 us -> 23 us  [the longest x2 15.9 us: project(): pl.pallas_call(functools.partial(project_kernel, len(parts)), grid=(width...]
where the time goes in v4:
time: 310 us; the launch traced here: 309 us
  blocking collectives  94 us (30%)
  Pallas kernels  88.8 us (29%)
  waiting for transfers between devices  78.5 us (25%)
  local copies, waits for them, and re-layouts  14.8 us (5%)
  between operations  13.2 us (4%)
  starting transfers between devices  11.2 us (4%)
  matrix products  8.19 us (3%)
    all_gather x3, blocking collectives, gather(): return lax.all_gather(rows, 'bag', axis=1, tiled=True)  75.3 us
    reduce_scatter x2, waiting for transfers between devices, to_home(): lax.psum_scatter(terms(rows, output_weight), 'bag', scatter_dimension=1,...  62.2 us
    pallas_call x3, Pallas kernels, make_qkv(): pl.pallas_call(functools.partial(qkv_kernel, which), grid=(width // step,...  29.6 us
    all_to_all x1, blocking collectives, exchange(): lax.all_to_all(outgoing.reshape(bags, -1, width), 'dp', split_axis=0, con...  18.7 us
    pallas_call x2, Pallas kernels, attend(): pl.pallas_call(functools.partial(attend_kernel, (len(queries), len(keys))...  17.3 us
    pallas_call x2, Pallas kernels, project(): pl.pallas_call(functools.partial(project_kernel, len(parts)), grid=(width...  15.9 us
    all_to_all x3, starting transfers between devices, exchange(): lax.all_to_all(outgoing.reshape(bags, -1, width), 'dp', split_axis=0, con...  11 us
    pallas_call x2, Pallas kernels, terms(): pl.pallas_call(term_kernel, grid=(width // step,), in_specs=[pl.BlockSpec...  8.55 us
  transfers between devices with their start and end apart: 8, of which 4 were waited for; matrix products, arithmetic and copies ran while one was open for 5% of the time, Pallas kernels for 19%

profile of v4, /device:TPU:0, one launch (start us, length us, event | category | flops | bytes accessed | tf_op | source)
XLA Modules:
  0.0 308.7 jit_solution(14824303047771728757)
XLA Ops:
  6.5 0.0 all-gather.4.cloned.1.call-start
  6.5 1.3 dynamic_slice.3
  7.9 3.4 %order.1 = (bf16[336,512]{1,0:T(8,128)(2,1)}, bf16[192,512]{1,0:T(8,128)(2,1)}, s32[1,512]{1,0:T(1,128)}, s32[512,1]{1,0:T(8,128)}, bf16[336,768]{1,0:T(8,128)(2...) custom-call(s32[1,512]{1,0:T(1,128)} %bitcast.32, bf16[512,768]{1,0:T(8,128)(2,1)} %tokens.1), custom_call_target="tpu_custom_call" | custom-call | tf_op jit(solution)/shard_map/order/pallas_call | solution.py:417
  11.3 0.0 all-gather.4.cloned.1.call-update
  11.4 1.4 copy.12.lengths
  12.7 1.3 copy.13.modality
  14.1 3.3 %send_plan.1 = (bf16[640,336]{1,0:T(8,128)(2,1)}, bf16[384,192]{1,0:T(8,128)(2,1)}, f32[336,128]{1,0:T(8,128)}, f32[192,128]{1,0:T(8,128)}, bf16[512,640]{1,0:T(8,128)(2,1)}, /*index=5*/bf16[512,384]{1,0:T(8,128)(2,1)}) custom-call(s32[8,4]{1,0:T(8,128)} %copy.12.lengths, s32[8,4]{1,0:T(8,128)} %copy.13.modality, s32[1,512]{1,0:T(1,128)} %bitcast.33, ...), custom_call_target="tpu_custom_call" | custom-call | tf_op jit(solution)/shard_map/send_plan/pallas_call | solution.py:432
  17.4 26.6 %all_gather.19.refs_0_ = bf16[96,3072]{1,0:T(8,128)(2,1)} all-gather(bf16[96,768]{1,0:T(8,128)(2,1)} %get-tuple-element.48), channel_id=1, replica_groups=mesh['dp'=8,'bag'=4] {'bag'}, dimensions={1}, use_global_device_ids=true | all-gather | bytes 737280 | tf_op jit(solution)/shard_map/all_gather | solution.py:353
  44.0 0.0 copy-done.8
  44.0 24.4 %all_gather.20.refs_1_ = bf16[96,3072]{1,0:T(8,128)(2,1)} all-gather(bf16[96,768]{1,0:T(8,128)(2,1)S(1)} %copy-done.8), channel_id=1, replica_groups=mesh['dp'=8,'bag'=4] {'bag'}, dimensions={1}, use_global_device_ids=true | all-gather | bytes 737280 | tf_op jit(solution)/shard_map/all_gather | solution.py:353
  68.4 7.2 %project.2.refs_1_ = bf16[384,768]{1,0:T(8,128)(2,1)} custom-call(f32[192,128]{1,0:T(8,128)} %get-tuple-element.46.kinds, bf16[2,3072,768]{2,1,0:T(8,128)(2,1)} %weight.5, bf16[384,192]{1,0:T(8,128)(2,1)} %get-tuple-element.47.send, bf16[96,3072]{1,0:T(8,128)(2,1)} %all_gather.19.refs_0_, bf16[96,3072]{1,0:T(8,128)(2,1)} %all_gather.20.refs_1_), custom_call_target="tpu_custom_call" | custom-call | flops 1811939328 | bytes 9437184 | tf_op jit(solution)/shard_map/project/pallas_call | solution.py:223
  75.6 3.6 %all-to-all-start.1 = ((bf16[8,48,768]{2,1,0:T(8,128)(2,1)}), bf16[8,48,768]{2,1,0:T(8,128)(2,1)S(1)}, u32[]{:S(2)}, u32[]{:S(2)}) async-start(bf16[8,48,768]{2,1,0:T(8,128)(2,1)} %bitcast.24), calls=%async_computation.1 | async-start | bytes 1179648 | tf_op jit(solution)/shard_map/all_to_all | solution.py:465
  79.2 0.0 all-gather.8.cloned.1.call-start
  79.2 0.0 copy-done.9
  79.2 0.6 reshape.40.plan
  79.8 2.0 pack_plan.1
  81.8 8.7 %project.3.refs_0_ = bf16[640,768]{1,0:T(8,128)(2,1)} custom-call(f32[336,128]{1,0:T(8,128)} %get-tuple-element.43.kinds, bf16[2,3072,768]{2,1,0:T(8,128)(2,1)} %weight.5, bf16[640,336]{1,0:T(8,128)(2,1)} %get-tuple-element.44.send, bf16[336,3072]{1,0:T(8,128)(2,1)} %all-gather.4.cloned.1.call-done.refs_0_, bf16[384,768]{1,0:T(8,128)(2,1)} %project.2.refs_1_), custom_call_target="tpu_custom_call" | custom-call | flops 3170893824 | bytes 9437184 | tf_op jit(solution)/shard_map/project/pallas_call | solution.py:223
  90.5 0.0 all-to-all-done.1
  90.5 0.8 copy-done.4
  91.4 2.3 pack.3
  93.6 0.0 all-gather.8.cloned.1.call-update
  93.7 0.0 all-gather.6.cloned.1.call-start
  93.7 0.0 copy-done.3
  93.7 18.7 %all_to_all.20 = bf16[8,80,768]{2,1,0:T(8,128)(2,1)} all-to-all(bf16[8,80,768]{2,1,0:T(8,128)(2,1)S(1)} %bitcast.23), channel_id=1, replica_groups=mesh['dp'=8,'bag'=4] {'dp'}, dimensions={0} | all-to-all | bytes 1966080 | tf_op jit(solution)/shard_map/all_to_all | solution.py:465
  112.4 2.8 pack.2
  115.2 0.0 all-gather.6.cloned.1.call-update
  115.3 0.0 reduce-scatter.3.cloned.1.call-start
  115.3 3.6 %bag_plan.1 = (bf16[640,416]{1,0:T(8,128)(2,1)}, bf16[384,240]{1,0:T(8,128)(2,1)}, f32[656,128]{1,0:T(8,128)}) custom-call(s32[1]{0:T(128)} %bitcast.1.me, s32[8,4]{1,0:T(8,128)} %copy.12.lengths, s32[8,512]{1,0:T(8,128)} %reshape.40.plan, bf16[416,640]{1,0:T(8,128)(2,1)} %get-tuple-element.39.pack_even.onehot, ...), custom_call_target="tpu_custom_call" | custom-call | tf_op jit(solution)/shard_map/bag_plan/pallas_call | solution.py:452
  118.9 1.6 slice.9.sample_col
  120.6 1.1 slice_reduce_fusion
  121.7 0.6 reshape_squeeze.3.sample_row
  122.3 0.0 copy-done.6
  122.3 24.2 %all_gather.21.rows_in = bf16[160,3072]{1,0:T(8,128)(2,1)} all-gather(bf16[160,768]{1,0:T(8,128)(2,1)S(1)} %copy-done.6), channel_id=1, replica_groups=mesh['dp'=8,'bag'=4] {'bag'}, dimensions={1}, use_global_device_ids=true | all-gather | bytes 1228800 | tf_op jit(solution)/shard_map/all_gather | solution.py:353
  146.5 9.0 %qkv.3 = (bf16[160,768]{1,0:T(8,128)(2,1)}, bf16[160,768]{1,0:T(8,128)(2,1)}, bf16[160,768]{1,0:T(8,128)(2,1)}) custom-call(bf16[160,3072]{1,0:T(8,128)(2,1)} %all_gather.21.rows_in, f32[3,2,256]{2,1,0:T(2,128)} %bitcast.29, bf16[3,3072,768]{2,1,0:T(8,128)(2,1)} %refs_2_.5, bf16[3,3072,768]{2,1,0:T(8,128)(2,1)} %refs_2_.5, bf16[3,3072,768]{2,1,0:T(8,128)(2,1)} %refs_2_.5), custom_call_target="tpu_custom_call" | custom-call | flops 2264924160 | bytes 14155776 | tf_op jit(solution)/shard_map/qkv/pallas_call | solution.py:271
  155.5 10.2 %qkv.4 = (bf16[240,768]{1,0:T(8,128)(2,1)}, bf16[240,768]{1,0:T(8,128)(2,1)}, bf16[240,768]{1,0:T(8,128)(2,1)}) custom-call(bf16[240,3072]{1,0:T(8,128)(2,1)} %all-gather.8.cloned.1.call-done.rows_in, f32[3,2,256]{2,1,0:T(2,128)} %bitcast.30, bf16[3,3072,768]{2,1,0:T(8,128)(2,1)} %refs_2_.5, bf16[3,3072,768]{2,1,0:T(8,128)(2,1)} %refs_2_.5, ...), custom_call_target="tpu_custom_call" | custom-call | flops 3397386240 | bytes 14155776 | tf_op jit(solution)/shard_map/qkv/pallas_call | solution.py:271
  165.7 7.7 %all-gather.6.cloned.1.call-done.rows_in = bf16[256,3072]{1,0:T(8,128)(2,1)} async-done(((bf16[256,768]{1,0:T(8,128)(2,1)}), bf16[256,3072]{1,0:T(8,128)(2,1)}) %all-gather.6.cloned.1.call-update) | async-done | bytes 1572880 | tf_op jit(solution)/shard_map/all_gather | solution.py:353
  173.5 10.4 %qkv.5 = (bf16[256,768]{1,0:T(8,128)(2,1)}, bf16[256,768]{1,0:T(8,128)(2,1)}, bf16[256,768]{1,0:T(8,128)(2,1)}) custom-call(bf16[256,3072]{1,0:T(8,128)(2,1)} %all-gather.6.cloned.1.call-done.rows_in, f32[3,2,256]{2,1,0:T(2,128)} %bitcast.31, bf16[3,3072,768]{2,1,0:T(8,128)(2,1)} %refs_2_.5, bf16[3,3072,768]{2,1,0:T(8,128)(2,1)} %refs_2_.5, ...), custom_call_target="tpu_custom_call" | custom-call | flops 3623878656 | bytes 14155776 | tf_op jit(solution)/shard_map/qkv/pallas_call | solution.py:271
  183.8 9.0 %attend.2.rows.refs_7_ = bf16[416,768]{1,0:T(8,128)(2,1)} custom-call(f32[416,128]{1,0:T(8,128)} %slice.9.sample_col, f32[1,656]{1,0:T(1,128)} %reshape_squeeze.3.sample_row, bf16[160,768]{1,0:T(8,128)(2,1)} %get-tuple-element.51.refs_4_.refs_0_, bf16[256,768]{1,0:T(8,128)(2,1)} %get-tuple-element.54.refs_1_, ...), custom_call_target="tpu_custom_call" | custom-call | flops 1676673024 | bytes 4030464 | tf_op jit(solution)/shard_map/attend/pallas_call | solution.py:328
  192.9 0.0 slice-done
  192.9 0.0 slice-done.1
  192.9 0.0 copy-start.1
  192.9 1.1 copy-done.1
  194.0 4.7 %terms.2 = bf16[416,3072]{1,0:T(8,128)(2,1)} custom-call(bf16[416,768]{1,0:T(8,128)(2,1)S(1)} %copy-done.1, bf16[768,3072]{1,0:T(8,128)(2,1)S(1)} %bitcast.22), custom_call_target="tpu_custom_call" | custom-call | flops 1962934272 | bytes 4718592 | tf_op jit(solution)/shard_map/terms/pallas_call | solution.py:374
  198.7 0.0 reduce-scatter.3.cloned.1.call-update
  198.7 0.0 reduce-scatter.5.cloned.1.call-start
  198.8 1.6 slice.11.sample_col
  200.3 8.3 %attend.3.rows = bf16[240,768]{1,0:T(8,128)(2,1)} custom-call(f32[240,128]{1,0:T(8,128)} %slice.11.sample_col, f32[1,656]{1,0:T(1,128)} %reshape_squeeze.3.sample_row, bf16[240,768]{1,0:T(8,128)(2,1)} %get-tuple-element.53.refs_3_.refs_0_, bf16[160,768]{1,0:T(8,128)(2,1)} %get-tuple-element.55.refs_2_.refs_1_, ...), custom_call_target="tpu_custom_call" | custom-call | flops 967311360 | bytes 4030464 | tf_op jit(solution)/shard_map/attend/pallas_call | solution.py:328
  208.6 2.3 copy-done
  211.0 1.0 copy-done.2
  211.9 3.9 %terms.3 = bf16[240,3072]{1,0:T(8,128)(2,1)} custom-call(bf16[240,768]{1,0:T(8,128)(2,1)S(1)} %copy-done.2, bf16[768,3072]{1,0:T(8,128)(2,1)S(1)} %copy-done), custom_call_target="tpu_custom_call" | custom-call | flops 1132462080 | bytes 4718592 | tf_op jit(solution)/shard_map/terms/pallas_call | solution.py:374
  215.8 0.0 reduce-scatter.5.cloned.1.call-update
  215.8 33.0 %reduce-scatter.3.cloned.1.call-done = bf16[416,768]{1,0:T(8,128)(2,1)} async-done(((bf16[416,3072]{1,0:T(8,128)(2,1)}), bf16[416,768]{1,0:T(8,128)(2,1)}) %reduce-scatter.3.cloned.1.call-update) | async-done | bytes 638992 | tf_op jit(solution)/shard_map/reduce_scatter | solution.py:486
  248.8 0.0 copy-done.10
  248.8 2.7 convolution_convert_fusion
  251.5 3.8 %all-to-all-start.2 = ((bf16[8,80,768]{2,1,0:T(8,128)(2,1)}), bf16[8,80,768]{2,1,0:T(8,128)(2,1)S(1)}, u32[]{:S(2)}, u32[]{:S(2)}) async-start(bf16[8,80,768]{2,1,0:T(8,128)(2,1)} %bitcast.9), calls=%async_computation.3 | async-start | bytes 1966080 | tf_op jit(solution)/shard_map/all_to_all | solution.py:465
  255.3 29.2 %reduce-scatter.5.cloned.1.call-done = bf16[240,768]{1,0:T(8,128)(2,1)} async-done(((bf16[240,3072]{1,0:T(8,128)(2,1)}), bf16[240,768]{1,0:T(8,128)(2,1)}) %reduce-scatter.5.cloned.1.call-update) | async-done | bytes 368656 | tf_op jit(solution)/shard_map/reduce_scatter | solution.py:486
  284.5 0.0 copy-done.7
  284.5 2.1 convolution_convert_fusion.1
  286.6 0.0 all-to-all-done.2
  286.6 3.7 %all-to-all-start.3 = ((bf16[8,48,768]{2,1,0:T(8,128)(2,1)}), bf16[8,48,768]{2,1,0:T(8,128)(2,1)S(1)}, u32[]{:S(2)}, u32[]{:S(2)}) async-start(bf16[8,48,768]{2,1,0:T(8,128)(2,1)} %bitcast.11), calls=%async_computation.5 | async-start | bytes 1179648 | tf_op jit(solution)/shard_map/all_to_all | solution.py:465
  290.3 1.9 fusion
  292.2 8.5 %all-to-all-done.3 = bf16[8,48,768]{2,1,0:T(8,128)(2,1)S(1)} async-done(((bf16[8,48,768]{2,1,0:T(8,128)(2,1)}), bf16[8,48,768]{2,1,0:T(8,128)(2,1)S(1)}, u32[]{:S(2)}, u32[]{:S(2)}) %all-to-all-start.3) | async-done | bytes 589856 | tf_op jit(solution)/shard_map/all_to_all | solution.py:465
  300.7 0.0 copy-done.5
  300.7 1.5 add_convert_fusion
  (15 shorter events, 0.0 us)
Async XLA Ops:
  6.5 75.3 %all-gather.4.cloned.1.call-start = ((), (), s32[]{:S(2)}) async-start(), calls=%async_computation.6 | async-start | bytes 2580480 | tf_op jit(solution)/shard_map/all_gather | solution.py:353
  11.3 32.7 %copy-start.8 = (bf16[96,768]{1,0:T(8,128)(2,1)S(1)}, bf16[96,768]{1,0:T(8,128)(2,1)}, u32[]{:S(2)}) copy-start(bf16[96,768]{1,0:T(8,128)(2,1)} %get-tuple-element.49) | copy-start | bytes 442372
  68.4 10.8 %copy-start.9 = (s32[4096]{0:T(1024)S(1)}, s32[4096]{0:T(1024)}, u32[]{:S(2)}) copy-start(s32[4096]{0:T(1024)} %param.13) | copy-start | bytes 49156
  75.6 14.9 %all-to-all-start.1 = ((bf16[8,48,768]{2,1,0:T(8,128)(2,1)}), bf16[8,48,768]{2,1,0:T(8,128)(2,1)S(1)}, u32[]{:S(2)}, u32[]{:S(2)}) async-start(bf16[8,48,768]{2,1,0:T(8,128)(2,1)} %bitcast.24), calls=%async_computation.1 | async-start | bytes 1179648 | tf_op jit(solution)/shard_map/all_to_all | solution.py:465
  79.2 76.3 %all-gather.8.cloned.1.call-start = ((), (), s32[]{:S(2)}) async-start(), calls=%async_computation.8 | async-start | bytes 1843200 | tf_op jit(solution)/shard_map/all_gather | solution.py:353
  90.5 3.2 %copy-start.3 = (bf16[640,768]{1,0:T(8,128)(2,1)S(1)}, bf16[640,768]{1,0:T(8,128)(2,1)}, u32[]{:S(2)}) copy-start(bf16[640,768]{1,0:T(8,128)(2,1)} %project.3.refs_0_) | copy-start | bytes 2949124
  90.5 0.8 copy-start.4
  93.7 79.8 %all-gather.6.cloned.1.call-start = ((), (), s32[]{:S(2)}) async-start(), calls=%async_computation.7 | async-start | bytes 1966080 | tf_op jit(solution)/shard_map/all_gather | solution.py:353
  115.2 7.0 %copy-start.6 = (bf16[160,768]{1,0:T(8,128)(2,1)S(1)}, bf16[160,768]{1,0:T(8,128)(2,1)}, u32[]{:S(2)}) copy-start(bf16[160,768]{1,0:T(8,128)(2,1)} %get-tuple-element.50) | copy-start | bytes 737284
  115.3 133.5 %reduce-scatter.3.cloned.1.call-start = ((), (), s32[]{:S(2)}) async-start(), calls=%async_computation.9 | async-start | bytes 3194880 | tf_op jit(solution)/shard_map/reduce_scatter | solution.py:486
  155.5 37.4 %slice-start = ((s8[4718592]{0:T(1024)(128)(4,1)}), s8[524288]{0:T(1024)(128)(4,1)S(1)}, s32[]{:S(2)}) async-start(s8[4718592]{0:T(1024)(128)(4,1)} %bitcast.21), calls=%async_computation.11 | async-start | bytes 1048576
  173.5 19.4 %slice-start.1 = ((s8[4718592]{0:T(1024)(128)(4,1)}), s8[4194304]{0:T(1024)(128)(4,1)S(1)}, s32[]{:S(2)}) async-start(s8[4718592]{0:T(1024)(128)(4,1)} %bitcast.21), calls=%async_computation.12 | async-start | bytes 8388608
  192.9 1.1 copy-start.1
  198.7 85.8 %reduce-scatter.5.cloned.1.call-start = ((), (), s32[]{:S(2)}) async-start(), calls=%async_computation.10 | async-start | bytes 1843200 | tf_op jit(solution)/shard_map/reduce_scatter | solution.py:486
  208.6 2.3 copy-start
  211.0 1.0 copy-start.2
  211.9 36.9 %copy-start.10 = (bf16[640,416]{1,0:T(8,128)(2,1)S(1)}, bf16[640,416]{1,0:T(8,128)(2,1)}, u32[]{:S(2)}) copy-start(bf16[640,416]{1,0:T(8,128)(2,1)} %get-tuple-element.41) | copy-start | bytes 1597444
  251.5 33.0 %copy-start.7 = (bf16[384,240]{1,0:T(8,128)(2,1)S(1)}, bf16[384,240]{1,0:T(8,128)(2,1)}, u32[]{:S(2)}) copy-start(bf16[384,240]{1,0:T(8,128)(2,1)} %get-tuple-element.62) | copy-start | bytes 552964
  251.5 35.1 %all-to-all-start.2 = ((bf16[8,80,768]{2,1,0:T(8,128)(2,1)}), bf16[8,80,768]{2,1,0:T(8,128)(2,1)S(1)}, u32[]{:S(2)}, u32[]{:S(2)}) async-start(bf16[8,80,768]{2,1,0:T(8,128)(2,1)} %bitcast.9), calls=%async_computation.3 | async-start | bytes 1966080 | tf_op jit(solution)/shard_map/all_to_all | solution.py:465
  286.6 14.1 %all-to-all-start.3 = ((bf16[8,48,768]{2,1,0:T(8,128)(2,1)}), bf16[8,48,768]{2,1,0:T(8,128)(2,1)S(1)}, u32[]{:S(2)}, u32[]{:S(2)}) async-start(bf16[8,48,768]{2,1,0:T(8,128)(2,1)} %bitcast.11), calls=%async_computation.5 | async-start | bytes 1179648 | tf_op jit(solution)/shard_map/all_to_all | solution.py:465
  290.3 10.4 %copy-start.5 = (bf16[512,384]{1,0:T(8,128)(2,1)S(1)}, bf16[512,384]{1,0:T(8,128)(2,1)}, u32[]{:S(2)}) copy-start(bf16[512,384]{1,0:T(8,128)(2,1)} %get-tuple-element.61) | copy-start | bytes 1179652
Sparse Core Ops, SparseCore 0:
  11.5 65.6 all-gather.3
  93.8 39.8 all-gather.7
  135.3 38.1 all-gather.5
  198.8 49.9 reduce-scatter.2
  251.1 33.3 reduce-scatter.4

commit v5 on v4

--- a/solution.py
+++ b/solution.py
@@ -9,8 +9,8 @@
 
 HD = 64
 EPSILON = 1e-06
-PERIOD = 8
-FIRST = 5
+PERIOD = 10
+FIRST = 7
 SMALL_BYTES = 240 * 1024
 VMEM_LIMIT = 56 * 1024 * 1024
 SMALL_LIMIT = 24 * 1024 * 1024
@@ -231,7 +231,7 @@
         out_specs=pl.BlockSpec((slots, step), lambda i: (0, i)),
         out_shape=jax.ShapeDtypeStruct((slots, width), BF16),
         scratch_shapes=[pltpu.VMEM((rows, depth), BF16)],
-        compiler_params=params(),
+        compiler_params=params(SMALL_LIMIT),
         cost_estimate=pl.CostEstimate(
             flops=2 * rows * weight.size, bytes_accessed=weight.size * 2, transcendentals=0
         ),
@@ -278,7 +278,7 @@
         + [pl.BlockSpec(memory_space=pl.ANY)] * len(after),
         out_specs=[part] * len(which),
         out_shape=[shape] * len(which),
-        compiler_params=params(),
+        compiler_params=params(SMALL_LIMIT),
         cost_estimate=pl.CostEstimate(
             flops=2 * len(which) * rows * depth * width,
             bytes_accessed=2 * len(which) * depth * width,
@@ -403,7 +403,8 @@
     count, width = home_tokens.shape
     pack = count + count // 4
     capacity = 2 * count // bags
-    caps = (capacity // PERIOD * FIRST, capacity // PERIOD * (PERIOD - FIRST))
+    cycles = -(-capacity // PERIOD)
+    caps = (up16(cycles * FIRST), up16(cycles * (PERIOD - FIRST)))
     slots = tuple(bags * cap for cap in caps)
     home_rows = part_sizes(count, bags)
     bag_rows = part_sizes(pack, bags)
@@ -469,14 +470,14 @@
     arrived_odd = exchange(outgoing_odd)
     outgoing_even = project("project", [full_even], kind_even, mod_weight, send_even, [outgoing_odd])
     arrived_even = exchange(outgoing_even)
-    packed_odd, = move_rows("pack", pack_odd, arrived_odd, bag_rows[1:], [outgoing_even])
+    packed_odd, = move_rows("pack", pack_odd, arrived_odd, bag_rows[1:])
     bag_odd = gather(packed_odd)
     small = small_rows(width)
-    packed_early, packed_late = move_rows("pack", pack_even, arrived_even, (small, bag_rows[0] - small))
+    packed_early, packed_late = move_rows("pack", pack_even, arrived_even, (small, bag_rows[0] - small), [samples])
     bag_late = gather(packed_late)
     bag_early = gather(packed_early)
     every = (0, 1, 2)
-    odd = make_qkv(bag_odd, qkv_weight, norm_gain, every)
+    odd = make_qkv(bag_odd, qkv_weight, norm_gain, every, [bag_early])
     early = make_qkv(bag_early, qkv_weight, norm_gain, every)
     late = make_qkv(bag_late, qkv_weight, norm_gain, every, [odd[0], early[0]])
     keys = early[1], late[1], odd[1]

time: 310 us -> 329 us (1.061)
  local copies, waits for them, and re-layouts: 14.8 us -> 47.4 us
  blocking collectives: 94 us -> 71.4 us
  waiting for transfers between devices: 78.5 us -> 97.5 us
  Pallas kernels: 88.8 us -> 73.4 us
  starting transfers between devices: 11.2 us -> 14.9 us
    unnamed x28 -> x70, local copies, waits for them, and re-layouts: 7.97 us -> 43.3 us
    all_to_all x3 -> x4, waiting for transfers between devices: 8.53 us -> 29.1 us  [exchange(): lax.all_to_all(outgoing.reshape(bags, -1, width), 'dp', split_axis=0, con...]
    all_to_all x1 -> x0, blocking collectives: 18.7 us -> none  [exchange(): lax.all_to_all(outgoing.reshape(bags, -1, width), 'dp', split_axis=0, con...]
    pallas_call x3, Pallas kernels: 29.6 us -> 17.9 us  [make_qkv(): pl.pallas_call(functools.partial(qkv_kernel, which), grid=(width // step,...]
    all_gather x3, waiting for transfers between devices: 7.75 us -> 0.02 us  [gather(): return lax.all_gather(rows, 'bag', axis=1, tiled=True)]
    reduce_scatter x2, waiting for transfers between devices: 62.2 us -> 68.4 us  [to_home(): lax.psum_scatter(terms(rows, output_weight), 'bag', scatter_dimension=1,...]
    pallas_call x2, Pallas kernels: 15.9 us -> 10.7 us  [project(): pl.pallas_call(functools.partial(project_kernel, len(parts)), grid=(width...]
    all_gather x3 -> x2, blocking collectives: 75.3 us -> 71.4 us  [gather(): return lax.all_gather(rows, 'bag', axis=1, tiled=True)]
  transfers between devices with their start and end apart: 8 -> 9, of which waited for: 4 -> 5; matrix products, arithmetic and copies ran while one was open for 5% -> 4% of each run, Pallas kernels for 19% -> 14%
where the time goes in v5:
time: 329 us; the launch traced here: 327 us
  waiting for transfers between devices  97.5 us (30%)
  Pallas kernels  73.4 us (22%)
  blocking collectives  71.4 us (22%)
  local copies, waits for them, and re-layouts  47.4 us (14%)
  starting transfers between devices  14.9 us (5%)
  between operations  13.3 us (4%)
  matrix products  9.41 us (3%)
    all_gather x2, blocking collectives, gather(): return lax.all_gather(rows, 'bag', axis=1, tiled=True)  71.4 us
    reduce_scatter x2, waiting for transfers between devices, to_home(): lax.psum_scatter(terms(rows, output_weight), 'bag', scatter_dimension=1,...  68.4 us
    unnamed x70, local copies, waits for them, and re-layouts  43.3 us
    all_to_all x4, waiting for transfers between devices, exchange(): lax.all_to_all(outgoing.reshape(bags, -1, width), 'dp', split_axis=0, con...  29.1 us
    pallas_call x3, Pallas kernels, make_qkv(): pl.pallas_call(functools.partial(qkv_kernel, which), grid=(width // step,...  17.9 us
    pallas_call x2, Pallas kernels, attend(): pl.pallas_call(functools.partial(attend_kernel, (len(queries), len(keys))...  17.9 us
    all_to_all x4, starting transfers between devices, exchange(): lax.all_to_all(outgoing.reshape(bags, -1, width), 'dp', split_axis=0, con...  14.8 us
    pallas_call x2, Pallas kernels, project(): pl.pallas_call(functools.partial(project_kernel, len(parts)), grid=(width...  10.7 us
  transfers between devices with their start and end apart: 9, of which 5 were waited for; matrix products, arithmetic and copies ran while one was open for 4% of the time, Pallas kernels for 14%

profile of v5, /device:TPU:0, one launch (start us, length us, event | category | flops | bytes accessed | tf_op | source)
XLA Modules:
  0.0 327.4 jit_solution(10892526133128931642)
XLA Ops:
  6.5 1.3 dynamic_slice.3
  7.9 3.6 %order.1 = (bf16[384,512]{1,0:T(8,128)(2,1)}, bf16[160,512]{1,0:T(8,128)(2,1)}, s32[1,512]{1,0:T(1,128)}, s32[512,1]{1,0:T(8,128)}, bf16[384,768]{1,0:T(8,128)(2,1)}, /*index=5*/bf16[160,768]{1,0:T(8,128)(2,1)}) custom-call(s32[1,512]{1,0:T(1,128)} %bitcast.30, bf16[512,768]{1,0:T(8,128)(2,1)} %tokens.1), custom_call_target="tpu_custom_call" | custom-call | tf_op jit(solution)/shard_map/order/pallas_call | solution.py:418
  11.5 1.4 copy.12.lengths
  12.9 1.3 copy.13.modality
  14.2 3.5 %send_plan.1 = (bf16[768,384]{1,0:T(8,128)(2,1)}, bf16[384,160]{1,0:T(8,128)(2,1)}, f32[384,128]{1,0:T(8,128)}, f32[160,128]{1,0:T(8,128)}, bf16[512,768]{1,0:T(8,128)(2,1)}, /*index=5*/bf16[512,384]{1,0:T(8,128)(2,1)}) custom-call(s32[8,4]{1,0:T(8,128)} %copy.12.lengths, s32[8,4]{1,0:T(8,128)} %copy.13.modality, s32[1,512]{1,0:T(1,128)} %bitcast.31, ...), custom_call_target="tpu_custom_call" | custom-call | tf_op jit(solution)/shard_map/send_plan/pallas_call | solution.py:433
  17.7 37.8 %all_gather.16.refs_0_ = bf16[160,3072]{1,0:T(8,128)(2,1)S(1)} all-gather(bf16[160,768]{1,0:T(8,128)(2,1)S(1)} %copy-done.28), channel_id=1, replica_groups=mesh['dp'=8,'bag'=4] {'bag'}, dimensions={1}, use_global_device_ids=true | all-gather | bytes 1228800 | tf_op jit(solution)/shard_map/all_gather | solution.py:353
  55.6 3.7 %copy-done.3 = bf16[2,3072,768]{2,1,0:T(8,128)(2,1)S(1)} copy-done((bf16[2,3072,768]{2,1,0:T(8,128)(2,1)S(1)}, bf16[2,3072,768]{2,1,0:T(8,128)(2,1)}, u32[]{:S(2)}) %copy-start.3) | copy-done | bytes 9437208
  59.3 0.9 copy-done.21
  60.2 0.9 copy-done.22
  61.1 4.0 %project.2.refs_1_ = bf16[384,768]{1,0:T(8,128)(2,1)} custom-call(f32[160,128]{1,0:T(8,128)S(1)} %copy-done.22, bf16[2,3072,768]{2,1,0:T(8,128)(2,1)S(1)} %copy-done.3, bf16[384,160]{1,0:T(8,128)(2,1)S(1)} %copy-done.21, bf16[160,3072]{1,0:T(8,128)(2,1)S(1)} %all_gather.16.refs_0_), custom_call_target="tpu_custom_call" | custom-call | flops 1509949440 | bytes 9437184 | tf_op jit(solution)/shard_map/project/pallas_call | solution.py:223
  65.1 3.8 %all-to-all-start.1 = ((bf16[8,48,768]{2,1,0:T(8,128)(2,1)}), bf16[8,48,768]{2,1,0:T(8,128)(2,1)S(1)}, u32[]{:S(2)}, u32[]{:S(2)}) async-start(bf16[8,48,768]{2,1,0:T(8,128)(2,1)} %bitcast.7), calls=%async_computation.1 | async-start | bytes 1179648 | tf_op jit(solution)/shard_map/all_to_all | solution.py:466
  68.9 0.0 all-gather.8.cloned.1.call-start
  69.0 0.6 reshape.40.plan
  69.6 2.1 pack_plan.1
  71.7 7.7 %all-to-all-done.1 = bf16[8,48,768]{2,1,0:T(8,128)(2,1)S(1)} async-done(((bf16[8,48,768]{2,1,0:T(8,128)(2,1)}), bf16[8,48,768]{2,1,0:T(8,128)(2,1)S(1)}, u32[]{:S(2)}, u32[]{:S(2)}) %all-to-all-start.1) | async-done | bytes 589856 | tf_op jit(solution)/shard_map/all_to_all | solution.py:466
  79.4 0.8 copy-done.27
  80.2 2.2 pack.3
  82.5 3.7 %copy-done.4 = bf16[2,3072,768]{2,1,0:T(8,128)(2,1)S(1)} copy-done((bf16[2,3072,768]{2,1,0:T(8,128)(2,1)S(1)}, bf16[2,3072,768]{2,1,0:T(8,128)(2,1)}, u32[]{:S(2)}) %copy-start.4) | copy-done | bytes 9437208
  86.1 1.7 copy-done.7
  87.8 6.7 %project.3 = bf16[768,768]{1,0:T(8,128)(2,1)} custom-call(f32[384,128]{1,0:T(8,128)S(1)} %copy-done.20, bf16[2,3072,768]{2,1,0:T(8,128)(2,1)S(1)} %copy-done.4, bf16[768,384]{1,0:T(8,128)(2,1)S(1)} %copy-done.12, bf16[384,3072]{1,0:T(8,128)(2,1)S(1)} %copy-done.7, bf16[384,768]{1,0:T(8,128)(2,1)} %project.2.refs_1_), custom_call_target="tpu_custom_call" | custom-call | flops 3623878656 | bytes 9437184 | tf_op jit(solution)/shard_map/project/pallas_call | solution.py:223
  94.5 3.6 %all-to-all-start = ((bf16[8,96,768]{2,1,0:T(8,128)(2,1)}), bf16[8,96,768]{2,1,0:T(8,128)(2,1)S(1)}, u32[]{:S(2)}, u32[]{:S(2)}) async-start(bf16[8,96,768]{2,1,0:T(8,128)(2,1)} %bitcast.2), calls=%async_computation | async-start | bytes 2359296 | tf_op jit(solution)/shard_map/all_to_all | solution.py:466
  98.1 0.0 all-gather.6.cloned.1.call-start
  98.1 3.8 %bag_plan.1 = (bf16[768,480]{1,0:T(8,128)(2,1)}, bf16[384,192]{1,0:T(8,128)(2,1)}, f32[672,128]{1,0:T(8,128)}) custom-call(s32[1]{0:T(128)} %bitcast.1.me, s32[8,4]{1,0:T(8,128)} %copy.12.lengths, s32[8,512]{1,0:T(8,128)} %reshape.40.plan, bf16[480,768]{1,0:T(8,128)(2,1)} %get-tuple-element.38.pack_even.onehot, ...), custom_call_target="tpu_custom_call" | custom-call | tf_op jit(solution)/shard_map/bag_plan/pallas_call | solution.py:453
  101.9 12.9 %all-to-all-done = bf16[8,96,768]{2,1,0:T(8,128)(2,1)S(1)} async-done(((bf16[8,96,768]{2,1,0:T(8,128)(2,1)}), bf16[8,96,768]{2,1,0:T(8,128)(2,1)S(1)}, u32[]{:S(2)}, u32[]{:S(2)}) %all-to-all-start) | async-done | bytes 1179680 | tf_op jit(solution)/shard_map/all_to_all | solution.py:466
  114.8 1.1 copy-done.25
  115.9 3.0 pack.2
  118.9 0.0 reduce-scatter.3.cloned.1.call-start
  119.0 0.7 slice.9.sample_col
  119.7 0.2 slice_reduce_fusion
  119.9 0.6 reshape_squeeze.3.sample_row
  120.5 33.5 %all_gather.17.rows_in.refs_3_ = bf16[160,3072]{1,0:T(8,128)(2,1)S(1)} all-gather(bf16[160,768]{1,0:T(8,128)(2,1)} %get-tuple-element.48), channel_id=1, replica_groups=mesh['dp'=8,'bag'=4] {'bag'}, dimensions={1}, use_global_device_ids=true | all-gather | bytes 1228800 | tf_op jit(solution)/shard_map/all_gather | solution.py:353
  154.0 5.1 %copy-done = bf16[3,3072,768]{2,1,0:T(8,128)(2,1)S(1)} copy-done((bf16[3,3072,768]{2,1,0:T(8,128)(2,1)S(1)}, bf16[3,3072,768]{2,1,0:T(8,128)(2,1)}, u32[]{:S(2)}) %copy-start) | copy-done | bytes 14155800
  159.1 4.9 %qkv.3 = (bf16[160,768]{1,0:T(8,128)(2,1)S(1)}, bf16[160,768]{1,0:T(8,128)(2,1)S(1)}, bf16[160,768]{1,0:T(8,128)(2,1)S(1)}) custom-call(bf16[160,3072]{1,0:T(8,128)(2,1)S(1)} %all_gather.17.rows_in.refs_3_, f32[3,2,256]{2,1,0:T(2,128)S(1)} %bitcast.23, bf16[3,3072,768]{2,1,0:T(8,128)(2,1)S(1)} %copy-done, bf16[3,3072,768]{2,1,0:T(8,128)(2,1)S(1)} %copy-done, ...), custom_call_target="tpu_custom_call" | custom-call | flops 2264924160 | bytes 14155776 | tf_op jit(solution)/shard_map/qkv/pallas_call | solution.py:271
  164.0 0.7 copy-done.17
  164.7 0.7 copy-done.18
  165.4 5.1 %copy-done.1 = bf16[3,3072,768]{2,1,0:T(8,128)(2,1)S(1)} copy-done((bf16[3,3072,768]{2,1,0:T(8,128)(2,1)S(1)}, bf16[3,3072,768]{2,1,0:T(8,128)(2,1)}, u32[]{:S(2)}) %copy-start.1) | copy-done | bytes 14155800
  170.5 1.3 copy-done.9
  171.8 5.5 %qkv.4 = (bf16[192,768]{1,0:T(8,128)(2,1)S(1)}, bf16[192,768]{1,0:T(8,128)(2,1)S(1)}, bf16[192,768]{1,0:T(8,128)(2,1)S(1)}) custom-call(bf16[192,3072]{1,0:T(8,128)(2,1)S(1)} %copy-done.9, f32[3,2,256]{2,1,0:T(2,128)S(1)} %bitcast.24, bf16[3,3072,768]{2,1,0:T(8,128)(2,1)S(1)} %copy-done.1, bf16[3,3072,768]{2,1,0:T(8,128)(2,1)S(1)} %copy-done.1, ...), custom_call_target="tpu_custom_call" | custom-call | flops 2717908992 | bytes 14155776 | tf_op jit(solution)/shard_map/qkv/pallas_call | solution.py:271
  177.3 0.7 copy-done.15
  178.0 0.8 copy-done.16
  178.8 5.1 %copy-done.2 = bf16[3,3072,768]{2,1,0:T(8,128)(2,1)S(1)} copy-done((bf16[3,3072,768]{2,1,0:T(8,128)(2,1)S(1)}, bf16[3,3072,768]{2,1,0:T(8,128)(2,1)}, u32[]{:S(2)}) %copy-start.2) | copy-done | bytes 14155800
  183.9 1.5 copy-done.8
  185.4 7.6 %qkv.5 = (bf16[320,768]{1,0:T(8,128)(2,1)S(1)}, bf16[320,768]{1,0:T(8,128)(2,1)S(1)}, bf16[320,768]{1,0:T(8,128)(2,1)S(1)}) custom-call(bf16[320,3072]{1,0:T(8,128)(2,1)S(1)} %copy-done.8, f32[3,2,256]{2,1,0:T(2,128)S(1)} %bitcast.25, bf16[3,3072,768]{2,1,0:T(8,128)(2,1)S(1)} %copy-done.2, bf16[3,3072,768]{2,1,0:T(8,128)(2,1)S(1)} %copy-done.2, ...), custom_call_target="tpu_custom_call" | custom-call | flops 4529848320 | bytes 14155776 | tf_op jit(solution)/shard_map/qkv/pallas_call | solution.py:271
  193.0 0.8 copy-done.13
  193.8 0.8 copy-done.14
  194.6 0.8 copy-done.24
  195.4 10.2 %attend.2.rows.refs_7_ = bf16[480,768]{1,0:T(8,128)(2,1)} custom-call(f32[480,128]{1,0:T(8,128)} %slice.9.sample_col, f32[1,672]{1,0:T(1,128)} %reshape_squeeze.3.sample_row, bf16[160,768]{1,0:T(8,128)(2,1)} %copy-done.19, bf16[320,768]{1,0:T(8,128)(2,1)} %copy-done.24, bf16[160,768]{1,0:T(8,128)(2,1)} %copy-done.17, bf16[320,768]{1,0:T(8,128)(2,1)} %copy-done.13, ...), custom_call_target="tpu_custom_call" | custom-call | flops 1981808640 | bytes 4128768 | tf_op jit(solution)/shard_map/attend/pallas_call | solution.py:328
  205.6 1.1 copy-done.6
  206.7 5.0 %terms.2 = bf16[480,3072]{1,0:T(8,128)(2,1)} custom-call(bf16[480,768]{1,0:T(8,128)(2,1)S(1)} %copy-done.6, bf16[768,3072]{1,0:T(8,128)(2,1)S(1)} %bitcast.22), custom_call_target="tpu_custom_call" | custom-call | flops 2264924160 | bytes 4718592 | tf_op jit(solution)/shard_map/terms/pallas_call | solution.py:374
  211.7 0.0 reduce-scatter.5.cloned.1.call-start
  211.8 0.6 slice.11.sample_col
  212.4 7.7 %attend.3.rows = bf16[192,768]{1,0:T(8,128)(2,1)} custom-call(f32[192,128]{1,0:T(8,128)} %slice.11.sample_col, f32[1,672]{1,0:T(1,128)} %reshape_squeeze.3.sample_row, bf16[192,768]{1,0:T(8,128)(2,1)} %copy-done.11, bf16[160,768]{1,0:T(8,128)(2,1)} %copy-done.17, bf16[320,768]{1,0:T(8,128)(2,1)} %copy-done.13, bf16[192,768]{1,0:T(8,128)(2,1)} %copy-done.15, ...), custom_call_target="tpu_custom_call" | custom-call | flops 792723456 | bytes 4128768 | tf_op jit(solution)/shard_map/attend/pallas_call | solution.py:328
  220.1 2.4 copy-done.5
  222.5 1.0 copy-done.10
  223.4 3.7 %terms.3 = bf16[192,3072]{1,0:T(8,128)(2,1)} custom-call(bf16[192,768]{1,0:T(8,128)(2,1)S(1)} %copy-done.10, bf16[768,3072]{1,0:T(8,128)(2,1)S(1)} %copy-done.5), custom_call_target="tpu_custom_call" | custom-call | flops 905969664 | bytes 4718592 | tf_op jit(solution)/shard_map/terms/pallas_call | solution.py:374
  227.1 43.7 %reduce-scatter.3.cloned.1.call-done = bf16[480,768]{1,0:T(8,128)(2,1)} async-done(((bf16[480,3072]{1,0:T(8,128)(2,1)}), bf16[480,768]{1,0:T(8,128)(2,1)}) %reduce-scatter.3.cloned.1.call-update) | async-done | bytes 737296 | tf_op jit(solution)/shard_map/reduce_scatter | solution.py:487
  270.9 3.0 convolution_convert_fusion
  273.8 3.8 %all-to-all-start.2 = ((bf16[8,96,768]{2,1,0:T(8,128)(2,1)}), bf16[8,96,768]{2,1,0:T(8,128)(2,1)S(1)}, u32[]{:S(2)}, u32[]{:S(2)}) async-start(bf16[8,96,768]{2,1,0:T(8,128)(2,1)} %bitcast.9), calls=%async_computation.3 | async-start | bytes 2359296 | tf_op jit(solution)/shard_map/all_to_all | solution.py:466
  277.6 24.6 %reduce-scatter.5.cloned.1.call-done = bf16[192,768]{1,0:T(8,128)(2,1)} async-done(((bf16[192,3072]{1,0:T(8,128)(2,1)}), bf16[192,768]{1,0:T(8,128)(2,1)}) %reduce-scatter.5.cloned.1.call-update) | async-done | bytes 294928 | tf_op jit(solution)/shard_map/reduce_scatter | solution.py:487
  302.2 2.1 convolution_convert_fusion.1
  304.3 3.7 %all-to-all-start.3 = ((bf16[8,48,768]{2,1,0:T(8,128)(2,1)}), bf16[8,48,768]{2,1,0:T(8,128)(2,1)S(1)}, u32[]{:S(2)}, u32[]{:S(2)}) async-start(bf16[8,48,768]{2,1,0:T(8,128)(2,1)} %bitcast.11), calls=%async_computation.5 | async-start | bytes 1179648 | tf_op jit(solution)/shard_map/all_to_all | solution.py:466
  308.0 1.9 fusion
  309.9 8.5 %all-to-all-done.3 = bf16[8,48,768]{2,1,0:T(8,128)(2,1)S(1)} async-done(((bf16[8,48,768]{2,1,0:T(8,128)(2,1)}), bf16[8,48,768]{2,1,0:T(8,128)(2,1)S(1)}, u32[]{:S(2)}, u32[]{:S(2)}) %all-to-all-start.3) | async-done | bytes 589856 | tf_op jit(solution)/shard_map/all_to_all | solution.py:466
  318.4 2.4 add_convert_fusion
  (57 shorter events, 0.2 us)
Async XLA Ops:
  6.5 75.9 %all-gather.4.cloned.1.call-start = ((), (), s32[]{:S(2)}) async-start(), calls=%async_computation.6 | async-start | bytes 2949120 | tf_op jit(solution)/shard_map/all_gather | solution.py:353
  11.5 6.3 %copy-start.28 = (bf16[160,768]{1,0:T(8,128)(2,1)S(1)}, bf16[160,768]{1,0:T(8,128)(2,1)}, u32[]{:S(2)}) copy-start(bf16[160,768]{1,0:T(8,128)(2,1)} %get-tuple-element.47) | copy-start | bytes 737284
  55.6 3.7 %copy-start.3 = (bf16[2,3072,768]{2,1,0:T(8,128)(2,1)S(1)}, bf16[2,3072,768]{2,1,0:T(8,128)(2,1)}, u32[]{:S(2)}) copy-start(bf16[2,3072,768]{2,1,0:T(8,128)(2,1)} %weight.5) | copy-start | bytes 28311556
  59.3 0.9 copy-start.21
  60.2 0.9 copy-start.22
  61.1 7.8 %copy-start.30 = (s32[4096]{0:T(1024)S(1)}, s32[4096]{0:T(1024)}, u32[]{:S(2)}) copy-start(s32[4096]{0:T(1024)} %param.13) | copy-start | bytes 49156
  65.1 17.3 %copy-start.12 = (bf16[768,384]{1,0:T(8,128)(2,1)S(1)}, bf16[768,384]{1,0:T(8,128)(2,1)}, u32[]{:S(2)}) copy-start(bf16[768,384]{1,0:T(8,128)(2,1)} %get-tuple-element.43.send) | copy-start | bytes 1769476
  65.1 17.3 %copy-start.20 = (f32[384,128]{1,0:T(8,128)S(1)}, f32[384,128]{1,0:T(8,128)}, u32[]{:S(2)}) copy-start(f32[384,128]{1,0:T(8,128)} %get-tuple-element.42.kinds) | copy-start | bytes 589828
  65.1 14.2 %all-to-all-start.1 = ((bf16[8,48,768]{2,1,0:T(8,128)(2,1)}), bf16[8,48,768]{2,1,0:T(8,128)(2,1)S(1)}, u32[]{:S(2)}, u32[]{:S(2)}) async-start(bf16[8,48,768]{2,1,0:T(8,128)(2,1)} %bitcast.7), calls=%async_computation.1 | async-start | bytes 1179648 | tf_op jit(solution)/shard_map/all_to_all | solution.py:466
  68.9 96.5 %all-gather.8.cloned.1.call-start = ((), (), s32[]{:S(2)}) async-start(), calls=%async_computation.8 | async-start | bytes 1474560 | tf_op jit(solution)/shard_map/all_gather | solution.py:353
  79.4 0.8 copy-start.27
  82.4 3.7 %copy-start.4 = (bf16[2,3072,768]{2,1,0:T(8,128)(2,1)S(1)}, bf16[2,3072,768]{2,1,0:T(8,128)(2,1)}, u32[]{:S(2)}) copy-start(bf16[2,3072,768]{2,1,0:T(8,128)(2,1)} %weight.5) | copy-start | bytes 28311556
  86.1 1.7 copy-start.7
  94.5 20.3 %all-to-all-start = ((bf16[8,96,768]{2,1,0:T(8,128)(2,1)}), bf16[8,96,768]{2,1,0:T(8,128)(2,1)S(1)}, u32[]{:S(2)}, u32[]{:S(2)}) async-start(bf16[8,96,768]{2,1,0:T(8,128)(2,1)} %bitcast.2), calls=%async_computation | async-start | bytes 2359296 | tf_op jit(solution)/shard_map/all_to_all | solution.py:466
  98.1 80.7 %all-gather.6.cloned.1.call-start = ((), (), s32[]{:S(2)}) async-start(), calls=%async_computation.7 | async-start | bytes 2457600 | tf_op jit(solution)/shard_map/all_gather | solution.py:353
  101.9 17.1 %copy-start.26 = (f32[672,128]{1,0:T(8,128)S(1)}, f32[672,128]{1,0:T(8,128)}, u32[]{:S(2)}) copy-start(f32[672,128]{1,0:T(8,128)} %get-tuple-element.41.refs_0_) | copy-start | bytes 1032196
  114.8 1.1 copy-start.25
  118.9 35.1 %copy-start.23 = (f32[2,768]{1,0:T(2,128)S(1)}, f32[2,768]{1,0:T(2,128)}, u32[]{:S(2)}) copy-start(f32[2,768]{1,0:T(2,128)} %param.11) | copy-start | bytes 18436
  118.9 151.9 %reduce-scatter.3.cloned.1.call-start = ((), (), s32[]{:S(2)}) async-start(), calls=%async_computation.9 | async-start | bytes 3686400 | tf_op jit(solution)/shard_map/reduce_scatter | solution.py:487
  154.0 5.1 %copy-start = (bf16[3,3072,768]{2,1,0:T(8,128)(2,1)S(1)}, bf16[3,3072,768]{2,1,0:T(8,128)(2,1)}, u32[]{:S(2)}) copy-start(bf16[3,3072,768]{2,1,0:T(8,128)(2,1)} %refs_2_.5) | copy-start | bytes 42467332
  164.0 0.7 copy-start.17
  164.7 0.7 copy-start.18
  165.4 13.3 %copy-start.19 = (bf16[160,768]{1,0:T(8,128)(2,1)}, bf16[160,768]{1,0:T(8,128)(2,1)S(1)}, u32[]{:S(2)}) copy-start(bf16[160,768]{1,0:T(8,128)(2,1)S(1)} %get-tuple-element.49.refs_4_.refs_0_) | copy-start | bytes 737284
  165.4 5.1 %copy-start.1 = (bf16[3,3072,768]{2,1,0:T(8,128)(2,1)S(1)}, bf16[3,3072,768]{2,1,0:T(8,128)(2,1)}, u32[]{:S(2)}) copy-start(bf16[3,3072,768]{2,1,0:T(8,128)(2,1)} %refs_2_.5) | copy-start | bytes 42467332
  170.5 1.3 copy-start.9
  171.8 33.8 %slice-start = ((s8[4718592]{0:T(1024)(128)(4,1)}), s8[524288]{0:T(1024)(128)(4,1)S(1)}, s32[]{:S(2)}) async-start(s8[4718592]{0:T(1024)(128)(4,1)} %bitcast.21), calls=%async_computation.11 | async-start | bytes 1048576
  177.3 0.7 copy-start.15
  178.0 0.8 copy-start.16
  178.8 14.3 %copy-start.11 = (bf16[192,768]{1,0:T(8,128)(2,1)}, bf16[192,768]{1,0:T(8,128)(2,1)S(1)}, u32[]{:S(2)}) copy-start(bf16[192,768]{1,0:T(8,128)(2,1)S(1)} %get-tuple-element.51.refs_3_.refs_0_) | copy-start | bytes 884740
  178.8 5.1 %copy-start.2 = (bf16[3,3072,768]{2,1,0:T(8,128)(2,1)S(1)}, bf16[3,3072,768]{2,1,0:T(8,128)(2,1)}, u32[]{:S(2)}) copy-start(bf16[3,3072,768]{2,1,0:T(8,128)(2,1)} %refs_2_.5) | copy-start | bytes 42467332
  183.9 1.5 copy-start.8
  185.4 20.1 %slice-start.1 = ((s8[4718592]{0:T(1024)(128)(4,1)}), s8[4194304]{0:T(1024)(128)(4,1)S(1)}, s32[]{:S(2)}) async-start(s8[4718592]{0:T(1024)(128)(4,1)} %bitcast.21), calls=%async_computation.12 | async-start | bytes 8388608
  193.0 0.8 copy-start.13
  193.8 0.8 copy-start.14
  194.6 0.8 copy-start.24
  205.6 1.1 copy-start.6
  211.7 90.5 %reduce-scatter.5.cloned.1.call-start = ((), (), s32[]{:S(2)}) async-start(), calls=%async_computation.10 | async-start | bytes 1474560 | tf_op jit(solution)/shard_map/reduce_scatter | solution.py:487
  220.1 2.4 copy-start.5
  222.5 1.0 copy-start.10
  223.4 47.4 %copy-start.31 = (bf16[768,480]{1,0:T(8,128)(2,1)S(1)}, bf16[768,480]{1,0:T(8,128)(2,1)}, u32[]{:S(2)}) copy-start(bf16[768,480]{1,0:T(8,128)(2,1)} %get-tuple-element.40) | copy-start | bytes 2211844
  273.8 28.4 %copy-start.29 = (bf16[384,192]{1,0:T(8,128)(2,1)S(1)}, bf16[384,192]{1,0:T(8,128)(2,1)}, u32[]{:S(2)}) copy-start(bf16[384,192]{1,0:T(8,128)(2,1)} %get-tuple-element.60) | copy-start | bytes 442372
  273.8 30.5 %all-to-all-start.2 = ((bf16[8,96,768]{2,1,0:T(8,128)(2,1)}), bf16[8,96,768]{2,1,0:T(8,128)(2,1)S(1)}, u32[]{:S(2)}, u32[]{:S(2)}) async-start(bf16[8,96,768]{2,1,0:T(8,128)(2,1)} %bitcast.9), calls=%async_computation.3 | async-start | bytes 2359296 | tf_op jit(solution)/shard_map/all_to_all | solution.py:466
  304.3 14.1 %all-to-all-start.3 = ((bf16[8,48,768]{2,1,0:T(8,128)(2,1)}), bf16[8,48,768]{2,1,0:T(8,128)(2,1)S(1)}, u32[]{:S(2)}, u32[]{:S(2)}) async-start(bf16[8,48,768]{2,1,0:T(8,128)(2,1)} %bitcast.11), calls=%async_computation.5 | async-start | bytes 1179648 | tf_op jit(solution)/shard_map/all_to_all | solution.py:466
Sparse Core Ops, SparseCore 0:
  11.6 66.9 all-gather.3
  82.5 30.4 all-gather.7
  119.1 52.8 all-gather.5
  211.9 58.9 reduce-scatter.2
  273.1 29.0 reduce-scatter.4

commit v6 on v5

--- a/solution.py
+++ b/solution.py
@@ -231,7 +231,7 @@
         out_specs=pl.BlockSpec((slots, step), lambda i: (0, i)),
         out_shape=jax.ShapeDtypeStruct((slots, width), BF16),
         scratch_shapes=[pltpu.VMEM((rows, depth), BF16)],
-        compiler_params=params(SMALL_LIMIT),
+        compiler_params=params(),
         cost_estimate=pl.CostEstimate(
             flops=2 * rows * weight.size, bytes_accessed=weight.size * 2, transcendentals=0
         ),
@@ -278,7 +278,7 @@
         + [pl.BlockSpec(memory_space=pl.ANY)] * len(after),
         out_specs=[part] * len(which),
         out_shape=[shape] * len(which),
-        compiler_params=params(SMALL_LIMIT),
+        compiler_params=params(),
         cost_estimate=pl.CostEstimate(
             flops=2 * len(which) * rows * depth * width,
             bytes_accessed=2 * len(which) * depth * width,

time: 329 us -> 311 us (0.945)
  local copies, waits for them, and re-layouts: 47.4 us -> 13.1 us
  Pallas kernels: 73.4 us -> 90.6 us
    unnamed x70 -> x26, local copies, waits for them, and re-layouts: 43.3 us -> 8.99 us
    pallas_call x3, Pallas kernels: 17.9 us -> 29.8 us  [make_qkv(): pl.pallas_call(functools.partial(qkv_kernel, which), grid=(width // step,...]
    pallas_call x2, Pallas kernels: 10.7 us -> 16.2 us  [project(): pl.pallas_call(functools.partial(project_kernel, len(parts)), grid=(width...]
  transfers between devices with their start and end apart: 9 -> 9, of which waited for: 5 -> 5; matrix products, arithmetic and copies ran while one was open for 4% -> 4% of each run, Pallas kernels for 14% -> 20%
where the time goes in v6:
time: 311 us; the launch traced here: 310 us
  waiting for transfers between devices  97.1 us (31%)
  Pallas kernels  90.6 us (29%)
  blocking collectives  72.2 us (23%)
  starting transfers between devices  14.8 us (5%)
  between operations  13.2 us (4%)
  local copies, waits for them, and re-layouts  13.1 us (4%)
  matrix products  9.37 us (3%)
    all_gather x2, blocking collectives, gather(): return lax.all_gather(rows, 'bag', axis=1, tiled=True)  72.2 us
    reduce_scatter x2, waiting for transfers between devices, to_home(): lax.psum_scatter(terms(rows, output_weight), 'bag', scatter_dimension=1,...  67.8 us
    pallas_call x3, Pallas kernels, make_qkv(): pl.pallas_call(functools.partial(qkv_kernel, which), grid=(width // step,...  29.8 us
    all_to_all x4, waiting for transfers between devices, exchange(): lax.all_to_all(outgoing.reshape(bags, -1, width), 'dp', split_axis=0, con...  29.1 us
    pallas_call x2, Pallas kernels, attend(): pl.pallas_call(functools.partial(attend_kernel, (len(queries), len(keys))...  17.8 us
    pallas_call x2, Pallas kernels, project(): pl.pallas_call(functools.partial(project_kernel, len(parts)), grid=(width...  16.2 us
    all_to_all x4, starting transfers between devices, exchange(): lax.all_to_all(outgoing.reshape(bags, -1, width), 'dp', split_axis=0, con...  14.6 us
    dot_general x4, matrix products, dot(): return jnp.dot(left, right, preferred_element_type=F32)  9.37 us
  transfers between devices with their start and end apart: 9, of which 5 were waited for; matrix products, arithmetic and copies ran while one was open for 4% of the time, Pallas kernels for 20%

profile of v6, /device:TPU:0, one launch (start us, length us, event | category | flops | bytes accessed | tf_op | source)
XLA Modules:
  0.0 310.3 jit_solution(14931899426446670364)
XLA Ops:
  6.5 0.0 all-gather.4.cloned.1.call-start
  6.5 1.3 dynamic_slice.3
  7.9 3.6 %order.1 = (bf16[384,512]{1,0:T(8,128)(2,1)}, bf16[160,512]{1,0:T(8,128)(2,1)}, s32[1,512]{1,0:T(1,128)}, s32[512,1]{1,0:T(8,128)}, bf16[384,768]{1,0:T(8,128)(2,1)}, /*index=5*/bf16[160,768]{1,0:T(8,128)(2,1)}) custom-call(s32[1,512]{1,0:T(1,128)} %bitcast.32, bf16[512,768]{1,0:T(8,128)(2,1)} %tokens.1), custom_call_target="tpu_custom_call" | custom-call | tf_op jit(solution)/shard_map/order/pallas_call | solution.py:418
  11.4 0.0 copy-start.6
  11.4 0.0 all-gather.4.cloned.1.call-update
  11.5 1.4 copy.12.lengths
  12.9 1.3 copy.13.modality
  14.2 3.5 %send_plan.1 = (bf16[768,384]{1,0:T(8,128)(2,1)}, bf16[384,160]{1,0:T(8,128)(2,1)}, f32[384,128]{1,0:T(8,128)}, f32[160,128]{1,0:T(8,128)}, bf16[512,768]{1,0:T(8,128)(2,1)}, /*index=5*/bf16[512,384]{1,0:T(8,128)(2,1)}) custom-call(s32[8,4]{1,0:T(8,128)} %copy.12.lengths, s32[8,4]{1,0:T(8,128)} %copy.13.modality, s32[1,512]{1,0:T(1,128)} %bitcast.33, ...), custom_call_target="tpu_custom_call" | custom-call | tf_op jit(solution)/shard_map/send_plan/pallas_call | solution.py:433
  17.7 0.0 copy-done.6
  17.7 37.8 %all_gather.16.refs_0_ = bf16[160,3072]{1,0:T(8,128)(2,1)} all-gather(bf16[160,768]{1,0:T(8,128)(2,1)S(1)} %copy-done.6), channel_id=1, replica_groups=mesh['dp'=8,'bag'=4] {'bag'}, dimensions={1}, use_global_device_ids=true | all-gather | bytes 1228800 | tf_op jit(solution)/shard_map/all_gather | solution.py:353
  55.6 6.8 %project.2.refs_1_ = bf16[384,768]{1,0:T(8,128)(2,1)} custom-call(f32[160,128]{1,0:T(8,128)} %get-tuple-element.45.kinds, bf16[2,3072,768]{2,1,0:T(8,128)(2,1)} %weight.5, bf16[384,160]{1,0:T(8,128)(2,1)} %get-tuple-element.46.send, bf16[160,3072]{1,0:T(8,128)(2,1)} %all_gather.16.refs_0_), custom_call_target="tpu_custom_call" | custom-call | flops 1509949440 | bytes 9437184 | tf_op jit(solution)/shard_map/project/pallas_call | solution.py:223
  62.4 3.6 %all-to-all-start.1 = ((bf16[8,48,768]{2,1,0:T(8,128)(2,1)}), bf16[8,48,768]{2,1,0:T(8,128)(2,1)S(1)}, u32[]{:S(2)}, u32[]{:S(2)}) async-start(bf16[8,48,768]{2,1,0:T(8,128)(2,1)} %bitcast.23), calls=%async_computation.1 | async-start | bytes 1179648 | tf_op jit(solution)/shard_map/all_to_all | solution.py:466
  66.0 0.0 all-gather.8.cloned.1.call-start
  66.1 0.0 copy-done.8
  66.1 0.6 reshape.40.plan
  66.7 2.1 pack_plan.1
  68.8 7.7 %all-to-all-done.1 = bf16[8,48,768]{2,1,0:T(8,128)(2,1)S(1)} async-done(((bf16[8,48,768]{2,1,0:T(8,128)(2,1)}), bf16[8,48,768]{2,1,0:T(8,128)(2,1)S(1)}, u32[]{:S(2)}, u32[]{:S(2)}) %all-to-all-start.1) | async-done | bytes 589856 | tf_op jit(solution)/shard_map/all_to_all | solution.py:466
  76.5 0.8 copy-done.5
  77.3 2.2 pack.3
  79.5 0.0 all-gather.8.cloned.1.call-update
  79.5 0.0 all-gather.4.cloned.1.call-done.refs_0_
  79.5 9.4 %project.3 = bf16[768,768]{1,0:T(8,128)(2,1)} custom-call(f32[384,128]{1,0:T(8,128)} %get-tuple-element.42.kinds, bf16[2,3072,768]{2,1,0:T(8,128)(2,1)} %weight.5, bf16[768,384]{1,0:T(8,128)(2,1)} %get-tuple-element.43.send, bf16[384,3072]{1,0:T(8,128)(2,1)} %all-gather.4.cloned.1.call-done.refs_0_, bf16[384,768]{1,0:T(8,128)(2,1)} %project.2.refs_1_), custom_call_target="tpu_custom_call" | custom-call | flops 3623878656 | bytes 9437184 | tf_op jit(solution)/shard_map/project/pallas_call | solution.py:223
  88.9 3.6 %all-to-all-start = ((bf16[8,96,768]{2,1,0:T(8,128)(2,1)}), bf16[8,96,768]{2,1,0:T(8,128)(2,1)S(1)}, u32[]{:S(2)}, u32[]{:S(2)}) async-start(bf16[8,96,768]{2,1,0:T(8,128)(2,1)} %bitcast.24), calls=%async_computation | async-start | bytes 2359296 | tf_op jit(solution)/shard_map/all_to_all | solution.py:466
  92.4 0.0 all-gather.6.cloned.1.call-start
  92.5 3.8 %bag_plan.1 = (bf16[768,480]{1,0:T(8,128)(2,1)}, bf16[384,192]{1,0:T(8,128)(2,1)}, f32[672,128]{1,0:T(8,128)}) custom-call(s32[1]{0:T(128)} %bitcast.1.me, s32[8,4]{1,0:T(8,128)} %copy.12.lengths, s32[8,512]{1,0:T(8,128)} %reshape.40.plan, bf16[480,768]{1,0:T(8,128)(2,1)} %get-tuple-element.38.pack_even.onehot, ...), custom_call_target="tpu_custom_call" | custom-call | tf_op jit(solution)/shard_map/bag_plan/pallas_call | solution.py:453
  96.3 12.9 %all-to-all-done = bf16[8,96,768]{2,1,0:T(8,128)(2,1)S(1)} async-done(((bf16[8,96,768]{2,1,0:T(8,128)(2,1)}), bf16[8,96,768]{2,1,0:T(8,128)(2,1)S(1)}, u32[]{:S(2)}, u32[]{:S(2)}) %all-to-all-start) | async-done | bytes 1179680 | tf_op jit(solution)/shard_map/all_to_all | solution.py:466
  109.2 1.0 copy-done.3
  110.2 3.0 pack.2
  113.2 0.0 all-gather.6.cloned.1.call-update
  113.2 0.0 reduce-scatter.3.cloned.1.call-start
  113.3 0.0 copy-done.4
  113.3 0.7 slice.9.sample_col
  114.0 0.2 slice_reduce_fusion
  114.2 0.6 reshape_squeeze.3.sample_row
  114.8 34.3 %all_gather.17.rows_in.refs_3_ = bf16[160,3072]{1,0:T(8,128)(2,1)} all-gather(bf16[160,768]{1,0:T(8,128)(2,1)} %get-tuple-element.48), channel_id=1, replica_groups=mesh['dp'=8,'bag'=4] {'bag'}, dimensions={1}, use_global_device_ids=true | all-gather | bytes 1228800 | tf_op jit(solution)/shard_map/all_gather | solution.py:353
  149.1 9.1 %qkv.3 = (bf16[160,768]{1,0:T(8,128)(2,1)}, bf16[160,768]{1,0:T(8,128)(2,1)}, bf16[160,768]{1,0:T(8,128)(2,1)}) custom-call(bf16[160,3072]{1,0:T(8,128)(2,1)} %all_gather.17.rows_in.refs_3_, f32[3,2,256]{2,1,0:T(2,128)} %bitcast.29, bf16[3,3072,768]{2,1,0:T(8,128)(2,1)} %refs_2_.5, bf16[3,3072,768]{2,1,0:T(8,128)(2,1)} %refs_2_.5, bf16[3,3072,768]{2,1,0:T(8,128)(2,1)} %refs_2_.5), custom_call_target="tpu_custom_call" | custom-call | flops 2264924160 | bytes 14155776 | tf_op jit(solution)/shard_map/qkv/pallas_call | solution.py:271
  158.2 9.5 %qkv.4 = (bf16[192,768]{1,0:T(8,128)(2,1)}, bf16[192,768]{1,0:T(8,128)(2,1)}, bf16[192,768]{1,0:T(8,128)(2,1)}) custom-call(bf16[192,3072]{1,0:T(8,128)(2,1)} %all-gather.8.cloned.1.call-done.rows_in, f32[3,2,256]{2,1,0:T(2,128)} %bitcast.30, bf16[3,3072,768]{2,1,0:T(8,128)(2,1)} %refs_2_.5, bf16[3,3072,768]{2,1,0:T(8,128)(2,1)} %refs_2_.5, ...), custom_call_target="tpu_custom_call" | custom-call | flops 2717908992 | bytes 14155776 | tf_op jit(solution)/shard_map/qkv/pallas_call | solution.py:271
  167.7 11.2 %qkv.5 = (bf16[320,768]{1,0:T(8,128)(2,1)}, bf16[320,768]{1,0:T(8,128)(2,1)}, bf16[320,768]{1,0:T(8,128)(2,1)}) custom-call(bf16[320,3072]{1,0:T(8,128)(2,1)} %all-gather.6.cloned.1.call-done.rows_in, f32[3,2,256]{2,1,0:T(2,128)} %bitcast.31, bf16[3,3072,768]{2,1,0:T(8,128)(2,1)} %refs_2_.5, bf16[3,3072,768]{2,1,0:T(8,128)(2,1)} %refs_2_.5, ...), custom_call_target="tpu_custom_call" | custom-call | flops 4529848320 | bytes 14155776 | tf_op jit(solution)/shard_map/qkv/pallas_call | solution.py:271
  179.0 10.2 %attend.2.rows.refs_7_ = bf16[480,768]{1,0:T(8,128)(2,1)} custom-call(f32[480,128]{1,0:T(8,128)} %slice.9.sample_col, f32[1,672]{1,0:T(1,128)} %reshape_squeeze.3.sample_row, bf16[160,768]{1,0:T(8,128)(2,1)} %get-tuple-element.49.refs_4_.refs_0_, bf16[320,768]{1,0:T(8,128)(2,1)} %get-tuple-element.52.refs_1_, ...), custom_call_target="tpu_custom_call" | custom-call | flops 1981808640 | bytes 4128768 | tf_op jit(solution)/shard_map/attend/pallas_call | solution.py:328
  189.1 0.0 slice-done
  189.1 0.0 slice-done.1
  189.1 0.0 copy-start.1
  189.2 1.1 copy-done.1
  190.3 5.0 %terms.2 = bf16[480,3072]{1,0:T(8,128)(2,1)} custom-call(bf16[480,768]{1,0:T(8,128)(2,1)S(1)} %copy-done.1, bf16[768,3072]{1,0:T(8,128)(2,1)S(1)} %bitcast.22), custom_call_target="tpu_custom_call" | custom-call | flops 2264924160 | bytes 4718592 | tf_op jit(solution)/shard_map/terms/pallas_call | solution.py:374
  195.2 0.0 reduce-scatter.3.cloned.1.call-update
  195.2 0.0 reduce-scatter.5.cloned.1.call-start
  195.3 0.6 slice.11.sample_col
  195.9 7.7 %attend.3.rows = bf16[192,768]{1,0:T(8,128)(2,1)} custom-call(f32[192,128]{1,0:T(8,128)} %slice.11.sample_col, f32[1,672]{1,0:T(1,128)} %reshape_squeeze.3.sample_row, bf16[192,768]{1,0:T(8,128)(2,1)} %get-tuple-element.51.refs_3_.refs_0_, bf16[160,768]{1,0:T(8,128)(2,1)} %get-tuple-element.53.refs_2_.refs_1_, ...), custom_call_target="tpu_custom_call" | custom-call | flops 792723456 | bytes 4128768 | tf_op jit(solution)/shard_map/attend/pallas_call | solution.py:328
  203.6 2.3 copy-done
  205.9 1.0 copy-done.2
  206.9 3.7 %terms.3 = bf16[192,3072]{1,0:T(8,128)(2,1)} custom-call(bf16[192,768]{1,0:T(8,128)(2,1)S(1)} %copy-done.2, bf16[768,3072]{1,0:T(8,128)(2,1)S(1)} %copy-done), custom_call_target="tpu_custom_call" | custom-call | flops 905969664 | bytes 4718592 | tf_op jit(solution)/shard_map/terms/pallas_call | solution.py:374
  210.6 0.0 reduce-scatter.5.cloned.1.call-update
  210.6 43.2 %reduce-scatter.3.cloned.1.call-done = bf16[480,768]{1,0:T(8,128)(2,1)} async-done(((bf16[480,3072]{1,0:T(8,128)(2,1)}), bf16[480,768]{1,0:T(8,128)(2,1)}) %reduce-scatter.3.cloned.1.call-update) | async-done | bytes 737296 | tf_op jit(solution)/shard_map/reduce_scatter | solution.py:487
  253.8 0.0 copy-done.9
  253.8 2.9 convolution_convert_fusion
  256.7 3.8 %all-to-all-start.2 = ((bf16[8,96,768]{2,1,0:T(8,128)(2,1)}), bf16[8,96,768]{2,1,0:T(8,128)(2,1)S(1)}, u32[]{:S(2)}, u32[]{:S(2)}) async-start(bf16[8,96,768]{2,1,0:T(8,128)(2,1)} %bitcast.9), calls=%async_computation.3 | async-start | bytes 2359296 | tf_op jit(solution)/shard_map/all_to_all | solution.py:466
  260.5 24.7 %reduce-scatter.5.cloned.1.call-done = bf16[192,768]{1,0:T(8,128)(2,1)} async-done(((bf16[192,3072]{1,0:T(8,128)(2,1)}), bf16[192,768]{1,0:T(8,128)(2,1)}) %reduce-scatter.5.cloned.1.call-update) | async-done | bytes 294928 | tf_op jit(solution)/shard_map/reduce_scatter | solution.py:487
  285.1 0.0 copy-done.7
  285.1 2.1 convolution_convert_fusion.1
  287.2 0.0 all-to-all-done.2
  287.2 3.7 %all-to-all-start.3 = ((bf16[8,48,768]{2,1,0:T(8,128)(2,1)}), bf16[8,48,768]{2,1,0:T(8,128)(2,1)S(1)}, u32[]{:S(2)}, u32[]{:S(2)}) async-start(bf16[8,48,768]{2,1,0:T(8,128)(2,1)} %bitcast.11), calls=%async_computation.5 | async-start | bytes 1179648 | tf_op jit(solution)/shard_map/all_to_all | solution.py:466
  290.9 1.9 fusion
  292.8 8.5 %all-to-all-done.3 = bf16[8,48,768]{2,1,0:T(8,128)(2,1)S(1)} async-done(((bf16[8,48,768]{2,1,0:T(8,128)(2,1)}), bf16[8,48,768]{2,1,0:T(8,128)(2,1)S(1)}, u32[]{:S(2)}, u32[]{:S(2)}) %all-to-all-start.3) | async-done | bytes 589856 | tf_op jit(solution)/shard_map/all_to_all | solution.py:466
  301.4 2.4 add_convert_fusion
  (13 shorter events, 0.0 us)
Async XLA Ops:
  6.5 73.0 %all-gather.4.cloned.1.call-start = ((), (), s32[]{:S(2)}) async-start(), calls=%async_computation.6 | async-start | bytes 2949120 | tf_op jit(solution)/shard_map/all_gather | solution.py:353
  11.4 6.3 %copy-start.6 = (bf16[160,768]{1,0:T(8,128)(2,1)S(1)}, bf16[160,768]{1,0:T(8,128)(2,1)}, u32[]{:S(2)}) copy-start(bf16[160,768]{1,0:T(8,128)(2,1)} %get-tuple-element.47) | copy-start | bytes 737284
  55.6 10.5 %copy-start.8 = (s32[4096]{0:T(1024)S(1)}, s32[4096]{0:T(1024)}, u32[]{:S(2)}) copy-start(s32[4096]{0:T(1024)} %param.13) | copy-start | bytes 49156
  62.4 14.1 %all-to-all-start.1 = ((bf16[8,48,768]{2,1,0:T(8,128)(2,1)}), bf16[8,48,768]{2,1,0:T(8,128)(2,1)S(1)}, u32[]{:S(2)}, u32[]{:S(2)}) async-start(bf16[8,48,768]{2,1,0:T(8,128)(2,1)} %bitcast.23), calls=%async_computation.1 | async-start | bytes 1179648 | tf_op jit(solution)/shard_map/all_to_all | solution.py:466
  66.0 92.2 %all-gather.8.cloned.1.call-start = ((), (), s32[]{:S(2)}) async-start(), calls=%async_computation.8 | async-start | bytes 1474560 | tf_op jit(solution)/shard_map/all_gather | solution.py:353
  76.5 0.8 copy-start.5
  88.9 20.3 %all-to-all-start = ((bf16[8,96,768]{2,1,0:T(8,128)(2,1)}), bf16[8,96,768]{2,1,0:T(8,128)(2,1)S(1)}, u32[]{:S(2)}, u32[]{:S(2)}) async-start(bf16[8,96,768]{2,1,0:T(8,128)(2,1)} %bitcast.24), calls=%async_computation | async-start | bytes 2359296 | tf_op jit(solution)/shard_map/all_to_all | solution.py:466
  92.4 75.3 %all-gather.6.cloned.1.call-start = ((), (), s32[]{:S(2)}) async-start(), calls=%async_computation.7 | async-start | bytes 2457600 | tf_op jit(solution)/shard_map/all_gather | solution.py:353
  96.3 17.0 %copy-start.4 = (f32[672,128]{1,0:T(8,128)S(1)}, f32[672,128]{1,0:T(8,128)}, u32[]{:S(2)}) copy-start(f32[672,128]{1,0:T(8,128)} %get-tuple-element.41.refs_0_) | copy-start | bytes 1032196
  109.2 1.0 copy-start.3
  113.2 140.6 %reduce-scatter.3.cloned.1.call-start = ((), (), s32[]{:S(2)}) async-start(), calls=%async_computation.9 | async-start | bytes 3686400 | tf_op jit(solution)/shard_map/reduce_scatter | solution.py:487
  158.2 30.9 %slice-start = ((s8[4718592]{0:T(1024)(128)(4,1)}), s8[524288]{0:T(1024)(128)(4,1)S(1)}, s32[]{:S(2)}) async-start(s8[4718592]{0:T(1024)(128)(4,1)} %bitcast.21), calls=%async_computation.11 | async-start | bytes 1048576
  167.7 21.4 %slice-start.1 = ((s8[4718592]{0:T(1024)(128)(4,1)}), s8[4194304]{0:T(1024)(128)(4,1)S(1)}, s32[]{:S(2)}) async-start(s8[4718592]{0:T(1024)(128)(4,1)} %bitcast.21), calls=%async_computation.12 | async-start | bytes 8388608
  189.1 1.1 copy-start.1
  195.2 89.9 %reduce-scatter.5.cloned.1.call-start = ((), (), s32[]{:S(2)}) async-start(), calls=%async_computation.10 | async-start | bytes 1474560 | tf_op jit(solution)/shard_map/reduce_scatter | solution.py:487
  203.6 2.3 copy-start
  205.9 1.0 copy-start.2
  206.9 46.9 %copy-start.9 = (bf16[768,480]{1,0:T(8,128)(2,1)S(1)}, bf16[768,480]{1,0:T(8,128)(2,1)}, u32[]{:S(2)}) copy-start(bf16[768,480]{1,0:T(8,128)(2,1)} %get-tuple-element.40) | copy-start | bytes 2211844
  256.7 28.4 %copy-start.7 = (bf16[384,192]{1,0:T(8,128)(2,1)S(1)}, bf16[384,192]{1,0:T(8,128)(2,1)}, u32[]{:S(2)}) copy-start(bf16[384,192]{1,0:T(8,128)(2,1)} %get-tuple-element.60) | copy-start | bytes 442372
  256.7 30.5 %all-to-all-start.2 = ((bf16[8,96,768]{2,1,0:T(8,128)(2,1)}), bf16[8,96,768]{2,1,0:T(8,128)(2,1)S(1)}, u32[]{:S(2)}, u32[]{:S(2)}) async-start(bf16[8,96,768]{2,1,0:T(8,128)(2,1)} %bitcast.9), calls=%async_computation.3 | async-start | bytes 2359296 | tf_op jit(solution)/shard_map/all_to_all | solution.py:466
  287.2 14.1 %all-to-all-start.3 = ((bf16[8,48,768]{2,1,0:T(8,128)(2,1)}), bf16[8,48,768]{2,1,0:T(8,128)(2,1)S(1)}, u32[]{:S(2)}, u32[]{:S(2)}) async-start(bf16[8,48,768]{2,1,0:T(8,128)(2,1)} %bitcast.11), calls=%async_computation.5 | async-start | bytes 1179648 | tf_op jit(solution)/shard_map/all_to_all | solution.py:466
Sparse Core Ops, SparseCore 0:
  11.6 67.0 all-gather.3
  80.2 29.9 all-gather.7
  113.4 54.0 all-gather.5
  195.4 58.3 reduce-scatter.2
  256.1 29.0 reduce-scatter.4
